TPU v7x, 32 devices: a whole 2x2x4 slice. The times are simulated.
32 devices in a mesh: req: 8 (over z, y), mp: 4 (over x, core).
Axes of the slice: x: 2, y: 2, z: 4, core: 2. Of those that a mesh axis runs over, the one named last changes fastest.
Arguments:
- q_pre: bfloat16 [4096, 3072], P('req', 'mp'), may hold values from -64 to 64
- k_pre: bfloat16 [4096, 1024], P('req', 'mp'), may hold values from -64 to 64
- v_pre: bfloat16 [4096, 1024], P('req', 'mp'), may hold values from -12 to 12
- q_bias: float32 [3072], P('mp'), may hold values from -3 to 3
- k_bias: float32 [1024], P('mp'), may hold values from -3 to 3
- v_bias: float32 [1024], P('mp'), may hold values from -3 to 3
- segment_ids: int32 [4096], P('req'), may hold values from -1 to 31, as said below
- lengths: int32 [8, 4], replicated, may hold values from 64 to 128, as said below
- page_table: int32 [8, 4], replicated, may hold values from 0 to 31, as said below
- w_out: bfloat16 [3072, 5120], P('mp'), may hold values from -0.109375 to 0.109375
- residual: bfloat16 [4096, 5120], P('req'), may hold values from -4 to 4
- norm_gain: float32 [5120], replicated, may hold values from 0.1 to 1.9
- w_gate: bfloat16 [5120, 6912], P('req', 'mp'), may hold values from -0.078125 to 0.078125
- w_up: bfloat16 [5120, 6912], P('req', 'mp'), may hold values from -0.078125 to 0.078125
Outputs:
- hidden: bfloat16 [4096, 6912], P('req', 'mp')
- kv_cache: bfloat16 [32, 8, 128, 256], P('req', 'mp')
Inputs may be any that keep to these rules, and one draw needn't show every extreme that they name: Requests of block r lie in order from the block's first token, request j taking lengths[r, j] tokens; in every block one request has exactly 128 tokens. `segment_ids`: token t of block r carries r * 4 + j inside request j's run of tokens given by lengths, and -1 after the last request of its block. `page_table`: every page is named once; page p is held by req index p // 4; the requests of one block have pages held by different req indices.
All inputs are finite; a program needn't handle non-finite values.
Results may differ from a plain program's by a relative error of at most 0.019.
Values may be sent and summed in bfloat16 or wider, within the bound.
No kernel may reach another device: no remote copies, remote signals or barrier semaphores. Data moves between devices by JAX's collectives and lax.ppermute only.
A program may use at most 128 MiB of HBM per device.

v0:
```python
import math

import jax
import jax.numpy as jnp
from jax import lax
from jax.experimental import pallas as pl
from jax.experimental.pallas import tpu as pltpu
from jax.sharding import PartitionSpec as P

HD = 128
PAGE = 128
REQS = 4
CORES = 2
N_Z = 4
THETA = 1000000.0
EPS = 1e-06
NT = (((1,), (1,)), ((), ()))


def rope_tables(positions):
    half_dim = HD // 2
    frequencies = THETA ** (-jnp.arange(half_dim, dtype=jnp.float32) * (2.0 / HD))
    angles = positions[:, None] * frequencies[None, :]
    cosine = jnp.cos(angles)
    sine = jnp.sin(angles)
    return jnp.concatenate([cosine, cosine], axis=-1), jnp.concatenate([-sine, sine], axis=-1)


def attention_kernel(order, q_ref, k_ref, v_ref, qb_ref, kb_ref, vb_ref, cos_ref, sin_ref, segc_ref, segr_ref,
                     slot_ref, out_ref, send_ref, q_buf, k_buf, v_buf, kv_buf):
    rows = q_ref.shape[0]
    kv_heads = k_ref.shape[1] // HD
    q_heads = q_ref.shape[1] // HD
    group = q_heads // kv_heads
    live = segc_ref[...] >= 0
    cosine = cos_ref[...]
    sine = sin_ref[...]

    def turned(source, bias, head):
        cols = slice(head * HD, (head + 1) * HD)
        raw = source[:, cols].astype(jnp.float32) + bias[:, cols]
        return jnp.where(live, raw * cosine + pltpu.roll(raw, HD // 2, 1) * sine, 0.0).astype(jnp.bfloat16)

    for head in range(q_heads):
        q_buf[:, head * HD:(head + 1) * HD] = turned(q_ref, qb_ref, head)
    for head in range(kv_heads):
        cols = slice(head * HD, (head + 1) * HD)
        key = turned(k_ref, kb_ref, head)
        value = jnp.where(live, v_ref[:, cols].astype(jnp.float32) + vb_ref[:, cols], 0.0).astype(jnp.bfloat16)
        k_buf[:, cols] = key
        v_buf[:, cols] = value
        kv_buf[:, 2 * head * HD:(2 * head + 1) * HD] = key
        kv_buf[:, (2 * head + 1) * HD:(2 * head + 2) * HD] = value
    slots = slot_ref[...]
    for part in range(send_ref.shape[0] // rows):
        wanted = lax.broadcasted_iota(jnp.int32, (rows, rows), 0) + part * rows
        pick = jnp.where(wanted == slots, 1.0, 0.0).astype(jnp.bfloat16)
        send_ref[part * rows:(part + 1) * rows, :] = jnp.dot(
            pick, kv_buf[...], preferred_element_type=jnp.float32
        ).astype(jnp.bfloat16)
    scale = 1.0 / math.sqrt(HD)
    tile = PAGE
    for start in range(0, rows, tile):
        low = max(0, start - tile)
        high = start + tile
        seg_q = segc_ref[start:high, :]
        seg_k = segr_ref[:, low:high]
        row_at = lax.broadcasted_iota(jnp.int32, (tile, high - low), 0) + start
        col_at = lax.broadcasted_iota(jnp.int32, (tile, high - low), 1) + low
        allowed = (seg_q == seg_k) & (seg_k >= 0) & (col_at <= row_at)
        for head in range(q_heads):
            kv = head // group
            kv_cols = slice(kv * HD, (kv + 1) * HD)
            scores = lax.dot_general(
                q_buf[start:high, head * HD:(head + 1) * HD], k_buf[low:high, kv_cols], NT,
                preferred_element_type=jnp.float32,
            ) * scale
            row_max = jnp.max(jnp.where(allowed, scores, -1e30), axis=-1, keepdims=True)
            weights = jnp.where(allowed, jnp.exp(scores - row_max), 0.0)
            total = jnp.sum(weights, axis=-1, keepdims=True)
            probs = (weights / jnp.where(total > 0.0, total, 1.0)).astype(jnp.bfloat16)
            mixed = jnp.dot(
                probs, v_buf[low:high, kv_cols], preferred_element_type=jnp.float32
            ).astype(jnp.bfloat16)
            size = rows // len(order)
            for at in range(0, tile, size):
                to = order[(start + at) // size] * size
                out_ref[to:to + size, head * HD:(head + 1) * HD] = mixed[at:at + size]


def attention(q_pre, k_pre, v_pre, q_bias, k_bias, v_bias, cosine, sine, segs, slots, slot_count, order):
    rows, q_cols = q_pre.shape
    kv_cols = k_pre.shape[1]
    vmem = pl.BlockSpec(memory_space=pltpu.VMEM)
    return pl.pallas_call(
        lambda *refs: attention_kernel(order, *refs),
        out_shape=(
            jax.ShapeDtypeStruct((rows, q_cols), jnp.bfloat16),
            jax.ShapeDtypeStruct((slot_count, 2 * kv_cols), jnp.bfloat16),
        ),
        in_specs=[vmem] * 11,
        out_specs=(vmem, vmem),
        scratch_shapes=[
            pltpu.VMEM((rows, q_cols), jnp.bfloat16),
            pltpu.VMEM((rows, kv_cols), jnp.bfloat16),
            pltpu.VMEM((rows, kv_cols), jnp.bfloat16),
            pltpu.VMEM((rows, 2 * kv_cols), jnp.bfloat16),
        ],
        compiler_params=pltpu.CompilerParams(vmem_limit_bytes=32 * 2**20),
        cost_estimate=pl.CostEstimate(flops=10**8, bytes_accessed=2**16, transcendentals=0),
        name="attention",
    )(q_pre, k_pre, v_pre, q_bias[None], k_bias[None], v_bias[None], cosine, sine, segs[:, None], segs[None],
      slots[None])


def cache_kernel(source_ref, in_ref, out_ref):
    out_ref[0, 0] = in_ref[0]


def write_cache(sources, pages_in, kv_heads):
    grid_spec = pltpu.PrefetchScalarGridSpec(
        num_scalar_prefetch=1,
        grid=(REQS, kv_heads),
        in_specs=[pl.BlockSpec((1, PAGE, 2 * HD), lambda page, head, source: (source[page], 0, head))],
        out_specs=pl.BlockSpec((1, 1, PAGE, 2 * HD), lambda page, head, source: (page, head, 0, 0)),
    )
    return pl.pallas_call(
        cache_kernel,
        out_shape=jax.ShapeDtypeStruct((REQS, kv_heads, PAGE, 2 * HD), jnp.bfloat16),
        grid_spec=grid_spec,
        name="write_cache",
    )(sources, pages_in)


def mlp_kernel(count, pieces, halves, ids_ref, *refs):
    weights = (refs[:count], refs[count:2 * count])
    rows_in = refs[2 * count:2 * count + pieces]
    out_ref, gate_buf, up_buf, row_buf, acc, weight_sems, row_sems = refs[2 * count + pieces:]
    depth = weights[0][0].shape[1]
    piece = rows_in[0].shape[0] // halves
    first, second = [], []
    for index in range(pieces):
        for half in range(halves):
            at = pl.multiple_of((half * pieces + ids_ref[count + index]) * piece, piece)
            first.append(
                pltpu.make_async_copy(
                    rows_in[index].at[pl.ds(half * piece, piece), :],
                    row_buf.at[pl.ds(at, piece), :],
                    row_sems.at[index, half],
                )
            )
    for which, buf, copies in ((0, gate_buf, first), (1, up_buf, second)):
        for index in range(count):
            at = pl.multiple_of(ids_ref[index] * depth, depth)
            copies.append(
                pltpu.make_async_copy(weights[which][index], buf.at[:, pl.ds(at, depth)], weight_sems.at[which, index])
            )
    for copy in first + second:
        copy.start()
    tile = min(256, out_ref.shape[1])
    for copy in first:
        copy.wait()
    for start in range(0, out_ref.shape[1], tile):
        acc[:, start:start + tile] = lax.dot_general(
            gate_buf[...], row_buf[start:start + tile, :], NT, preferred_element_type=jnp.float32
        )
    for copy in second:
        copy.wait()
    for start in range(0, out_ref.shape[1], tile):
        up = lax.dot_general(up_buf[...], row_buf[start:start + tile, :], NT, preferred_element_type=jnp.float32)
        gate = acc[:, start:start + tile]
        out_ref[:, start:start + tile] = (gate / (1.0 + jnp.exp(-gate)) * up).astype(jnp.bfloat16)


def mlp_block(weights, weight_ids, rows_in, row_ids, halves):
    count, pieces = len(weight_ids), len(row_ids)
    units, depth = weights[0].shape
    width = rows_in[0].shape[1]
    piece = rows_in[0].shape[0] // halves
    tokens = piece * pieces * halves
    if depth % 128 or units % 16 or piece % 16:
        both = jnp.zeros((2, units, width), jnp.bfloat16)
        for index in range(count):
            pair = jnp.stack([weights[index], weights[count + index]])
            both = lax.dynamic_update_slice(both, pair, (0, 0, weight_ids[index] * depth))
        rows = jnp.zeros((tokens, width), jnp.bfloat16)
        for index in range(pieces):
            for half in range(halves):
                at = (half * pieces + row_ids[index]) * piece
                rows = lax.dynamic_update_slice(rows, rows_in[index][half * piece:(half + 1) * piece], (at, 0))
        gate = lax.dot_general(both[0], rows, NT, preferred_element_type=jnp.float32)
        up = lax.dot_general(both[1], rows, NT, preferred_element_type=jnp.float32)
        return (jax.nn.silu(gate) * up).astype(jnp.bfloat16)
    ids = jnp.stack([jnp.asarray(i, jnp.int32) for i in list(weight_ids) + list(row_ids)])
    anywhere = pl.BlockSpec(memory_space=pl.ANY)
    return pl.pallas_call(
        lambda *refs: mlp_kernel(count, pieces, halves, *refs),
        out_shape=jax.ShapeDtypeStruct((units, tokens), jnp.bfloat16),
        in_specs=[pl.BlockSpec(memory_space=pltpu.SMEM)] + [anywhere] * (2 * count + pieces),
        out_specs=pl.BlockSpec(memory_space=pltpu.VMEM),
        scratch_shapes=[
            pltpu.VMEM((units, width), jnp.bfloat16),
            pltpu.VMEM((units, width), jnp.bfloat16),
            pltpu.VMEM((tokens, width), jnp.bfloat16),
            pltpu.VMEM((units, tokens), jnp.float32),
            pltpu.SemaphoreType.DMA((2, count)),
            pltpu.SemaphoreType.DMA((pieces, halves)),
        ],
        compiler_params=pltpu.CompilerParams(vmem_limit_bytes=60 * 2**20),
        cost_estimate=pl.CostEstimate(flops=10**8, bytes_accessed=2**16, transcendentals=0),
        name="mlp_block",
    )(ids, *weights, *rows_in)


def after(value, *before):
    return lax.optimization_barrier((value,) + before)[0]


def shards(q_pre, k_pre, v_pre, q_bias, k_bias, v_bias, segment_ids, lengths, page_table, w_out, residual,
           norm_gain, w_gate, w_up):
    me_req = lax.axis_index("req")
    me_mp = lax.axis_index("mp")
    n_req = lax.axis_size("req")
    n_mp = lax.axis_size("mp")
    n_y = n_req // N_Z
    n_x = n_mp // CORES
    z = me_req // n_y
    y = me_req % n_y
    x = me_mp // CORES
    core = me_mp % CORES

    def along_z(value, moves):
        return lax.ppermute(value, "req", [(a * n_y + c, b * n_y + c) for a, b in moves for c in range(n_y)])

    def turn_z(value, shift):
        return along_z(value, [(a, (a + shift) % N_Z) for a in range(N_Z)])

    def along_y(value):
        return [
            lax.ppermute(
                value, "req", [(a * n_y + b, a * n_y + (b + step) % n_y) for a in range(N_Z) for b in range(n_y)]
            )
            for step in range(1, n_y)
        ]

    def along_x(value):
        return [
            lax.ppermute(
                value,
                "mp",
                [(a * CORES + b, (a + step) % n_x * CORES + b) for a in range(n_x) for b in range(CORES)],
            )
            for step in range(1, n_x)
        ]

    def across_cores(value):
        return lax.ppermute(
            value, "mp", [(a * CORES + b, a * CORES + 1 - b) for a in range(n_x) for b in range(CORES)]
        )

    units_all, depth = w_gate.shape[1], w_gate.shape[0]
    units = units_all // N_Z

    def share(weight_t, shift):
        return lax.dynamic_slice(weight_t, ((z + shift) % N_Z * units, 0), (units, depth))

    def source_ids(shift):
        source_z = (z - shift) % N_Z
        return [source_z * n_y + (y - step) % n_y for step in range(n_y)]

    gate_t, up_t = w_gate.T, w_up.T
    gate_2 = share(gate_t, 2)
    gate_t, up_t, gate_2, q_pre, segment_ids = lax.optimization_barrier((gate_t, up_t, gate_2, q_pre, segment_ids))
    gate_0, up_0 = share(gate_t, 0), share(up_t, 0)
    gate_2 = turn_z(gate_2, 2)
    gate_0_y, up_0_y = along_y(gate_0), along_y(up_0)

    rows = q_pre.shape[0]
    kv_heads = k_pre.shape[1] // HD
    own_lens = lax.dynamic_index_in_dim(lengths, me_req, 0, keepdims=False)
    own_pages = lax.dynamic_index_in_dim(page_table, me_req, 0, keepdims=False)
    own_owner = own_pages // REQS
    starts = jnp.cumsum(own_lens) - own_lens
    alive = segment_ids >= 0
    req_idx = jnp.clip(segment_ids - me_req * REQS, 0, REQS - 1)
    hit = req_idx[:, None] == jnp.arange(REQS)[None, :]
    row_start = jnp.sum(jnp.where(hit, starts[None, :], 0), axis=1)
    row_owner = jnp.sum(jnp.where(hit, own_owner[None, :], 0), axis=1)
    row_pos = jnp.arange(rows, dtype=jnp.int32) - row_start
    slots = jnp.where(alive, row_owner * PAGE + row_pos, -1)
    cosine, sine = rope_tables(row_pos.astype(jnp.float32))
    run = rows // n_mp // 2
    order = []
    for group in range(2 * n_mp):
        half, device = divmod(group, n_mp)
        order.append((device % CORES * n_x + device // CORES) * 2 + half)
    attended, kv_send = attention(
        q_pre, k_pre, v_pre, q_bias, k_bias, v_bias, cosine, sine, segment_ids, slots, n_req * PAGE, order
    )
    attended = attended.reshape(CORES, n_x * 2 * run, attended.shape[1])

    def project(which):
        picked = lax.dynamic_index_in_dim(attended, which, 0, keepdims=False)
        return jnp.dot(picked, w_out, preferred_element_type=jnp.float32).astype(jnp.bfloat16)

    kept, given = project(core), project(1 - core)
    up_2, gate_2, gate_0_y, up_0_y, kept, given = lax.optimization_barrier(
        (share(up_t, 2), gate_2, gate_0_y, up_0_y, kept, given)
    )
    up_2 = turn_z(up_2, 2)
    gate_2_y = along_y(gate_2)
    sibling = across_cores(given)
    width = sibling.shape[1]
    gate_1, up_2, gate_2_y, sibling = lax.optimization_barrier((share(gate_t, 1), up_2, gate_2_y, sibling))
    gate_1 = turn_z(gate_1, 1)
    up_2_y = along_y(up_2)
    pair = (kept.astype(jnp.float32) + sibling.astype(jnp.float32)).reshape(n_x, 2 * run, width)
    summed = lax.dynamic_index_in_dim(pair, x, 0, keepdims=False)
    outgoing = [
        lax.dynamic_index_in_dim(pair, (x + step) % n_x, 0, keepdims=False).astype(jnp.bfloat16)
        for step in range(1, n_x)
    ]
    gate_3, up_3, gate_1, up_2_y, outgoing = lax.optimization_barrier(
        (share(gate_t, 3), share(up_t, 3), gate_1, up_2_y, outgoing)
    )
    gate_3, up_3 = turn_z(gate_3, 3), turn_z(up_3, 3)
    gate_1_y = along_y(gate_1)
    incoming = [
        lax.ppermute(
            outgoing[step - 1],
            "mp",
            [(a * CORES + b, (a + step) % n_x * CORES + b) for a in range(n_x) for b in range(CORES)],
        )
        for step in range(1, n_x)
    ]
    up_1, gate_3, up_3, gate_1_y, incoming = lax.optimization_barrier(
        (share(up_t, 1), gate_3, up_3, gate_1_y, incoming)
    )
    up_1 = turn_z(up_1, 1)
    gate_3_y = along_y(gate_3)
    residual_rows = jnp.concatenate(
        [
            lax.dynamic_slice(residual, (me_mp * run, 0), (run, width)),
            lax.dynamic_slice(residual, (rows // 2 + me_mp * run, 0), (run, width)),
        ]
    )
    for other in incoming:
        summed = summed + other.astype(jnp.float32)
    state = residual_rows.astype(jnp.float32) + summed
    scale = lax.rsqrt(jnp.mean(state * state, axis=-1, keepdims=True) + EPS)
    normed = (state * scale * norm_gain).astype(jnp.bfloat16)
    near, up_1, gate_3_y = lax.optimization_barrier((normed, up_1, gate_3_y))

    row_ids = [(x - step) % n_x * CORES + core for step in range(n_x)]
    row_ids += [(x - step) % n_x * CORES + 1 - core for step in range(n_x)]
    flip = [[(a, a ^ by) for a in range(N_Z)] for by in range(N_Z)]
    middle = [(1, 2), (2, 1)]
    outward = [(1, 0), (2, 3)]
    at_end = (z == 0) | (z == N_Z - 1)
    up_1_y, up_3_y = along_y(up_1), along_y(up_3)
    near_x = along_x(near)
    next_1, middle_1 = along_z(near, flip[1]), along_z(near, middle)
    next_1, middle_1, up_1_y, up_3_y, near_x = lax.optimization_barrier((next_1, middle_1, up_1_y, up_3_y, near_x))
    next_2e, next_2m = along_z(middle_1, outward), along_z(next_1, middle)
    next_1_x = along_x(next_1)

    gates = [gate_0, *gate_0_y, gate_2, *gate_2_y, gate_1, *gate_1_y, gate_3, *gate_3_y]
    ups = [up_0, *up_0_y, up_2, *up_2_y, up_1, *up_1_y, up_3, *up_3_y]
    weights = gates + ups
    weight_ids = [i for shift in (0, 2, 1, 3) for i in source_ids(shift)]

    def shared(block, block_x):
        return [block, *block_x, *[across_cores(p) for p in (block, *block_x)]]

    def work(pieces):
        return mlp_block(weights, weight_ids, pieces, row_ids, pieces[0].shape[0] // run)

    pieces_0 = shared(near, near_x)
    next_2e, next_2m, next_1_x, pieces_0 = lax.optimization_barrier((next_2e, next_2m, next_1_x, pieces_0))
    next_3 = along_z(next_2m, outward)
    next_2 = jnp.where(at_end, next_2e, next_2m)
    next_2_x = along_x(next_2)
    hidden_0 = work(pieces_0)
    hidden_1 = work(shared(next_1, next_1_x))
    next_3, next_2_x, hidden_0, hidden_1, kv_send = lax.optimization_barrier(
        (next_3, next_2_x, hidden_0, hidden_1, kv_send)
    )
    next_3a = jnp.where(at_end, next_3[:run], middle_1[:run])
    next_3b = jnp.where(at_end, next_3[run:], middle_1[run:])
    next_3a_x = along_x(next_3a)
    pieces_2 = shared(next_2, next_2_x)
    next_3b, next_3a_x, pieces_2 = lax.optimization_barrier((next_3b, next_3a_x, pieces_2))
    next_3b_x = along_x(next_3b)
    kv_in = lax.all_to_all(
        kv_send.reshape(n_req, PAGE, 2 * kv_heads * HD), "req", split_axis=0, concat_axis=0, tiled=True
    )
    back_1 = along_z(hidden_1, flip[1])
    hidden_2 = work(pieces_2)
    pieces_3a = shared(next_3a, next_3a_x)
    next_3b_x, hidden_2, pieces_3a, kv_in = lax.optimization_barrier((next_3b_x, hidden_2, pieces_3a, kv_in))
    back_2 = along_z(hidden_2, flip[2])
    back_3a = along_z(work(pieces_3a), flip[3])
    back_3b = along_z(work(shared(next_3b, next_3b_x)), flip[3])
    hidden_t = jnp.zeros((units_all, rows), jnp.bfloat16)
    for by, at, done in (
        (0, 0, hidden_0),
        (1, 0, back_1),
        (2, 0, back_2),
        (3, 0, back_3a),
        (3, rows // 2, back_3b),
    ):
        hidden_t = lax.dynamic_update_slice(hidden_t, done, ((z ^ by) * units, at))

    mine = page_table[None] == (me_req * REQS + jnp.arange(REQS, dtype=jnp.int32))[:, None, None]
    sources = jnp.sum(jnp.where(mine, jnp.arange(n_req, dtype=jnp.int32)[None, :, None], 0), axis=(1, 2))
    cache_out = write_cache(sources.astype(jnp.int32), kv_in, kv_heads)
    return hidden_t.T, cache_out


def solution(mesh):
    in_specs = (
        P("req", "mp"),
        P("req", "mp"),
        P("req", "mp"),
        P("mp"),
        P("mp"),
        P("mp"),
        P("req"),
        P(),
        P(),
        P("mp", None),
        P("req", None),
        P(),
        P("req", "mp"),
        P("req", "mp"),
    )
    out_specs = (P("req", "mp"), P("req", "mp", None, None))
    return jax.shard_map(shards, mesh=mesh, in_specs=in_specs, out_specs=out_specs, check_vma=False)
```

profile of v0, /device:TPU:0, one launch (start us, length us, event | category | flops | bytes accessed | tf_op | source)
XLA Modules:
  0.0 316.6 jit_solution(11589480520410095867)
XLA Ops:
  16.6 4.5 %attention.1 = (bf16[512,768]{1,0:T(8,128)(2,1)S(1)}, bf16[1024,512]{1,0:T(8,128)(2,1)}) custom-call(bf16[512,768]{1,0:T(8,128)(2,1)S(1)} %copy-done, bf16[512,256]{1,0:T(8,128)(2,1)S(1)} %copy-done.1, bf16[512,256]{1,0:T(8,128)(2,1)S(1)} %copy-done.2, f32[1,768]{1,0:T(1,128)S(1)} %broadcast_in_dim.71.refs_3_, f32[1,256]{1,0:T(1,128)S(1)} %bitcast.46, ...), custom_call_target="tpu_custom_call" | custom-call | flops 100000000 | bytes 65536 | tf_op jit(solution)/shard_map/attention/pallas_call | solution.py:95
  21.2 7.1 %convolution_convert_fusion = bf16[256,5120]{1,0:T(8,128)(2,1)} fusion(bf16[768,5120]{1,0:T(8,128)(2,1)} %param.23, bf16[2,256,768]{2,1,0:T(8,128)(2,1)S(1)} %bitcast.48, s32[]{:T(128)S(6)} %select_n.201), kind=kOutput, calls=%fused_computation | convolution fusion | flops 2014576640 | bytes 10878980 | tf_op jit(solution)/shard_map/dot_general | solution.py:304
  32.9 4.1 %collective-permute-done.refs_3_ = bf16[432,640]{1,0:T(8,128)(2,1)} collective-permute-done((bf16[432,640]{1,0:T(8,128)(2,1)}, bf16[432,640]{1,0:T(8,128)(2,1)}, u32[]{:S(2)}, u32[]{:S(2)}) %collective-permute-start) | collective-permute-done | bytes 552992 | tf_op jit(solution)/shard_map/ppermute | solution.py:233
  38.7 26.1 %collective-permute-done.3.refs_11_ = bf16[432,640]{1,0:T(8,128)(2,1)S(1)} collective-permute-done((bf16[432,640]{1,0:T(8,128)(2,1)S(1)}, bf16[432,640]{1,0:T(8,128)(2,1)S(1)}, u32[]{:S(2)}, u32[]{:S(2)}) %collective-permute-start.3) | collective-permute-done | bytes 552992 | tf_op jit(solution)/shard_map/ppermute | solution.py:233
  72.4 8.6 %collective-permute-done.6.refs_5_ = bf16[432,640]{1,0:T(8,128)(2,1)S(1)} collective-permute-done((bf16[432,640]{1,0:T(8,128)(2,1)}, bf16[432,640]{1,0:T(8,128)(2,1)S(1)}, u32[]{:S(2)}, u32[]{:S(2)}) %collective-permute-start.6) | collective-permute-done | bytes 552992 | tf_op jit(solution)/shard_map/ppermute | solution.py:233
  87.0 8.5 %collective-permute-done.10.refs_6_ = bf16[432,640]{1,0:T(8,128)(2,1)S(1)} collective-permute-done((bf16[432,640]{1,0:T(8,128)(2,1)S(1)}, bf16[432,640]{1,0:T(8,128)(2,1)S(1)}, u32[]{:S(2)}, u32[]{:S(2)}) %collective-permute-start.10) | collective-permute-done | bytes 552992 | tf_op jit(solution)/shard_map/ppermute | solution.py:240
  95.6 4.0 %collective-permute-done.8.refs_7_ = bf16[432,640]{1,0:T(8,128)(2,1)S(1)} collective-permute-done((bf16[432,640]{1,0:T(8,128)(2,1)S(1)}, bf16[432,640]{1,0:T(8,128)(2,1)S(1)}, u32[]{:S(2)}, u32[]{:S(2)}) %collective-permute-start.8) | collective-permute-done | bytes 552992 | tf_op jit(solution)/shard_map/ppermute | solution.py:233
  99.6 9.1 %collective-permute-done.9.refs_15_ = bf16[432,640]{1,0:T(8,128)(2,1)S(1)} collective-permute-done((bf16[432,640]{1,0:T(8,128)(2,1)}, bf16[432,640]{1,0:T(8,128)(2,1)S(1)}, u32[]{:S(2)}, u32[]{:S(2)}) %collective-permute-start.9) | collective-permute-done | bytes 552992 | tf_op jit(solution)/shard_map/ppermute | solution.py:233
  118.6 9.9 %collective-permute-done.12.refs_13_ = bf16[432,640]{1,0:T(8,128)(2,1)S(1)} collective-permute-done((bf16[432,640]{1,0:T(8,128)(2,1)S(1)}, bf16[432,640]{1,0:T(8,128)(2,1)S(1)}, u32[]{:S(2)}, u32[]{:S(2)}) %collective-permute-start.12) | collective-permute-done | bytes 552992 | tf_op jit(solution)/shard_map/ppermute | solution.py:233
  133.9 13.4 %collective-permute-done.17.refs_16_ = bf16[432,640]{1,0:T(8,128)(2,1)S(1)} collective-permute-done((bf16[432,640]{1,0:T(8,128)(2,1)S(1)}, bf16[432,640]{1,0:T(8,128)(2,1)S(1)}, u32[]{:S(2)}, u32[]{:S(2)}) %collective-permute-start.17) | collective-permute-done | bytes 552992 | tf_op jit(solution)/shard_map/ppermute | solution.py:240
  147.3 7.1 %collective-permute-done.16.refs_14_ = bf16[432,640]{1,0:T(8,128)(2,1)S(1)} collective-permute-done((bf16[432,640]{1,0:T(8,128)(2,1)S(1)}, bf16[432,640]{1,0:T(8,128)(2,1)S(1)}, u32[]{:S(2)}, u32[]{:S(2)}) %collective-permute-start.16) | collective-permute-done | bytes 552992 | tf_op jit(solution)/shard_map/ppermute | solution.py:240
  162.9 23.6 %collective-permute-done.19 = bf16[128,5120]{1,0:T(8,128)(2,1)} collective-permute-done((bf16[128,5120]{1,0:T(8,128)(2,1)}, bf16[128,5120]{1,0:T(8,128)(2,1)}, u32[]{:S(2)}, u32[]{:S(2)}) %collective-permute-start.19) | collective-permute-done | bytes 1310752 | tf_op jit(solution)/shard_map/ppermute | solution.py:233
  193.0 11.6 %mlp_block.5 = bf16[432,512]{1,0:T(8,128)(2,1)} custom-call(s32[12]{0:T(128)} %stack.38.refs_0_, bf16[432,640]{1,0:T(8,128)(2,1)} %copy-done.8, bf16[432,640]{1,0:T(8,128)(2,1)} %collective-permute-done.1.refs_2_, bf16[432,640]{1,0:T(8,128)(2,1)} %collective-permute-done.refs_3_, bf16[432,640]{1,0:T(8,128)(2,1)} %copy-done.11, bf16[432,640]{1,0:T(8,128)(2,1)} %copy-done.12, ...), custom_call_target="tpu_custom_call" | custom-call | flops 100000000 | bytes 65536 | tf_op jit(solution)/shard_map/mlp_block/pallas_call | solution.py:196
  204.6 11.5 %mlp_block.6 = bf16[432,512]{1,0:T(8,128)(2,1)} custom-call(s32[12]{0:T(128)} %stack.38.refs_0_, bf16[432,640]{1,0:T(8,128)(2,1)} %copy-done.8, bf16[432,640]{1,0:T(8,128)(2,1)} %collective-permute-done.1.refs_2_, bf16[432,640]{1,0:T(8,128)(2,1)} %collective-permute-done.refs_3_, bf16[432,640]{1,0:T(8,128)(2,1)} %copy-done.11, bf16[432,640]{1,0:T(8,128)(2,1)} %copy-done.12, ...), custom_call_target="tpu_custom_call" | custom-call | flops 100000000 | bytes 65536 | tf_op jit(solution)/shard_map/mlp_block/pallas_call | solution.py:196
  216.2 4.3 %collective-permute-done.25.refs_18_ = bf16[128,5120]{1,0:T(8,128)(2,1)} collective-permute-done((bf16[128,5120]{1,0:T(8,128)(2,1)S(1)}, bf16[128,5120]{1,0:T(8,128)(2,1)}, u32[]{:S(2)}, u32[]{:S(2)}) %collective-permute-start.25) | collective-permute-done | bytes 1310752 | tf_op jit(solution)/shard_map/ppermute | solution.py:248
  220.4 5.1 %collective-permute-done.24 = bf16[128,5120]{1,0:T(8,128)(2,1)} collective-permute-done((bf16[128,5120]{1,0:T(8,128)(2,1)}, bf16[128,5120]{1,0:T(8,128)(2,1)}, u32[]{:S(2)}, u32[]{:S(2)}) %collective-permute-start.24) | collective-permute-done | bytes 1310752 | tf_op jit(solution)/shard_map/ppermute | solution.py:233
  225.6 4.4 %all-to-all-start = ((bf16[8,128,512]{2,1,0:T(8,128)(2,1)}), bf16[8,128,512]{2,1,0:T(8,128)(2,1)S(1)}, u32[]{:S(2)}, u32[]{:S(2)}) async-start(bf16[8,128,512]{2,1,0:T(8,128)(2,1)} %bitcast.26), calls=%async_computation | async-start | bytes 2097152 | tf_op jit(solution)/shard_map/all_to_all | solution.py:394
  233.1 16.6 %collective-permute-done.29.refs_18_ = bf16[64,5120]{1,0:T(8,128)(2,1)} collective-permute-done((bf16[64,5120]{1,0:T(8,128)(2,1)}, bf16[64,5120]{1,0:T(8,128)(2,1)}, u32[]{:S(2)}, u32[]{:S(2)}) %collective-permute-start.29) | collective-permute-done | bytes 655392 | tf_op jit(solution)/shard_map/ppermute | solution.py:248
  250.8 11.7 %mlp_block.7 = bf16[432,512]{1,0:T(8,128)(2,1)} custom-call(s32[12]{0:T(128)} %stack.38.refs_0_, bf16[432,640]{1,0:T(8,128)(2,1)} %copy-done.8, bf16[432,640]{1,0:T(8,128)(2,1)} %collective-permute-done.1.refs_2_, bf16[432,640]{1,0:T(8,128)(2,1)} %collective-permute-done.refs_3_, bf16[432,640]{1,0:T(8,128)(2,1)} %copy-done.11, bf16[432,640]{1,0:T(8,128)(2,1)} %copy-done.12, ...), custom_call_target="tpu_custom_call" | custom-call | flops 100000000 | bytes 65536 | tf_op jit(solution)/shard_map/mlp_block/pallas_call | solution.py:196
  272.6 10.7 %mlp_block.8 = bf16[432,256]{1,0:T(8,128)(2,1)} custom-call(s32[12]{0:T(128)} %stack.38.refs_0_, bf16[432,640]{1,0:T(8,128)(2,1)} %copy-done.8, bf16[432,640]{1,0:T(8,128)(2,1)} %collective-permute-done.1.refs_2_, bf16[432,640]{1,0:T(8,128)(2,1)} %collective-permute-done.refs_3_, bf16[432,640]{1,0:T(8,128)(2,1)} %copy-done.11, bf16[432,640]{1,0:T(8,128)(2,1)} %copy-done.12, ...), custom_call_target="tpu_custom_call" | custom-call | flops 100000000 | bytes 65536 | tf_op jit(solution)/shard_map/mlp_block/pallas_call | solution.py:196
  284.0 3.9 %collective-permute-done.28 = bf16[432,512]{1,0:T(8,128)(2,1)} collective-permute-done((bf16[432,512]{1,0:T(8,128)(2,1)}, bf16[432,512]{1,0:T(8,128)(2,1)}, u32[]{:S(2)}, u32[]{:S(2)}) %collective-permute-start.28) | collective-permute-done | bytes 442400 | tf_op jit(solution)/shard_map/ppermute | solution.py:233
  289.8 5.4 %write_cache.1 = bf16[4,2,128,256]{3,2,1,0:T(8,128)(2,1)} custom-call(s32[4]{0:T(128)} %select_reduce_fusion.source_ref, bf16[8,128,512]{2,1,0:T(8,128)(2,1)} %copy-done.22), custom_call_target="tpu_custom_call" | custom-call | tf_op jit(solution)/shard_map/write_cache/pallas_call | solution.py:127
  296.1 10.6 %mlp_block.9 = bf16[432,256]{1,0:T(8,128)(2,1)} custom-call(s32[12]{0:T(128)} %stack.38.refs_0_, bf16[432,640]{1,0:T(8,128)(2,1)} %copy-done.8, bf16[432,640]{1,0:T(8,128)(2,1)} %collective-permute-done.1.refs_2_, bf16[432,640]{1,0:T(8,128)(2,1)} %collective-permute-done.refs_3_, bf16[432,640]{1,0:T(8,128)(2,1)} %copy-done.11, bf16[432,640]{1,0:T(8,128)(2,1)} %copy-done.12, ...), custom_call_target="tpu_custom_call" | custom-call | flops 100000000 | bytes 65536 | tf_op jit(solution)/shard_map/mlp_block/pallas_call | solution.py:196
  311.6 4.3 %collective-permute-done.39 = bf16[432,256]{1,0:T(8,128)(2,1)S(1)} collective-permute-done((bf16[432,256]{1,0:T(8,128)(2,1)}, bf16[432,256]{1,0:T(8,128)(2,1)S(1)}, u32[]{:S(2)}, u32[]{:S(2)}) %collective-permute-start.39) | collective-permute-done | bytes 221216 | tf_op jit(solution)/shard_map/ppermute | solution.py:233
  (176 shorter events, 88.9 us)
Async XLA Ops:
  5.4 26.6 %collective-permute-start.1 = (bf16[432,640]{1,0:T(8,128)(2,1)S(1)}, bf16[432,640]{1,0:T(8,128)(2,1)}, u32[]{:S(2)}, u32[]{:S(2)}) collective-permute-start(bf16[432,640]{1,0:T(8,128)(2,1)S(1)} %get-tuple-element.132.refs_1_), channel_id=1, source_target_pairs={{0,4},{4,0},{8,12},{12,8},{16,20},{20,16},{24,28},{28,24},{1,5},{5... | collective-permute-start | bytes 1658888 | tf_op jit(solution)/shard_map/ppermute | solution.py:240
  9.8 27.2 %collective-permute-start = (bf16[432,640]{1,0:T(8,128)(2,1)}, bf16[432,640]{1,0:T(8,128)(2,1)}, u32[]{:S(2)}, u32[]{:S(2)}) collective-permute-start(bf16[432,640]{1,0:T(8,128)(2,1)} %dynamic-slice_bitcast_fusion), channel_id=1, source_target_pairs={{0,16},{4,20},{8,24},{12,28},{16,0},{20,4},{24,8},{28,12},{1,17},{... | collective-permute-start | bytes 1658888 | tf_op jit(solution)/shard_map/ppermute | solution.py:233
  37.0 27.7 %collective-permute-start.5 = (bf16[256,5120]{1,0:T(8,128)(2,1)}, bf16[256,5120]{1,0:T(8,128)(2,1)}, u32[]{:S(2)}, u32[]{:S(2)}) collective-permute-start(bf16[256,5120]{1,0:T(8,128)(2,1)} %convolution_convert_fusion), channel_id=1, source_target_pairs={{0,1},{1,0},{2,3},{3,2},{4,5},{5,4},{6,7},{7,6},{8,9},{9,8},{10,11... | collective-permute-start | bytes 7864328 | tf_op jit(solution)/shard_map/ppermute | solution.py:257
  37.0 27.7 %collective-permute-start.3 = (bf16[432,640]{1,0:T(8,128)(2,1)S(1)}, bf16[432,640]{1,0:T(8,128)(2,1)S(1)}, u32[]{:S(2)}, u32[]{:S(2)}) collective-permute-start(bf16[432,640]{1,0:T(8,128)(2,1)S(1)} %copy-done.31), channel_id=1, source_target_pairs={{0,16},{4,20},{8,24},{12,28},{16,0},{20,4},{24,8},{28,12},{1,17},{... | collective-permute-start | bytes 1658888 | tf_op jit(solution)/shard_map/ppermute | solution.py:233
  37.0 27.7 %collective-permute-start.4 = (bf16[432,640]{1,0:T(8,128)(2,1)}, bf16[432,640]{1,0:T(8,128)(2,1)S(1)}, u32[]{:S(2)}, u32[]{:S(2)}) collective-permute-start(bf16[432,640]{1,0:T(8,128)(2,1)} %collective-permute-done.refs_3_), channel_id=1, source_target_pairs={{0,4},{4,0},{8,12},{12,8},{16,20},{20,16},{24,28},{28,24},{1,5},{5... | collective-permute-start | bytes 1658888 | tf_op jit(solution)/shard_map/ppermute | solution.py:240
  81.0 29.7 %collective-permute-start.11 = (bf16[128,5120]{1,0:T(8,128)(2,1)S(1)}, bf16[128,5120]{1,0:T(8,128)(2,1)}, u32[]{:S(2)}, u32[]{:S(2)}) collective-permute-start(bf16[128,5120]{1,0:T(8,128)(2,1)S(1)} %fusion.1), channel_id=1, source_target_pairs={{0,2},{1,3},{2,0},{3,1},{4,6},{5,7},{6,4},{7,5},{8,10},{9,11},{10,... | collective-permute-start | bytes 3932168 | tf_op jit(solution)/shard_map/ppermute | solution.py:329
  128.5 27.9 %collective-permute-start.14 = (bf16[128,5120]{1,0:T(8,128)(2,1)}, bf16[128,5120]{1,0:T(8,128)(2,1)}, u32[]{:S(2)}, u32[]{:S(2)}) collective-permute-start(bf16[128,5120]{1,0:T(8,128)(2,1)} %multiply_convert_fusion.refs_17_), channel_id=1, source_target_pairs={{0,8},{4,12},{8,0},{12,4},{16,24},{20,28},{24,16},{28,20},{1,9},{5... | collective-permute-start | bytes 3932168 | tf_op jit(solution)/shard_map/ppermute | solution.py:233
  128.6 27.8 %collective-permute-start.15 = (bf16[128,5120]{1,0:T(8,128)(2,1)}, bf16[128,5120]{1,0:T(8,128)(2,1)}, u32[]{:S(2)}, u32[]{:S(2)}) collective-permute-start(bf16[128,5120]{1,0:T(8,128)(2,1)} %multiply_convert_fusion.refs_17_), channel_id=1, source_target_pairs={{8,16},{12,20},{16,8},{20,12},{9,17},{13,21},{17,9},{21,13},{10,18... | collective-permute-start | bytes 3932168 | tf_op jit(solution)/shard_map/ppermute | solution.py:233
  130.3 27.5 %collective-permute-start.18 = (bf16[128,5120]{1,0:T(8,128)(2,1)}, bf16[128,5120]{1,0:T(8,128)(2,1)S(1)}, u32[]{:S(2)}, u32[]{:S(2)}) collective-permute-start(bf16[128,5120]{1,0:T(8,128)(2,1)} %multiply_convert_fusion.refs_17_), channel_id=1, source_target_pairs={{0,2},{1,3},{2,0},{3,1},{4,6},{5,7},{6,4},{7,5},{8,10},{9,11},{10,... | collective-permute-start | bytes 3932168 | tf_op jit(solution)/shard_map/ppermute | solution.py:248
  157.8 28.7 %collective-permute-start.19 = (bf16[128,5120]{1,0:T(8,128)(2,1)}, bf16[128,5120]{1,0:T(8,128)(2,1)}, u32[]{:S(2)}, u32[]{:S(2)}) collective-permute-start(bf16[128,5120]{1,0:T(8,128)(2,1)} %collective-permute-done.15), channel_id=1, source_target_pairs={{8,0},{12,4},{16,24},{20,28},{9,1},{13,5},{17,25},{21,29},{10,2},{... | collective-permute-start | bytes 3932168 | tf_op jit(solution)/shard_map/ppermute | solution.py:233
  159.1 27.4 %collective-permute-start.20 = (bf16[128,5120]{1,0:T(8,128)(2,1)}, bf16[128,5120]{1,0:T(8,128)(2,1)}, u32[]{:S(2)}, u32[]{:S(2)}) collective-permute-start(bf16[128,5120]{1,0:T(8,128)(2,1)} %collective-permute-done.14.refs_17_), channel_id=1, source_target_pairs={{8,16},{12,20},{16,8},{20,12},{9,17},{13,21},{17,9},{21,13},{10,18... | collective-permute-start | bytes 3932168 | tf_op jit(solution)/shard_map/ppermute | solution.py:233
  160.8 26.8 %collective-permute-start.21 = (bf16[128,5120]{1,0:T(8,128)(2,1)}, bf16[128,5120]{1,0:T(8,128)(2,1)}, u32[]{:S(2)}, u32[]{:S(2)}) collective-permute-start(bf16[128,5120]{1,0:T(8,128)(2,1)} %collective-permute-done.14.refs_17_), channel_id=1, source_target_pairs={{0,2},{1,3},{2,0},{3,1},{4,6},{5,7},{6,4},{7,5},{8,10},{9,11},{10,... | collective-permute-start | bytes 3932168 | tf_op jit(solution)/shard_map/ppermute | solution.py:248
  162.4 25.2 %collective-permute-start.23 = (bf16[128,5120]{1,0:T(8,128)(2,1)S(1)}, bf16[128,5120]{1,0:T(8,128)(2,1)}, u32[]{:S(2)}, u32[]{:S(2)}) collective-permute-start(bf16[128,5120]{1,0:T(8,128)(2,1)S(1)} %collective-permute-done.18.refs_18_), channel_id=1, source_target_pairs={{0,1},{1,0},{2,3},{3,2},{4,5},{5,4},{6,7},{7,6},{8,9},{9,8},{10,11... | collective-permute-start | bytes 3932168 | tf_op jit(solution)/shard_map/ppermute | solution.py:257
  162.4 42.2 %collective-permute-start.26 = (bf16[128,5120]{1,0:T(8,128)(2,1)}, bf16[128,5120]{1,0:T(8,128)(2,1)}, u32[]{:S(2)}, u32[]{:S(2)}) collective-permute-start(bf16[128,5120]{1,0:T(8,128)(2,1)} %collective-permute-done.14.refs_17_), channel_id=1, source_target_pairs={{0,1},{1,0},{2,3},{3,2},{4,5},{5,4},{6,7},{7,6},{8,9},{9,8},{10,11... | collective-permute-start | bytes 3932168 | tf_op jit(solution)/shard_map/ppermute | solution.py:257
  189.1 31.3 %collective-permute-start.25 = (bf16[128,5120]{1,0:T(8,128)(2,1)S(1)}, bf16[128,5120]{1,0:T(8,128)(2,1)}, u32[]{:S(2)}, u32[]{:S(2)}) collective-permute-start(bf16[128,5120]{1,0:T(8,128)(2,1)S(1)} %broadcast_select_fusion.refs_17_), channel_id=1, source_target_pairs={{0,2},{1,3},{2,0},{3,1},{4,6},{5,7},{6,4},{7,5},{8,10},{9,11},{10,... | collective-permute-start | bytes 3932168 | tf_op jit(solution)/shard_map/ppermute | solution.py:248
  190.7 34.9 %collective-permute-start.24 = (bf16[128,5120]{1,0:T(8,128)(2,1)}, bf16[128,5120]{1,0:T(8,128)(2,1)}, u32[]{:S(2)}, u32[]{:S(2)}) collective-permute-start(bf16[128,5120]{1,0:T(8,128)(2,1)} %collective-permute-done.20), channel_id=1, source_target_pairs={{8,0},{12,4},{16,24},{20,28},{9,1},{13,5},{17,25},{21,29},{10,2},{... | collective-permute-start | bytes 3932168 | tf_op jit(solution)/shard_map/ppermute | solution.py:233
  192.8 40.4 %collective-permute-start.30 = (bf16[128,5120]{1,0:T(8,128)(2,1)S(1)}, bf16[128,5120]{1,0:T(8,128)(2,1)}, u32[]{:S(2)}, u32[]{:S(2)}) collective-permute-start(bf16[128,5120]{1,0:T(8,128)(2,1)S(1)} %broadcast_select_fusion.refs_17_), channel_id=1, source_target_pairs={{0,1},{1,0},{2,3},{3,2},{4,5},{5,4},{6,7},{7,6},{8,9},{9,8},{10,11... | collective-permute-start | bytes 3932168 | tf_op jit(solution)/shard_map/ppermute | solution.py:257
  225.6 24.2 %collective-permute-start.31 = (bf16[128,5120]{1,0:T(8,128)(2,1)}, bf16[128,5120]{1,0:T(8,128)(2,1)}, u32[]{:S(2)}, u32[]{:S(2)}) collective-permute-start(bf16[128,5120]{1,0:T(8,128)(2,1)} %collective-permute-done.25.refs_18_), channel_id=1, source_target_pairs={{0,1},{1,0},{2,3},{3,2},{4,5},{5,4},{6,7},{7,6},{8,9},{9,8},{10,11... | collective-permute-start | bytes 3932168 | tf_op jit(solution)/shard_map/ppermute | solution.py:257
  225.6 37.0 %all-to-all-start = ((bf16[8,128,512]{2,1,0:T(8,128)(2,1)}), bf16[8,128,512]{2,1,0:T(8,128)(2,1)S(1)}, u32[]{:S(2)}, u32[]{:S(2)}) async-start(bf16[8,128,512]{2,1,0:T(8,128)(2,1)} %bitcast.26), calls=%async_computation | async-start | bytes 2097152 | tf_op jit(solution)/shard_map/all_to_all | solution.py:394
  233.1 29.4 %collective-permute-start.33 = (bf16[64,5120]{1,0:T(8,128)(2,1)}, bf16[64,5120]{1,0:T(8,128)(2,1)}, u32[]{:S(2)}, u32[]{:S(2)}) collective-permute-start(bf16[64,5120]{1,0:T(8,128)(2,1)} %get-tuple-element.116.refs_17_), channel_id=1, source_target_pairs={{0,1},{1,0},{2,3},{3,2},{4,5},{5,4},{6,7},{7,6},{8,9},{9,8},{10,11... | collective-permute-start | bytes 1966088 | tf_op jit(solution)/shard_map/ppermute | solution.py:257
  250.3 44.9 %collective-permute-start.37 = (bf16[64,5120]{1,0:T(8,128)(2,1)S(1)}, bf16[64,5120]{1,0:T(8,128)(2,1)S(1)}, u32[]{:S(2)}, u32[]{:S(2)}) collective-permute-start(bf16[64,5120]{1,0:T(8,128)(2,1)S(1)} %get-tuple-element.108.refs_17_), channel_id=1, source_target_pairs={{0,1},{1,0},{2,3},{3,2},{4,5},{5,4},{6,7},{7,6},{8,9},{9,8},{10,11... | collective-permute-start | bytes 1966088 | tf_op jit(solution)/shard_map/ppermute | solution.py:257
  265.8 29.4 %collective-permute-start.38 = (bf16[64,5120]{1,0:T(8,128)(2,1)S(1)}, bf16[64,5120]{1,0:T(8,128)(2,1)}, u32[]{:S(2)}, u32[]{:S(2)}) collective-permute-start(bf16[64,5120]{1,0:T(8,128)(2,1)S(1)} %collective-permute-done.32.refs_18_), channel_id=1, source_target_pairs={{0,1},{1,0},{2,3},{3,2},{4,5},{5,4},{6,7},{7,6},{8,9},{9,8},{10,11... | collective-permute-start | bytes 1966088 | tf_op jit(solution)/shard_map/ppermute | solution.py:257
  267.3 41.8 %collective-permute-start.35 = (bf16[432,512]{1,0:T(8,128)(2,1)}, bf16[432,512]{1,0:T(8,128)(2,1)}, u32[]{:S(2)}, u32[]{:S(2)}) collective-permute-start(bf16[432,512]{1,0:T(8,128)(2,1)} %mlp_block.7), channel_id=1, source_target_pairs={{0,16},{4,20},{8,24},{12,28},{16,0},{20,4},{24,8},{28,12},{1,17},{... | collective-permute-start | bytes 1327112 | tf_op jit(solution)/shard_map/ppermute | solution.py:233
  283.4 27.6 %collective-permute-start.36 = (bf16[432,256]{1,0:T(8,128)(2,1)}, bf16[432,256]{1,0:T(8,128)(2,1)S(1)}, u32[]{:S(2)}, u32[]{:S(2)}) collective-permute-start(bf16[432,256]{1,0:T(8,128)(2,1)} %mlp_block.8), channel_id=1, source_target_pairs={{0,24},{4,28},{8,16},{12,20},{16,8},{20,12},{24,0},{28,4},{1,25},{... | collective-permute-start | bytes 663560 | tf_op jit(solution)/shard_map/ppermute | solution.py:233
  (55 other events, 964.0 us)
where the time goes:
time: 317 us
  waiting for transfers between devices  159 us (50%)
  Pallas kernels  66.1 us (21%)
  starting transfers between devices  42.5 us (13%)
  local copies, waits for them, and re-layouts  18.8 us (6%)
  other arithmetic  17.7 us (6%)
  matrix products  10.8 us (3%)
    ppermute x15, waiting for transfers between devices, along_z(): lax.ppermute(value, 'req', [(a * n_y + c, b * n_y + c) for a, b in moves...  101 us
    pallas_call x5, Pallas kernels, mlp_block(): pl.pallas_call(lambda *refs: mlp_kernel(count, pieces, halves, *refs), ou...  56.2 us
    ppermute x8, waiting for transfers between devices, along_y(): lax.ppermute(value, 'req', [(a * n_y + b, a * n_y + (b + step) % n_y) for...  30 us
    ppermute x5, waiting for transfers between devices, along_x(): lax.ppermute(value, 'mp', [(a * CORES + b, (a + step) % n_x * CORES + b)...  26.7 us
    ppermute x15, starting transfers between devices, along_z(): lax.ppermute(value, 'req', [(a * n_y + c, b * n_y + c) for a, b in moves...  17.9 us
    ppermute x8, starting transfers between devices, along_y(): lax.ppermute(value, 'req', [(a * n_y + b, a * n_y + (b + step) % n_y) for...  11.6 us
    dot_general x2, matrix products, project(): jnp.dot(picked, w_out, preferred_element_type=jnp.float32)  10.8 us
  transfers between devices with their start and end apart: 41, of which 21 were waited for; matrix products, arithmetic and copies ran while one was open for 11% of the time, Pallas kernels for 21%

commit v1 on v0

--- a/solution.py
+++ b/solution.py
@@ -113,21 +113,31 @@
       slots[None])
 
 
-def cache_kernel(source_ref, in_ref, out_ref):
-    out_ref[0, 0] = in_ref[0]
+def cache_kernel(source_ref, in_ref, out_ref, sems):
+    copies = []
+    for page in range(out_ref.shape[0]):
+        for head in range(out_ref.shape[1]):
+            copies.append(
+                pltpu.make_async_copy(
+                    in_ref.at[source_ref[page], :, pl.ds(head * 2 * HD, 2 * HD)],
+                    out_ref.at[page, head],
+                    sems.at[page, head],
+                )
+            )
+    for copy in copies:
+        copy.start()
+    for copy in copies:
+        copy.wait()
 
 
 def write_cache(sources, pages_in, kv_heads):
-    grid_spec = pltpu.PrefetchScalarGridSpec(
-        num_scalar_prefetch=1,
-        grid=(REQS, kv_heads),
-        in_specs=[pl.BlockSpec((1, PAGE, 2 * HD), lambda page, head, source: (source[page], 0, head))],
-        out_specs=pl.BlockSpec((1, 1, PAGE, 2 * HD), lambda page, head, source: (page, head, 0, 0)),
-    )
+    anywhere = pl.BlockSpec(memory_space=pl.ANY)
     return pl.pallas_call(
         cache_kernel,
         out_shape=jax.ShapeDtypeStruct((REQS, kv_heads, PAGE, 2 * HD), jnp.bfloat16),
-        grid_spec=grid_spec,
+        in_specs=[pl.BlockSpec(memory_space=pltpu.SMEM), anywhere],
+        out_specs=anywhere,
+        scratch_shapes=[pltpu.SemaphoreType.DMA((REQS, kv_heads))],
         name="write_cache",
     )(sources, pages_in)
 
@@ -149,26 +159,31 @@
                     row_sems.at[index, half],
                 )
             )
-    for which, buf, copies in ((0, gate_buf, first), (1, up_buf, second)):
-        for index in range(count):
-            at = pl.multiple_of(ids_ref[index] * depth, depth)
-            copies.append(
-                pltpu.make_async_copy(weights[which][index], buf.at[:, pl.ds(at, depth)], weight_sems.at[which, index])
+    for index in range(count):
+        for which, buf in ((0, gate_buf), (1, up_buf)):
+            second.append(
+                pltpu.make_async_copy(weights[which][index], buf.at[index], weight_sems.at[which, index])
             )
     for copy in first + second:
         copy.start()
-    tile = min(256, out_ref.shape[1])
     for copy in first:
         copy.wait()
-    for start in range(0, out_ref.shape[1], tile):
-        acc[:, start:start + tile] = lax.dot_general(
-            gate_buf[...], row_buf[start:start + tile, :], NT, preferred_element_type=jnp.float32
-        )
-    for copy in second:
-        copy.wait()
-    for start in range(0, out_ref.shape[1], tile):
-        up = lax.dot_general(up_buf[...], row_buf[start:start + tile, :], NT, preferred_element_type=jnp.float32)
-        gate = acc[:, start:start + tile]
+    tokens = out_ref.shape[1]
+    tile = min(256, tokens)
+    for index in range(count):
+        second[2 * index].wait()
+        second[2 * index + 1].wait()
+        at = pl.multiple_of(ids_ref[index] * depth, depth)
+        for start in range(0, tokens, tile):
+            block = row_buf[start:start + tile, pl.ds(at, depth)]
+            for which, buf in ((0, gate_buf), (1, up_buf)):
+                term = lax.dot_general(buf[index], block, NT, preferred_element_type=jnp.float32)
+                if index:
+                    term = acc[which, :, start:start + tile] + term
+                acc[which, :, start:start + tile] = term
+    for start in range(0, tokens, tile):
+        gate = acc[0, :, start:start + tile]
+        up = acc[1, :, start:start + tile]
         out_ref[:, start:start + tile] = (gate / (1.0 + jnp.exp(-gate)) * up).astype(jnp.bfloat16)
 
 
@@ -199,10 +214,10 @@
         in_specs=[pl.BlockSpec(memory_space=pltpu.SMEM)] + [anywhere] * (2 * count + pieces),
         out_specs=pl.BlockSpec(memory_space=pltpu.VMEM),
         scratch_shapes=[
-            pltpu.VMEM((units, width), jnp.bfloat16),
-            pltpu.VMEM((units, width), jnp.bfloat16),
+            pltpu.VMEM((count, units, depth), jnp.bfloat16),
+            pltpu.VMEM((count, units, depth), jnp.bfloat16),
             pltpu.VMEM((tokens, width), jnp.bfloat16),
-            pltpu.VMEM((units, tokens), jnp.float32),
+            pltpu.VMEM((2, units, tokens), jnp.float32),
             pltpu.SemaphoreType.DMA((2, count)),
             pltpu.SemaphoreType.DMA((pieces, halves)),
         ],
@@ -273,7 +288,7 @@
     gate_t, up_t, gate_2, q_pre, segment_ids = lax.optimization_barrier((gate_t, up_t, gate_2, q_pre, segment_ids))
     gate_0, up_0 = share(gate_t, 0), share(up_t, 0)
     gate_2 = turn_z(gate_2, 2)
-    gate_0_y, up_0_y = along_y(gate_0), along_y(up_0)
+    gate_0_y = along_y(gate_0)
 
     rows = q_pre.shape[0]
     kv_heads = k_pre.shape[1] // HD
@@ -304,14 +319,17 @@
         return jnp.dot(picked, w_out, preferred_element_type=jnp.float32).astype(jnp.bfloat16)
 
     kept, given = project(core), project(1 - core)
-    up_2, gate_2, gate_0_y, up_0_y, kept, given = lax.optimization_barrier(
-        (share(up_t, 2), gate_2, gate_0_y, up_0_y, kept, given)
+    up_2, up_0, gate_2, gate_0_y, kept, given = lax.optimization_barrier(
+        (share(up_t, 2), up_0, gate_2, gate_0_y, kept, given)
     )
     up_2 = turn_z(up_2, 2)
+    up_0_y = along_y(up_0)
     gate_2_y = along_y(gate_2)
     sibling = across_cores(given)
     width = sibling.shape[1]
-    gate_1, up_2, gate_2_y, sibling = lax.optimization_barrier((share(gate_t, 1), up_2, gate_2_y, sibling))
+    gate_1, up_2, up_0_y, gate_2_y, sibling = lax.optimization_barrier(
+        (share(gate_t, 1), up_2, up_0_y, gate_2_y, sibling)
+    )
     gate_1 = turn_z(gate_1, 1)
     up_2_y = along_y(up_2)
     pair = (kept.astype(jnp.float32) + sibling.astype(jnp.float32)).reshape(n_x, 2 * run, width)
@@ -388,18 +406,22 @@
     next_3a = jnp.where(at_end, next_3[:run], middle_1[:run])
     next_3b = jnp.where(at_end, next_3[run:], middle_1[run:])
     next_3a_x = along_x(next_3a)
-    pieces_2 = shared(next_2, next_2_x)
-    next_3b, next_3a_x, pieces_2 = lax.optimization_barrier((next_3b, next_3a_x, pieces_2))
-    next_3b_x = along_x(next_3b)
+    hidden_2 = work(shared(next_2, next_2_x))
+    back_1 = along_z(hidden_1, flip[1])
     kv_in = lax.all_to_all(
         kv_send.reshape(n_req, PAGE, 2 * kv_heads * HD), "req", split_axis=0, concat_axis=0, tiled=True
     )
-    back_1 = along_z(hidden_1, flip[1])
-    hidden_2 = work(pieces_2)
-    pieces_3a = shared(next_3a, next_3a_x)
-    next_3b_x, hidden_2, pieces_3a, kv_in = lax.optimization_barrier((next_3b_x, hidden_2, pieces_3a, kv_in))
+    next_3b, next_3a_x, hidden_2, back_1, kv_in = lax.optimization_barrier(
+        (next_3b, next_3a_x, hidden_2, back_1, kv_in)
+    )
+    next_3b_x = along_x(next_3b)
     back_2 = along_z(hidden_2, flip[2])
-    back_3a = along_z(work(pieces_3a), flip[3])
+    hidden_3a = work(shared(next_3a, next_3a_x))
+    mine = page_table[None] == (me_req * REQS + jnp.arange(REQS, dtype=jnp.int32))[:, None, None]
+    sources = jnp.sum(jnp.where(mine, jnp.arange(n_req, dtype=jnp.int32)[None, :, None], 0), axis=(1, 2))
+    cache_out = write_cache(sources.astype(jnp.int32), kv_in, kv_heads)
+    next_3b_x, hidden_3a, back_2, cache_out = lax.optimization_barrier((next_3b_x, hidden_3a, back_2, cache_out))
+    back_3a = along_z(hidden_3a, flip[3])
     back_3b = along_z(work(shared(next_3b, next_3b_x)), flip[3])
     hidden_t = jnp.zeros((units_all, rows), jnp.bfloat16)
     for by, at, done in (
@@ -410,10 +432,6 @@
         (3, rows // 2, back_3b),
     ):
         hidden_t = lax.dynamic_update_slice(hidden_t, done, ((z ^ by) * units, at))
-
-    mine = page_table[None] == (me_req * REQS + jnp.arange(REQS, dtype=jnp.int32))[:, None, None]
-    sources = jnp.sum(jnp.where(mine, jnp.arange(n_req, dtype=jnp.int32)[None, :, None], 0), axis=(1, 2))
-    cache_out = write_cache(sources.astype(jnp.int32), kv_in, kv_heads)
     return hidden_t.T, cache_out
 
 

time: 317 us -> 315 us (level)
  waiting for transfers between devices: 159 us -> 144 us
  Pallas kernels: 66.1 us -> 80.3 us
    ppermute x5, waiting for transfers between devices: 26.7 us -> 4.23 us  [along_x(): lax.ppermute(value, 'mp', [(a * CORES + b, (a + step) % n_x * CORES + b)...]
    pallas_call x1, Pallas kernels: 5.41 us -> 17.7 us  [write_cache(): pl.pallas_call(cache_kernel, out_shape=jax.ShapeDtypeStruct((REQS, kv_hea...]
    ppermute x15, waiting for transfers between devices: 101 us -> 107 us  [along_z(): lax.ppermute(value, 'req', [(a * n_y + c, b * n_y + c) for a, b in moves...]
    dynamic_update_slice x5, local copies, waits for them, and re-layouts: 5.8 us -> 1.15 us  [shards(): hidden_t = lax.dynamic_update_slice(hidden_t, done, ((z ^ by) * units, at))]
    ppermute x15, starting transfers between devices: 17.9 us -> 22.4 us  [along_z(): lax.ppermute(value, 'req', [(a * n_y + c, b * n_y + c) for a, b in moves...]
  transfers between devices with their start and end apart: 41 -> 41, of which waited for: 21 -> 19; matrix products, arithmetic and copies ran while one was open for 11% -> 10% of each run, Pallas kernels for 21% -> 26%
where the time goes in v1:
time: 315 us; the launch traced here: 314 us
  waiting for transfers between devices  144 us (46%)
  Pallas kernels  80.3 us (25%)
  starting transfers between devices  43.2 us (14%)
  local copies, waits for them, and re-layouts  17.5 us (6%)
  other arithmetic  17 us (5%)
  matrix products  10.8 us (3%)
    ppermute x15, waiting for transfers between devices, along_z(): lax.ppermute(value, 'req', [(a * n_y + c, b * n_y + c) for a, b in moves...  107 us
    pallas_call x5, Pallas kernels, mlp_block(): pl.pallas_call(lambda *refs: mlp_kernel(count, pieces, halves, *refs), ou...  58 us
    ppermute x8, waiting for transfers between devices, along_y(): lax.ppermute(value, 'req', [(a * n_y + b, a * n_y + (b + step) % n_y) for...  29.3 us
    ppermute x15, starting transfers between devices, along_z(): lax.ppermute(value, 'req', [(a * n_y + c, b * n_y + c) for a, b in moves...  22.4 us
    pallas_call x1, Pallas kernels, write_cache(): pl.pallas_call(cache_kernel, out_shape=jax.ShapeDtypeStruct((REQS, kv_hea...  17.7 us
    dot_general x2, matrix products, project(): jnp.dot(picked, w_out, preferred_element_type=jnp.float32)  10.8 us
    ppermute x8, starting transfers between devices, along_y(): lax.ppermute(value, 'req', [(a * n_y + b, a * n_y + (b + step) % n_y) for...  8.6 us
    dynamic_slice x3, local copies, waits for them, and re-layouts, share(): lax.dynamic_slice(weight_t, ((z + shift) % N_Z * units, 0), (units, depth))  7.37 us
  transfers between devices with their start and end apart: 41, of which 19 were waited for; matrix products, arithmetic and copies ran while one was open for 10% of the time, Pallas kernels for 26%

profile of v1, /device:TPU:0, one launch (start us, length us, event | category | flops | bytes accessed | tf_op | source)
XLA Modules:
  0.0 314.2 jit_solution(9564750623808489633)
XLA Ops:
  16.6 4.5 %attention.1 = (bf16[512,768]{1,0:T(8,128)(2,1)S(1)}, bf16[1024,512]{1,0:T(8,128)(2,1)}) custom-call(bf16[512,768]{1,0:T(8,128)(2,1)S(1)} %copy-done, bf16[512,256]{1,0:T(8,128)(2,1)S(1)} %copy-done.1, bf16[512,256]{1,0:T(8,128)(2,1)S(1)} %copy-done.2, f32[1,768]{1,0:T(1,128)S(1)} %broadcast_in_dim.71.refs_3_, f32[1,256]{1,0:T(1,128)S(1)} %bitcast.46, ...), custom_call_target="tpu_custom_call" | custom-call | flops 100000000 | bytes 65536 | tf_op jit(solution)/shard_map/attention/pallas_call | solution.py:95
  21.1 7.1 %convolution_convert_fusion = bf16[256,5120]{1,0:T(8,128)(2,1)} fusion(bf16[768,5120]{1,0:T(8,128)(2,1)} %param.23, bf16[2,256,768]{2,1,0:T(8,128)(2,1)S(1)} %bitcast.48, s32[]{:T(128)S(6)} %select_n.201), kind=kOutput, calls=%fused_computation | convolution fusion | flops 2014576640 | bytes 10878980 | tf_op jit(solution)/shard_map/dot_general | solution.py:319
  28.2 3.8 %convolution_convert_fusion.1 = bf16[256,5120]{1,0:T(8,128)(2,1)} fusion(bf16[768,5120]{1,0:T(8,128)(2,1)S(1)} %bitcast.57, bf16[2,256,768]{2,1,0:T(8,128)(2,1)S(1)} %bitcast.49, s32[]{:T(128)S(6)} %select_n.200), kind=kOutput, calls=%fused_computation.1 | convolution fusion | flops 2014576640 | bytes 10878980 | tf_op jit(solution)/shard_map/dot_general | solution.py:319
  32.0 3.3 %collective-permute-done.refs_3_ = bf16[432,640]{1,0:T(8,128)(2,1)} collective-permute-done((bf16[432,640]{1,0:T(8,128)(2,1)}, bf16[432,640]{1,0:T(8,128)(2,1)}, u32[]{:S(2)}, u32[]{:S(2)}) %collective-permute-start) | collective-permute-done | bytes 552992 | tf_op jit(solution)/shard_map/ppermute | solution.py:248
  37.4 25.6 %collective-permute-done.2.refs_11_ = bf16[432,640]{1,0:T(8,128)(2,1)S(1)} collective-permute-done((bf16[432,640]{1,0:T(8,128)(2,1)S(1)}, bf16[432,640]{1,0:T(8,128)(2,1)S(1)}, u32[]{:S(2)}, u32[]{:S(2)}) %collective-permute-start.2) | collective-permute-done | bytes 552992 | tf_op jit(solution)/shard_map/ppermute | solution.py:248
  66.4 3.4 %convert_add_fusion = f32[256,5120]{1,0:T(8,128)S(1)} fusion(bf16[256,5120]{1,0:T(8,128)(2,1)} %collective-permute-done.5, bf16[256,5120]{1,0:T(8,128)(2,1)} %convolution_convert_fusion.1), kind=kLoop, calls=%fused_computation.2 | loop fusion | flops 3932160 | bytes 10485760 | tf_op jit(solution)/shard_map/add | solution.py:335
  73.3 5.9 %collective-permute-done.6.refs_5_ = bf16[432,640]{1,0:T(8,128)(2,1)S(1)} collective-permute-done((bf16[432,640]{1,0:T(8,128)(2,1)}, bf16[432,640]{1,0:T(8,128)(2,1)S(1)}, u32[]{:S(2)}, u32[]{:S(2)}) %collective-permute-start.6) | collective-permute-done | bytes 552992 | tf_op jit(solution)/shard_map/ppermute | solution.py:248
  85.0 8.8 %collective-permute-done.10.refs_6_ = bf16[432,640]{1,0:T(8,128)(2,1)S(1)} collective-permute-done((bf16[432,640]{1,0:T(8,128)(2,1)S(1)}, bf16[432,640]{1,0:T(8,128)(2,1)S(1)}, u32[]{:S(2)}, u32[]{:S(2)}) %collective-permute-start.10) | collective-permute-done | bytes 552992 | tf_op jit(solution)/shard_map/ppermute | solution.py:255
  96.9 9.0 %collective-permute-done.9.refs_15_ = bf16[432,640]{1,0:T(8,128)(2,1)S(1)} collective-permute-done((bf16[432,640]{1,0:T(8,128)(2,1)}, bf16[432,640]{1,0:T(8,128)(2,1)S(1)}, u32[]{:S(2)}, u32[]{:S(2)}) %collective-permute-start.9) | collective-permute-done | bytes 552992 | tf_op jit(solution)/shard_map/ppermute | solution.py:248
  105.9 3.3 %collective-permute-done.11 = bf16[128,5120]{1,0:T(8,128)(2,1)} collective-permute-done((bf16[128,5120]{1,0:T(8,128)(2,1)}, bf16[128,5120]{1,0:T(8,128)(2,1)}, u32[]{:S(2)}, u32[]{:S(2)}) %collective-permute-start.11) | collective-permute-done | bytes 1310752 | tf_op jit(solution)/shard_map/ppermute | solution.py:347
  116.2 10.7 %collective-permute-done.12.refs_13_ = bf16[432,640]{1,0:T(8,128)(2,1)S(1)} collective-permute-done((bf16[432,640]{1,0:T(8,128)(2,1)S(1)}, bf16[432,640]{1,0:T(8,128)(2,1)S(1)}, u32[]{:S(2)}, u32[]{:S(2)}) %collective-permute-start.12) | collective-permute-done | bytes 552992 | tf_op jit(solution)/shard_map/ppermute | solution.py:248
  132.2 13.4 %collective-permute-done.17.refs_16_ = bf16[432,640]{1,0:T(8,128)(2,1)S(1)} collective-permute-done((bf16[432,640]{1,0:T(8,128)(2,1)S(1)}, bf16[432,640]{1,0:T(8,128)(2,1)S(1)}, u32[]{:S(2)}, u32[]{:S(2)}) %collective-permute-start.17) | collective-permute-done | bytes 552992 | tf_op jit(solution)/shard_map/ppermute | solution.py:255
  145.7 6.9 %collective-permute-done.16.refs_14_ = bf16[432,640]{1,0:T(8,128)(2,1)S(1)} collective-permute-done((bf16[432,640]{1,0:T(8,128)(2,1)S(1)}, bf16[432,640]{1,0:T(8,128)(2,1)S(1)}, u32[]{:S(2)}, u32[]{:S(2)}) %collective-permute-start.16) | collective-permute-done | bytes 552992 | tf_op jit(solution)/shard_map/ppermute | solution.py:255
  161.1 23.3 %collective-permute-done.19 = bf16[128,5120]{1,0:T(8,128)(2,1)} collective-permute-done((bf16[128,5120]{1,0:T(8,128)(2,1)}, bf16[128,5120]{1,0:T(8,128)(2,1)}, u32[]{:S(2)}, u32[]{:S(2)}) %collective-permute-start.19) | collective-permute-done | bytes 1310752 | tf_op jit(solution)/shard_map/ppermute | solution.py:248
  191.7 13.0 %mlp_block.5 = bf16[432,512]{1,0:T(8,128)(2,1)} custom-call(s32[12]{0:T(128)} %stack.38.refs_0_, bf16[432,640]{1,0:T(8,128)(2,1)} %copy-done.8, bf16[432,640]{1,0:T(8,128)(2,1)} %collective-permute-done.1.refs_2_, bf16[432,640]{1,0:T(8,128)(2,1)} %collective-permute-done.refs_3_, bf16[432,640]{1,0:T(8,128)(2,1)} %copy-done.12, bf16[432,640]{1,0:T(8,128)(2,1)} %copy-done.13, ...), custom_call_target="tpu_custom_call" | custom-call | flops 100000000 | bytes 65536 | tf_op jit(solution)/shard_map/mlp_block/pallas_call | solution.py:211
  204.7 12.9 %mlp_block.6 = bf16[432,512]{1,0:T(8,128)(2,1)} custom-call(s32[12]{0:T(128)} %stack.38.refs_0_, bf16[432,640]{1,0:T(8,128)(2,1)} %copy-done.8, bf16[432,640]{1,0:T(8,128)(2,1)} %collective-permute-done.1.refs_2_, bf16[432,640]{1,0:T(8,128)(2,1)} %collective-permute-done.refs_3_, bf16[432,640]{1,0:T(8,128)(2,1)} %copy-done.12, bf16[432,640]{1,0:T(8,128)(2,1)} %copy-done.13, ...), custom_call_target="tpu_custom_call" | custom-call | flops 100000000 | bytes 65536 | tf_op jit(solution)/shard_map/mlp_block/pallas_call | solution.py:211
  219.4 4.9 %collective-permute-done.24 = bf16[128,5120]{1,0:T(8,128)(2,1)} collective-permute-done((bf16[128,5120]{1,0:T(8,128)(2,1)}, bf16[128,5120]{1,0:T(8,128)(2,1)}, u32[]{:S(2)}, u32[]{:S(2)}) %collective-permute-start.24) | collective-permute-done | bytes 1310752 | tf_op jit(solution)/shard_map/ppermute | solution.py:248
  224.3 3.8 %all-to-all-start = ((bf16[8,128,512]{2,1,0:T(8,128)(2,1)}), bf16[8,128,512]{2,1,0:T(8,128)(2,1)S(1)}, u32[]{:S(2)}, u32[]{:S(2)}) async-start(bf16[8,128,512]{2,1,0:T(8,128)(2,1)} %bitcast.26), calls=%async_computation | async-start | bytes 2097152 | tf_op jit(solution)/shard_map/all_to_all | solution.py:411
  232.3 13.0 %mlp_block.7 = bf16[432,512]{1,0:T(8,128)(2,1)} custom-call(s32[12]{0:T(128)} %stack.38.refs_0_, bf16[432,640]{1,0:T(8,128)(2,1)} %copy-done.8, bf16[432,640]{1,0:T(8,128)(2,1)} %collective-permute-done.1.refs_2_, bf16[432,640]{1,0:T(8,128)(2,1)} %collective-permute-done.refs_3_, bf16[432,640]{1,0:T(8,128)(2,1)} %copy-done.12, bf16[432,640]{1,0:T(8,128)(2,1)} %copy-done.13, ...), custom_call_target="tpu_custom_call" | custom-call | flops 100000000 | bytes 65536 | tf_op jit(solution)/shard_map/mlp_block/pallas_call | solution.py:211
  245.3 12.2 %collective-permute-done.31 = bf16[432,512]{1,0:T(8,128)(2,1)S(1)} collective-permute-done((bf16[432,512]{1,0:T(8,128)(2,1)S(1)}, bf16[432,512]{1,0:T(8,128)(2,1)S(1)}, u32[]{:S(2)}, u32[]{:S(2)}) %collective-permute-start.31) | collective-permute-done | bytes 442400 | tf_op jit(solution)/shard_map/ppermute | solution.py:248
  262.1 17.7 %write_cache.1 = bf16[4,2,128,256]{3,2,1,0:T(8,128)(2,1)} custom-call(s32[4]{0:T(128)} %select_reduce_fusion.source_ref, bf16[8,128,512]{2,1,0:T(8,128)(2,1)} %copy-done.22), custom_call_target="tpu_custom_call" | custom-call | tf_op jit(solution)/shard_map/write_cache/pallas_call | solution.py:135
  279.9 9.7 %mlp_block.8 = bf16[432,256]{1,0:T(8,128)(2,1)} custom-call(s32[12]{0:T(128)} %stack.38.refs_0_, bf16[432,640]{1,0:T(8,128)(2,1)} %copy-done.8, bf16[432,640]{1,0:T(8,128)(2,1)} %collective-permute-done.1.refs_2_, bf16[432,640]{1,0:T(8,128)(2,1)} %collective-permute-done.refs_3_, bf16[432,640]{1,0:T(8,128)(2,1)} %copy-done.12, bf16[432,640]{1,0:T(8,128)(2,1)} %copy-done.13, ...), custom_call_target="tpu_custom_call" | custom-call | flops 100000000 | bytes 65536 | tf_op jit(solution)/shard_map/mlp_block/pallas_call | solution.py:211
  293.7 9.5 %mlp_block.9 = bf16[432,256]{1,0:T(8,128)(2,1)} custom-call(s32[12]{0:T(128)} %stack.38.refs_0_, bf16[432,640]{1,0:T(8,128)(2,1)} %copy-done.8, bf16[432,640]{1,0:T(8,128)(2,1)} %collective-permute-done.1.refs_2_, bf16[432,640]{1,0:T(8,128)(2,1)} %collective-permute-done.refs_3_, bf16[432,640]{1,0:T(8,128)(2,1)} %copy-done.12, bf16[432,640]{1,0:T(8,128)(2,1)} %copy-done.13, ...), custom_call_target="tpu_custom_call" | custom-call | flops 100000000 | bytes 65536 | tf_op jit(solution)/shard_map/mlp_block/pallas_call | solution.py:211
  305.8 7.2 %collective-permute-done.39 = bf16[432,256]{1,0:T(8,128)(2,1)S(1)} collective-permute-done((bf16[432,256]{1,0:T(8,128)(2,1)}, bf16[432,256]{1,0:T(8,128)(2,1)S(1)}, u32[]{:S(2)}, u32[]{:S(2)}) %collective-permute-start.39) | collective-permute-done | bytes 221216 | tf_op jit(solution)/shard_map/ppermute | solution.py:248
  (188 shorter events, 80.0 us)
Async XLA Ops:
  5.2 26.7 %collective-permute-start.1 = (bf16[432,640]{1,0:T(8,128)(2,1)S(1)}, bf16[432,640]{1,0:T(8,128)(2,1)}, u32[]{:S(2)}, u32[]{:S(2)}) collective-permute-start(bf16[432,640]{1,0:T(8,128)(2,1)S(1)} %get-tuple-element.122.refs_1_), channel_id=1, source_target_pairs={{0,4},{4,0},{8,12},{12,8},{16,20},{20,16},{24,28},{28,24},{1,5},{5... | collective-permute-start | bytes 1658888 | tf_op jit(solution)/shard_map/ppermute | solution.py:255
  8.2 27.1 %collective-permute-start = (bf16[432,640]{1,0:T(8,128)(2,1)}, bf16[432,640]{1,0:T(8,128)(2,1)}, u32[]{:S(2)}, u32[]{:S(2)}) collective-permute-start(bf16[432,640]{1,0:T(8,128)(2,1)} %dynamic-slice_bitcast_fusion), channel_id=1, source_target_pairs={{0,16},{4,20},{8,24},{12,28},{16,0},{20,4},{24,8},{28,12},{1,17},{... | collective-permute-start | bytes 1658888 | tf_op jit(solution)/shard_map/ppermute | solution.py:248
  35.3 27.7 %collective-permute-start.5 = (bf16[256,5120]{1,0:T(8,128)(2,1)}, bf16[256,5120]{1,0:T(8,128)(2,1)}, u32[]{:S(2)}, u32[]{:S(2)}) collective-permute-start(bf16[256,5120]{1,0:T(8,128)(2,1)} %convolution_convert_fusion), channel_id=1, source_target_pairs={{0,1},{1,0},{2,3},{3,2},{4,5},{5,4},{6,7},{7,6},{8,9},{9,8},{10,11... | collective-permute-start | bytes 7864328 | tf_op jit(solution)/shard_map/ppermute | solution.py:272
  35.3 27.7 %collective-permute-start.2 = (bf16[432,640]{1,0:T(8,128)(2,1)S(1)}, bf16[432,640]{1,0:T(8,128)(2,1)S(1)}, u32[]{:S(2)}, u32[]{:S(2)}) collective-permute-start(bf16[432,640]{1,0:T(8,128)(2,1)S(1)} %copy-done.32), channel_id=1, source_target_pairs={{0,16},{4,20},{8,24},{12,28},{16,0},{20,4},{24,8},{28,12},{1,17},{... | collective-permute-start | bytes 1658888 | tf_op jit(solution)/shard_map/ppermute | solution.py:248
  35.3 27.7 %collective-permute-start.3 = (bf16[432,640]{1,0:T(8,128)(2,1)S(1)}, bf16[432,640]{1,0:T(8,128)(2,1)S(1)}, u32[]{:S(2)}, u32[]{:S(2)}) collective-permute-start(bf16[432,640]{1,0:T(8,128)(2,1)S(1)} %get-tuple-element.67.refs_9_), channel_id=1, source_target_pairs={{0,4},{4,0},{8,12},{12,8},{16,20},{20,16},{24,28},{28,24},{1,5},{5... | collective-permute-start | bytes 1658888 | tf_op jit(solution)/shard_map/ppermute | solution.py:255
  35.8 27.2 %collective-permute-start.4 = (bf16[432,640]{1,0:T(8,128)(2,1)}, bf16[432,640]{1,0:T(8,128)(2,1)S(1)}, u32[]{:S(2)}, u32[]{:S(2)}) collective-permute-start(bf16[432,640]{1,0:T(8,128)(2,1)} %collective-permute-done.refs_3_), channel_id=1, source_target_pairs={{0,4},{4,0},{8,12},{12,8},{16,20},{20,16},{24,28},{28,24},{1,5},{5... | collective-permute-start | bytes 1658888 | tf_op jit(solution)/shard_map/ppermute | solution.py:255
  79.4 29.7 %collective-permute-start.11 = (bf16[128,5120]{1,0:T(8,128)(2,1)}, bf16[128,5120]{1,0:T(8,128)(2,1)}, u32[]{:S(2)}, u32[]{:S(2)}) collective-permute-start(bf16[128,5120]{1,0:T(8,128)(2,1)} %fusion.1), channel_id=1, source_target_pairs={{0,2},{1,3},{2,0},{3,1},{4,6},{5,7},{6,4},{7,5},{8,10},{9,11},{10,... | collective-permute-start | bytes 3932168 | tf_op jit(solution)/shard_map/ppermute | solution.py:347
  126.9 27.7 %collective-permute-start.14 = (bf16[128,5120]{1,0:T(8,128)(2,1)}, bf16[128,5120]{1,0:T(8,128)(2,1)S(1)}, u32[]{:S(2)}, u32[]{:S(2)}) collective-permute-start(bf16[128,5120]{1,0:T(8,128)(2,1)} %multiply_convert_fusion.refs_17_), channel_id=1, source_target_pairs={{0,8},{4,12},{8,0},{12,4},{16,24},{20,28},{24,16},{28,20},{1,9},{5... | collective-permute-start | bytes 3932168 | tf_op jit(solution)/shard_map/ppermute | solution.py:248
  127.0 27.6 %collective-permute-start.15 = (bf16[128,5120]{1,0:T(8,128)(2,1)}, bf16[128,5120]{1,0:T(8,128)(2,1)}, u32[]{:S(2)}, u32[]{:S(2)}) collective-permute-start(bf16[128,5120]{1,0:T(8,128)(2,1)} %multiply_convert_fusion.refs_17_), channel_id=1, source_target_pairs={{8,16},{12,20},{16,8},{20,12},{9,17},{13,21},{17,9},{21,13},{10,18... | collective-permute-start | bytes 3932168 | tf_op jit(solution)/shard_map/ppermute | solution.py:248
  128.7 27.4 %collective-permute-start.18 = (bf16[128,5120]{1,0:T(8,128)(2,1)}, bf16[128,5120]{1,0:T(8,128)(2,1)}, u32[]{:S(2)}, u32[]{:S(2)}) collective-permute-start(bf16[128,5120]{1,0:T(8,128)(2,1)} %multiply_convert_fusion.refs_17_), channel_id=1, source_target_pairs={{0,2},{1,3},{2,0},{3,1},{4,6},{5,7},{6,4},{7,5},{8,10},{9,11},{10,... | collective-permute-start | bytes 3932168 | tf_op jit(solution)/shard_map/ppermute | solution.py:263
  156.1 28.3 %collective-permute-start.19 = (bf16[128,5120]{1,0:T(8,128)(2,1)}, bf16[128,5120]{1,0:T(8,128)(2,1)}, u32[]{:S(2)}, u32[]{:S(2)}) collective-permute-start(bf16[128,5120]{1,0:T(8,128)(2,1)} %collective-permute-done.15), channel_id=1, source_target_pairs={{8,0},{12,4},{16,24},{20,28},{9,1},{13,5},{17,25},{21,29},{10,2},{... | collective-permute-start | bytes 3932168 | tf_op jit(solution)/shard_map/ppermute | solution.py:248
  157.4 27.0 %collective-permute-start.20 = (bf16[128,5120]{1,0:T(8,128)(2,1)S(1)}, bf16[128,5120]{1,0:T(8,128)(2,1)}, u32[]{:S(2)}, u32[]{:S(2)}) collective-permute-start(bf16[128,5120]{1,0:T(8,128)(2,1)S(1)} %collective-permute-done.14.refs_17_), channel_id=1, source_target_pairs={{8,16},{12,20},{16,8},{20,12},{9,17},{13,21},{17,9},{21,13},{10,18... | collective-permute-start | bytes 3932168 | tf_op jit(solution)/shard_map/ppermute | solution.py:248
  159.1 26.2 %collective-permute-start.21 = (bf16[128,5120]{1,0:T(8,128)(2,1)S(1)}, bf16[128,5120]{1,0:T(8,128)(2,1)}, u32[]{:S(2)}, u32[]{:S(2)}) collective-permute-start(bf16[128,5120]{1,0:T(8,128)(2,1)S(1)} %collective-permute-done.14.refs_17_), channel_id=1, source_target_pairs={{0,2},{1,3},{2,0},{3,1},{4,6},{5,7},{6,4},{7,5},{8,10},{9,11},{10,... | collective-permute-start | bytes 3932168 | tf_op jit(solution)/shard_map/ppermute | solution.py:263
  160.6 44.1 %collective-permute-start.26 = (bf16[128,5120]{1,0:T(8,128)(2,1)S(1)}, bf16[128,5120]{1,0:T(8,128)(2,1)}, u32[]{:S(2)}, u32[]{:S(2)}) collective-permute-start(bf16[128,5120]{1,0:T(8,128)(2,1)S(1)} %collective-permute-done.14.refs_17_), channel_id=1, source_target_pairs={{0,1},{1,0},{2,3},{3,2},{4,5},{5,4},{6,7},{7,6},{8,9},{9,8},{10,11... | collective-permute-start | bytes 3932168 | tf_op jit(solution)/shard_map/ppermute | solution.py:272
  187.9 31.5 %collective-permute-start.25 = (bf16[128,5120]{1,0:T(8,128)(2,1)}, bf16[128,5120]{1,0:T(8,128)(2,1)}, u32[]{:S(2)}, u32[]{:S(2)}) collective-permute-start(bf16[128,5120]{1,0:T(8,128)(2,1)} %broadcast_select_fusion.refs_17_), channel_id=1, source_target_pairs={{0,2},{1,3},{2,0},{3,1},{4,6},{5,7},{6,4},{7,5},{8,10},{9,11},{10,... | collective-permute-start | bytes 3932168 | tf_op jit(solution)/shard_map/ppermute | solution.py:263
  189.4 34.9 %collective-permute-start.24 = (bf16[128,5120]{1,0:T(8,128)(2,1)}, bf16[128,5120]{1,0:T(8,128)(2,1)}, u32[]{:S(2)}, u32[]{:S(2)}) collective-permute-start(bf16[128,5120]{1,0:T(8,128)(2,1)} %collective-permute-done.20), channel_id=1, source_target_pairs={{8,0},{12,4},{16,24},{20,28},{9,1},{13,5},{17,25},{21,29},{10,2},{... | collective-permute-start | bytes 3932168 | tf_op jit(solution)/shard_map/ppermute | solution.py:248
  191.5 40.8 %collective-permute-start.29 = (bf16[128,5120]{1,0:T(8,128)(2,1)}, bf16[128,5120]{1,0:T(8,128)(2,1)}, u32[]{:S(2)}, u32[]{:S(2)}) collective-permute-start(bf16[128,5120]{1,0:T(8,128)(2,1)} %broadcast_select_fusion.refs_17_), channel_id=1, source_target_pairs={{0,1},{1,0},{2,3},{3,2},{4,5},{5,4},{6,7},{7,6},{8,9},{9,8},{10,11... | collective-permute-start | bytes 3932168 | tf_op jit(solution)/shard_map/ppermute | solution.py:272
  224.3 33.2 %all-to-all-start = ((bf16[8,128,512]{2,1,0:T(8,128)(2,1)}), bf16[8,128,512]{2,1,0:T(8,128)(2,1)S(1)}, u32[]{:S(2)}, u32[]{:S(2)}) async-start(bf16[8,128,512]{2,1,0:T(8,128)(2,1)} %bitcast.26), calls=%async_computation | async-start | bytes 2097152 | tf_op jit(solution)/shard_map/all_to_all | solution.py:411
  230.0 27.5 %collective-permute-start.28 = (bf16[64,5120]{1,0:T(8,128)(2,1)S(1)}, bf16[64,5120]{1,0:T(8,128)(2,1)}, u32[]{:S(2)}, u32[]{:S(2)}) collective-permute-start(bf16[64,5120]{1,0:T(8,128)(2,1)S(1)} %get-tuple-element.120.refs_17_), channel_id=1, source_target_pairs={{0,2},{1,3},{2,0},{3,1},{4,6},{5,7},{6,4},{7,5},{8,10},{9,11},{10,... | collective-permute-start | bytes 1966088 | tf_op jit(solution)/shard_map/ppermute | solution.py:263
  230.6 26.9 %collective-permute-start.31 = (bf16[432,512]{1,0:T(8,128)(2,1)S(1)}, bf16[432,512]{1,0:T(8,128)(2,1)S(1)}, u32[]{:S(2)}, u32[]{:S(2)}) collective-permute-start(bf16[432,512]{1,0:T(8,128)(2,1)S(1)} %copy-done.33), channel_id=1, source_target_pairs={{0,8},{4,12},{8,0},{12,4},{16,24},{20,28},{24,16},{28,20},{1,9},{5... | collective-permute-start | bytes 1327112 | tf_op jit(solution)/shard_map/ppermute | solution.py:248
  232.3 47.6 %collective-permute-start.33 = (bf16[64,5120]{1,0:T(8,128)(2,1)S(1)}, bf16[64,5120]{1,0:T(8,128)(2,1)}, u32[]{:S(2)}, u32[]{:S(2)}) collective-permute-start(bf16[64,5120]{1,0:T(8,128)(2,1)S(1)} %get-tuple-element.120.refs_17_), channel_id=1, source_target_pairs={{0,1},{1,0},{2,3},{3,2},{4,5},{5,4},{6,7},{7,6},{8,9},{9,8},{10,11... | collective-permute-start | bytes 1966088 | tf_op jit(solution)/shard_map/ppermute | solution.py:272
  258.2 31.3 %collective-permute-start.32 = (bf16[64,5120]{1,0:T(8,128)(2,1)S(1)}, bf16[64,5120]{1,0:T(8,128)(2,1)S(1)}, u32[]{:S(2)}, u32[]{:S(2)}) collective-permute-start(bf16[64,5120]{1,0:T(8,128)(2,1)S(1)} %get-tuple-element.108.refs_17_), channel_id=1, source_target_pairs={{0,2},{1,3},{2,0},{3,1},{4,6},{5,7},{6,4},{7,5},{8,10},{9,11},{10,... | collective-permute-start | bytes 1966088 | tf_op jit(solution)/shard_map/ppermute | solution.py:263
  258.7 30.8 %collective-permute-start.35 = (bf16[432,512]{1,0:T(8,128)(2,1)}, bf16[432,512]{1,0:T(8,128)(2,1)S(1)}, u32[]{:S(2)}, u32[]{:S(2)}) collective-permute-start(bf16[432,512]{1,0:T(8,128)(2,1)} %mlp_block.7), channel_id=1, source_target_pairs={{0,16},{4,20},{8,24},{12,28},{16,0},{20,4},{24,8},{28,12},{1,17},{... | collective-permute-start | bytes 1327112 | tf_op jit(solution)/shard_map/ppermute | solution.py:248
  262.1 31.6 %collective-permute-start.37 = (bf16[64,5120]{1,0:T(8,128)(2,1)S(1)}, bf16[64,5120]{1,0:T(8,128)(2,1)}, u32[]{:S(2)}, u32[]{:S(2)}) collective-permute-start(bf16[64,5120]{1,0:T(8,128)(2,1)S(1)} %get-tuple-element.108.refs_17_), channel_id=1, source_target_pairs={{0,1},{1,0},{2,3},{3,2},{4,5},{5,4},{6,7},{7,6},{8,9},{9,8},{10,11... | collective-permute-start | bytes 1966088 | tf_op jit(solution)/shard_map/ppermute | solution.py:272
  (61 other events, 950.5 us)

commit v2 on v1

--- a/solution.py
+++ b/solution.py
@@ -113,31 +113,20 @@
       slots[None])
 
 
-def cache_kernel(source_ref, in_ref, out_ref, sems):
-    copies = []
+def cache_kernel(source_ref, in_ref, out_ref):
     for page in range(out_ref.shape[0]):
         for head in range(out_ref.shape[1]):
-            copies.append(
-                pltpu.make_async_copy(
-                    in_ref.at[source_ref[page], :, pl.ds(head * 2 * HD, 2 * HD)],
-                    out_ref.at[page, head],
-                    sems.at[page, head],
-                )
-            )
-    for copy in copies:
-        copy.start()
-    for copy in copies:
-        copy.wait()
+            out_ref[page, head] = in_ref[source_ref[page], :, head * 2 * HD:(head + 1) * 2 * HD]
 
 
 def write_cache(sources, pages_in, kv_heads):
-    anywhere = pl.BlockSpec(memory_space=pl.ANY)
+    vmem = pl.BlockSpec(memory_space=pltpu.VMEM)
     return pl.pallas_call(
         cache_kernel,
         out_shape=jax.ShapeDtypeStruct((REQS, kv_heads, PAGE, 2 * HD), jnp.bfloat16),
-        in_specs=[pl.BlockSpec(memory_space=pltpu.SMEM), anywhere],
-        out_specs=anywhere,
-        scratch_shapes=[pltpu.SemaphoreType.DMA((REQS, kv_heads))],
+        in_specs=[pl.BlockSpec(memory_space=pltpu.SMEM), vmem],
+        out_specs=vmem,
+        cost_estimate=pl.CostEstimate(flops=0, bytes_accessed=2**16, transcendentals=0),
         name="write_cache",
     )(sources, pages_in)
 
@@ -146,7 +135,8 @@
     weights = (refs[:count], refs[count:2 * count])
     rows_in = refs[2 * count:2 * count + pieces]
     out_ref, gate_buf, up_buf, row_buf, acc, weight_sems, row_sems = refs[2 * count + pieces:]
-    depth = weights[0][0].shape[1]
+    units, depth = weights[0][0].shape
+    parts = weight_sems.shape[2]
     piece = rows_in[0].shape[0] // halves
     first, second = [], []
     for index in range(pieces):
@@ -161,9 +151,13 @@
             )
     for index in range(count):
         for which, buf in ((0, gate_buf), (1, up_buf)):
-            second.append(
-                pltpu.make_async_copy(weights[which][index], buf.at[index], weight_sems.at[which, index])
-            )
+            for part in range(parts):
+                some = pl.ds(part * (units // parts), units // parts)
+                second.append(
+                    pltpu.make_async_copy(
+                        weights[which][index].at[some, :], buf.at[index, some, :], weight_sems.at[which, index, part]
+                    )
+                )
     for copy in first + second:
         copy.start()
     for copy in first:
@@ -171,8 +165,8 @@
     tokens = out_ref.shape[1]
     tile = min(256, tokens)
     for index in range(count):
-        second[2 * index].wait()
-        second[2 * index + 1].wait()
+        for copy in second[2 * parts * index:2 * parts * (index + 1)]:
+            copy.wait()
         at = pl.multiple_of(ids_ref[index] * depth, depth)
         for start in range(0, tokens, tile):
             block = row_buf[start:start + tile, pl.ds(at, depth)]
@@ -218,7 +212,7 @@
             pltpu.VMEM((count, units, depth), jnp.bfloat16),
             pltpu.VMEM((tokens, width), jnp.bfloat16),
             pltpu.VMEM((2, units, tokens), jnp.float32),
-            pltpu.SemaphoreType.DMA((2, count)),
+            pltpu.SemaphoreType.DMA((2, count, 3 if units % 48 == 0 else 1)),
             pltpu.SemaphoreType.DMA((pieces, halves)),
         ],
         compiler_params=pltpu.CompilerParams(vmem_limit_bytes=60 * 2**20),
@@ -395,32 +389,33 @@
 
     pieces_0 = shared(near, near_x)
     next_2e, next_2m, next_1_x, pieces_0 = lax.optimization_barrier((next_2e, next_2m, next_1_x, pieces_0))
+    kv_send = after(kv_send, next_2e, next_2m)
+    kv_in = lax.all_to_all(
+        kv_send.reshape(n_req, PAGE, 2 * kv_heads * HD), "req", split_axis=0, concat_axis=0, tiled=True
+    )
     next_3 = along_z(next_2m, outward)
     next_2 = jnp.where(at_end, next_2e, next_2m)
     next_2_x = along_x(next_2)
     hidden_0 = work(pieces_0)
     hidden_1 = work(shared(next_1, next_1_x))
-    next_3, next_2_x, hidden_0, hidden_1, kv_send = lax.optimization_barrier(
-        (next_3, next_2_x, hidden_0, hidden_1, kv_send)
+    next_3, next_2_x, hidden_0, hidden_1, kv_in = lax.optimization_barrier(
+        (next_3, next_2_x, hidden_0, hidden_1, kv_in)
     )
     next_3a = jnp.where(at_end, next_3[:run], middle_1[:run])
     next_3b = jnp.where(at_end, next_3[run:], middle_1[run:])
     next_3a_x = along_x(next_3a)
     hidden_2 = work(shared(next_2, next_2_x))
     back_1 = along_z(hidden_1, flip[1])
-    kv_in = lax.all_to_all(
-        kv_send.reshape(n_req, PAGE, 2 * kv_heads * HD), "req", split_axis=0, concat_axis=0, tiled=True
-    )
-    next_3b, next_3a_x, hidden_2, back_1, kv_in = lax.optimization_barrier(
-        (next_3b, next_3a_x, hidden_2, back_1, kv_in)
+    mine = page_table[None] == (me_req * REQS + jnp.arange(REQS, dtype=jnp.int32))[:, None, None]
+    sources = jnp.sum(jnp.where(mine, jnp.arange(n_req, dtype=jnp.int32)[None, :, None], 0), axis=(1, 2))
+    cache_out = write_cache(sources.astype(jnp.int32), kv_in, kv_heads)
+    next_3b, next_3a_x, hidden_2, back_1, cache_out = lax.optimization_barrier(
+        (next_3b, next_3a_x, hidden_2, back_1, cache_out)
     )
     next_3b_x = along_x(next_3b)
     back_2 = along_z(hidden_2, flip[2])
     hidden_3a = work(shared(next_3a, next_3a_x))
-    mine = page_table[None] == (me_req * REQS + jnp.arange(REQS, dtype=jnp.int32))[:, None, None]
-    sources = jnp.sum(jnp.where(mine, jnp.arange(n_req, dtype=jnp.int32)[None, :, None], 0), axis=(1, 2))
-    cache_out = write_cache(sources.astype(jnp.int32), kv_in, kv_heads)
-    next_3b_x, hidden_3a, back_2, cache_out = lax.optimization_barrier((next_3b_x, hidden_3a, back_2, cache_out))
+    next_3b_x, hidden_3a = lax.optimization_barrier((next_3b_x, hidden_3a))
     back_3a = along_z(hidden_3a, flip[3])
     back_3b = along_z(work(shared(next_3b, next_3b_x)), flip[3])
     hidden_t = jnp.zeros((units_all, rows), jnp.bfloat16)

time: 315 us -> 316 us (level); the launches traced: 314 us -> 310 us
  Pallas kernels: 80.3 us -> 66.8 us
  waiting for transfers between devices: 144 us -> 149 us
  local copies, waits for them, and re-layouts: 17.5 us -> 21.3 us
    pallas_call x1, Pallas kernels: 17.7 us -> 2.06 us  [write_cache(): pl.pallas_call(cache_kernel, out_shape=jax.ShapeDtypeStruct((REQS, kv_hea...]
    unnamed x88 -> x90, local copies, waits for them, and re-layouts: 5.39 us -> 8.14 us
  transfers between devices with their start and end apart: 41 -> 41, of which waited for: 19 -> 20; matrix products, arithmetic and copies ran while one was open for 10% -> 11% of each run, Pallas kernels for 26% -> 22%
where the time goes in v2:
time: 316 us; the launch traced here: 310 us
  waiting for transfers between devices  149 us (47%)
  Pallas kernels  66.8 us (21%)
  starting transfers between devices  44.2 us (14%)
  local copies, waits for them, and re-layouts  21.3 us (7%)
  other arithmetic  16.8 us (5%)
  matrix products  10.8 us (3%)
    ppermute x15, waiting for transfers between devices, along_z(): lax.ppermute(value, 'req', [(a * n_y + c, b * n_y + c) for a, b in moves...  108 us
    pallas_call x5, Pallas kernels, mlp_block(): pl.pallas_call(lambda *refs: mlp_kernel(count, pieces, halves, *refs), ou...  60.2 us
    ppermute x8, waiting for transfers between devices, along_y(): lax.ppermute(value, 'req', [(a * n_y + b, a * n_y + (b + step) % n_y) for...  29.3 us
    ppermute x15, starting transfers between devices, along_z(): lax.ppermute(value, 'req', [(a * n_y + c, b * n_y + c) for a, b in moves...  20.1 us
    dot_general x2, matrix products, project(): jnp.dot(picked, w_out, preferred_element_type=jnp.float32)  10.8 us
    ppermute x8, starting transfers between devices, along_y(): lax.ppermute(value, 'req', [(a * n_y + b, a * n_y + (b + step) % n_y) for...  8.6 us
    unnamed x90, local copies, waits for them, and re-layouts  8.14 us
    dynamic_slice x3, local copies, waits for them, and re-layouts, share(): lax.dynamic_slice(weight_t, ((z + shift) % N_Z * units, 0), (units, depth))  7.38 us
  transfers between devices with their start and end apart: 41, of which 20 were waited for; matrix products, arithmetic and copies ran while one was open for 11% of the time, Pallas kernels for 22%

profile of v2, /device:TPU:0, one launch (start us, length us, event | category | flops | bytes accessed | tf_op | source)
XLA Modules:
  0.0 310.5 jit_solution(10340994130585660068)
XLA Ops:
  16.6 4.5 %attention.1 = (bf16[512,768]{1,0:T(8,128)(2,1)S(1)}, bf16[1024,512]{1,0:T(8,128)(2,1)}) custom-call(bf16[512,768]{1,0:T(8,128)(2,1)S(1)} %copy-done, bf16[512,256]{1,0:T(8,128)(2,1)S(1)} %copy-done.1, bf16[512,256]{1,0:T(8,128)(2,1)S(1)} %copy-done.2, f32[1,768]{1,0:T(1,128)S(1)} %broadcast_in_dim.71.refs_3_, f32[1,256]{1,0:T(1,128)S(1)} %bitcast.46, ...), custom_call_target="tpu_custom_call" | custom-call | flops 100000000 | bytes 65536 | tf_op jit(solution)/shard_map/attention/pallas_call | solution.py:95
  21.1 7.1 %convolution_convert_fusion = bf16[256,5120]{1,0:T(8,128)(2,1)} fusion(bf16[768,5120]{1,0:T(8,128)(2,1)} %param.23, bf16[2,256,768]{2,1,0:T(8,128)(2,1)S(1)} %bitcast.48, s32[]{:T(128)S(6)} %select_n.201), kind=kOutput, calls=%fused_computation | convolution fusion | flops 2014576640 | bytes 10878980 | tf_op jit(solution)/shard_map/dot_general | solution.py:313
  28.2 3.8 %convolution_convert_fusion.1 = bf16[256,5120]{1,0:T(8,128)(2,1)} fusion(bf16[768,5120]{1,0:T(8,128)(2,1)S(1)} %bitcast.57, bf16[2,256,768]{2,1,0:T(8,128)(2,1)S(1)} %bitcast.49, s32[]{:T(128)S(6)} %select_n.200), kind=kOutput, calls=%fused_computation.1 | convolution fusion | flops 2014576640 | bytes 10878980 | tf_op jit(solution)/shard_map/dot_general | solution.py:313
  32.0 3.2 %collective-permute-done.refs_3_ = bf16[432,640]{1,0:T(8,128)(2,1)} collective-permute-done((bf16[432,640]{1,0:T(8,128)(2,1)}, bf16[432,640]{1,0:T(8,128)(2,1)}, u32[]{:S(2)}, u32[]{:S(2)}) %collective-permute-start) | collective-permute-done | bytes 552992 | tf_op jit(solution)/shard_map/ppermute | solution.py:242
  37.4 25.6 %collective-permute-done.2.refs_11_ = bf16[432,640]{1,0:T(8,128)(2,1)S(1)} collective-permute-done((bf16[432,640]{1,0:T(8,128)(2,1)S(1)}, bf16[432,640]{1,0:T(8,128)(2,1)S(1)}, u32[]{:S(2)}, u32[]{:S(2)}) %collective-permute-start.2) | collective-permute-done | bytes 552992 | tf_op jit(solution)/shard_map/ppermute | solution.py:242
  66.3 3.4 %convert_add_fusion = f32[256,5120]{1,0:T(8,128)S(1)} fusion(bf16[256,5120]{1,0:T(8,128)(2,1)} %collective-permute-done.5, bf16[256,5120]{1,0:T(8,128)(2,1)} %convolution_convert_fusion.1), kind=kLoop, calls=%fused_computation.2 | loop fusion | flops 3932160 | bytes 10485760 | tf_op jit(solution)/shard_map/add | solution.py:329
  73.3 5.9 %collective-permute-done.6.refs_5_ = bf16[432,640]{1,0:T(8,128)(2,1)S(1)} collective-permute-done((bf16[432,640]{1,0:T(8,128)(2,1)}, bf16[432,640]{1,0:T(8,128)(2,1)S(1)}, u32[]{:S(2)}, u32[]{:S(2)}) %collective-permute-start.6) | collective-permute-done | bytes 552992 | tf_op jit(solution)/shard_map/ppermute | solution.py:242
  85.0 8.8 %collective-permute-done.10.refs_6_ = bf16[432,640]{1,0:T(8,128)(2,1)S(1)} collective-permute-done((bf16[432,640]{1,0:T(8,128)(2,1)S(1)}, bf16[432,640]{1,0:T(8,128)(2,1)S(1)}, u32[]{:S(2)}, u32[]{:S(2)}) %collective-permute-start.10) | collective-permute-done | bytes 552992 | tf_op jit(solution)/shard_map/ppermute | solution.py:249
  93.8 3.1 collective-permute-done.8.refs_7_
  96.9 9.0 %collective-permute-done.9.refs_15_ = bf16[432,640]{1,0:T(8,128)(2,1)S(1)} collective-permute-done((bf16[432,640]{1,0:T(8,128)(2,1)S(1)}, bf16[432,640]{1,0:T(8,128)(2,1)S(1)}, u32[]{:S(2)}, u32[]{:S(2)}) %collective-permute-start.9) | collective-permute-done | bytes 552992 | tf_op jit(solution)/shard_map/ppermute | solution.py:242
  105.8 3.3 %collective-permute-done.11 = bf16[128,5120]{1,0:T(8,128)(2,1)} collective-permute-done((bf16[128,5120]{1,0:T(8,128)(2,1)}, bf16[128,5120]{1,0:T(8,128)(2,1)}, u32[]{:S(2)}, u32[]{:S(2)}) %collective-permute-start.11) | collective-permute-done | bytes 1310752 | tf_op jit(solution)/shard_map/ppermute | solution.py:341
  116.0 10.7 %collective-permute-done.12.refs_13_ = bf16[432,640]{1,0:T(8,128)(2,1)S(1)} collective-permute-done((bf16[432,640]{1,0:T(8,128)(2,1)S(1)}, bf16[432,640]{1,0:T(8,128)(2,1)S(1)}, u32[]{:S(2)}, u32[]{:S(2)}) %collective-permute-start.12) | collective-permute-done | bytes 552992 | tf_op jit(solution)/shard_map/ppermute | solution.py:242
  132.0 13.4 %collective-permute-done.17.refs_16_ = bf16[432,640]{1,0:T(8,128)(2,1)S(1)} collective-permute-done((bf16[432,640]{1,0:T(8,128)(2,1)S(1)}, bf16[432,640]{1,0:T(8,128)(2,1)S(1)}, u32[]{:S(2)}, u32[]{:S(2)}) %collective-permute-start.17) | collective-permute-done | bytes 552992 | tf_op jit(solution)/shard_map/ppermute | solution.py:249
  145.5 6.9 %collective-permute-done.16.refs_14_ = bf16[432,640]{1,0:T(8,128)(2,1)S(1)} collective-permute-done((bf16[432,640]{1,0:T(8,128)(2,1)S(1)}, bf16[432,640]{1,0:T(8,128)(2,1)S(1)}, u32[]{:S(2)}, u32[]{:S(2)}) %collective-permute-start.16) | collective-permute-done | bytes 552992 | tf_op jit(solution)/shard_map/ppermute | solution.py:249
  160.9 23.3 %collective-permute-done.19 = bf16[128,5120]{1,0:T(8,128)(2,1)} collective-permute-done((bf16[128,5120]{1,0:T(8,128)(2,1)}, bf16[128,5120]{1,0:T(8,128)(2,1)}, u32[]{:S(2)}, u32[]{:S(2)}) %collective-permute-start.19) | collective-permute-done | bytes 1310752 | tf_op jit(solution)/shard_map/ppermute | solution.py:242
  185.2 6.1 %all-to-all-start = ((bf16[8,128,512]{2,1,0:T(8,128)(2,1)}), bf16[8,128,512]{2,1,0:T(8,128)(2,1)}, u32[]{:S(2)}, u32[]{:S(2)}) async-start(bf16[8,128,512]{2,1,0:T(8,128)(2,1)} %bitcast.26), calls=%async_computation | async-start | bytes 2097152 | tf_op jit(solution)/shard_map/all_to_all | solution.py:393
  197.9 13.4 %mlp_block.5 = bf16[432,512]{1,0:T(8,128)(2,1)} custom-call(s32[12]{0:T(128)} %stack.38.refs_0_, bf16[432,640]{1,0:T(8,128)(2,1)} %copy-done.8, bf16[432,640]{1,0:T(8,128)(2,1)} %collective-permute-done.1.refs_2_, bf16[432,640]{1,0:T(8,128)(2,1)} %collective-permute-done.refs_3_, bf16[432,640]{1,0:T(8,128)(2,1)} %copy-done.12, bf16[432,640]{1,0:T(8,128)(2,1)} %copy-done.13, ...), custom_call_target="tpu_custom_call" | custom-call | flops 100000000 | bytes 65536 | tf_op jit(solution)/shard_map/mlp_block/pallas_call | solution.py:205
  211.3 13.4 %mlp_block.6 = bf16[432,512]{1,0:T(8,128)(2,1)} custom-call(s32[12]{0:T(128)} %stack.38.refs_0_, bf16[432,640]{1,0:T(8,128)(2,1)} %copy-done.8, bf16[432,640]{1,0:T(8,128)(2,1)} %collective-permute-done.1.refs_2_, bf16[432,640]{1,0:T(8,128)(2,1)} %collective-permute-done.refs_3_, bf16[432,640]{1,0:T(8,128)(2,1)} %copy-done.12, bf16[432,640]{1,0:T(8,128)(2,1)} %copy-done.13, ...), custom_call_target="tpu_custom_call" | custom-call | flops 100000000 | bytes 65536 | tf_op jit(solution)/shard_map/mlp_block/pallas_call | solution.py:205
  225.4 9.8 %collective-permute-done.24 = bf16[128,5120]{1,0:T(8,128)(2,1)S(1)} collective-permute-done((bf16[128,5120]{1,0:T(8,128)(2,1)}, bf16[128,5120]{1,0:T(8,128)(2,1)S(1)}, u32[]{:S(2)}, u32[]{:S(2)}) %collective-permute-start.24) | collective-permute-done | bytes 1310752 | tf_op jit(solution)/shard_map/ppermute | solution.py:242
  243.5 13.5 %mlp_block.7 = bf16[432,512]{1,0:T(8,128)(2,1)} custom-call(s32[12]{0:T(128)} %stack.38.refs_0_, bf16[432,640]{1,0:T(8,128)(2,1)} %copy-done.8, bf16[432,640]{1,0:T(8,128)(2,1)} %collective-permute-done.1.refs_2_, bf16[432,640]{1,0:T(8,128)(2,1)} %collective-permute-done.refs_3_, bf16[432,640]{1,0:T(8,128)(2,1)} %copy-done.12, bf16[432,640]{1,0:T(8,128)(2,1)} %copy-done.13, ...), custom_call_target="tpu_custom_call" | custom-call | flops 100000000 | bytes 65536 | tf_op jit(solution)/shard_map/mlp_block/pallas_call | solution.py:205
  261.0 10.0 %mlp_block.8 = bf16[432,256]{1,0:T(8,128)(2,1)} custom-call(s32[12]{0:T(128)} %stack.38.refs_0_, bf16[432,640]{1,0:T(8,128)(2,1)} %copy-done.8, bf16[432,640]{1,0:T(8,128)(2,1)} %collective-permute-done.1.refs_2_, bf16[432,640]{1,0:T(8,128)(2,1)} %collective-permute-done.refs_3_, bf16[432,640]{1,0:T(8,128)(2,1)} %copy-done.12, bf16[432,640]{1,0:T(8,128)(2,1)} %copy-done.13, ...), custom_call_target="tpu_custom_call" | custom-call | flops 100000000 | bytes 65536 | tf_op jit(solution)/shard_map/mlp_block/pallas_call | solution.py:205
  271.0 3.9 %collective-permute-done.33.refs_18_ = bf16[64,5120]{1,0:T(8,128)(2,1)S(1)} collective-permute-done((bf16[64,5120]{1,0:T(8,128)(2,1)S(1)}, bf16[64,5120]{1,0:T(8,128)(2,1)S(1)}, u32[]{:S(2)}, u32[]{:S(2)}) %collective-permute-start.33) | collective-permute-done | bytes 655392 | tf_op jit(solution)/shard_map/ppermute | solution.py:257
  281.2 9.9 %mlp_block.9 = bf16[432,256]{1,0:T(8,128)(2,1)} custom-call(s32[12]{0:T(128)} %stack.38.refs_0_, bf16[432,640]{1,0:T(8,128)(2,1)} %copy-done.8, bf16[432,640]{1,0:T(8,128)(2,1)} %collective-permute-done.1.refs_2_, bf16[432,640]{1,0:T(8,128)(2,1)} %collective-permute-done.refs_3_, bf16[432,640]{1,0:T(8,128)(2,1)} %copy-done.12, bf16[432,640]{1,0:T(8,128)(2,1)} %copy-done.13, ...), custom_call_target="tpu_custom_call" | custom-call | flops 100000000 | bytes 65536 | tf_op jit(solution)/shard_map/mlp_block/pallas_call | solution.py:205
  292.7 15.5 %collective-permute-done.32 = bf16[432,512]{1,0:T(8,128)(2,1)} collective-permute-done((bf16[432,512]{1,0:T(8,128)(2,1)}, bf16[432,512]{1,0:T(8,128)(2,1)}, u32[]{:S(2)}, u32[]{:S(2)}) %collective-permute-start.32) | collective-permute-done | bytes 442400 | tf_op jit(solution)/shard_map/ppermute | solution.py:242
  (190 shorter events, 81.5 us)
Async XLA Ops:
  5.2 26.8 %collective-permute-start.1 = (bf16[432,640]{1,0:T(8,128)(2,1)S(1)}, bf16[432,640]{1,0:T(8,128)(2,1)}, u32[]{:S(2)}, u32[]{:S(2)}) collective-permute-start(bf16[432,640]{1,0:T(8,128)(2,1)S(1)} %get-tuple-element.120.refs_1_), channel_id=1, source_target_pairs={{0,4},{4,0},{8,12},{12,8},{16,20},{20,16},{24,28},{28,24},{1,5},{5... | collective-permute-start | bytes 1658888 | tf_op jit(solution)/shard_map/ppermute | solution.py:249
  8.2 27.1 %collective-permute-start = (bf16[432,640]{1,0:T(8,128)(2,1)}, bf16[432,640]{1,0:T(8,128)(2,1)}, u32[]{:S(2)}, u32[]{:S(2)}) collective-permute-start(bf16[432,640]{1,0:T(8,128)(2,1)} %dynamic-slice_bitcast_fusion), channel_id=1, source_target_pairs={{0,16},{4,20},{8,24},{12,28},{16,0},{20,4},{24,8},{28,12},{1,17},{... | collective-permute-start | bytes 1658888 | tf_op jit(solution)/shard_map/ppermute | solution.py:242
  35.2 27.7 %collective-permute-start.5 = (bf16[256,5120]{1,0:T(8,128)(2,1)}, bf16[256,5120]{1,0:T(8,128)(2,1)}, u32[]{:S(2)}, u32[]{:S(2)}) collective-permute-start(bf16[256,5120]{1,0:T(8,128)(2,1)} %convolution_convert_fusion), channel_id=1, source_target_pairs={{0,1},{1,0},{2,3},{3,2},{4,5},{5,4},{6,7},{7,6},{8,9},{9,8},{10,11... | collective-permute-start | bytes 7864328 | tf_op jit(solution)/shard_map/ppermute | solution.py:266
  35.2 27.7 %collective-permute-start.2 = (bf16[432,640]{1,0:T(8,128)(2,1)S(1)}, bf16[432,640]{1,0:T(8,128)(2,1)S(1)}, u32[]{:S(2)}, u32[]{:S(2)}) collective-permute-start(bf16[432,640]{1,0:T(8,128)(2,1)S(1)} %copy-done.35), channel_id=1, source_target_pairs={{0,16},{4,20},{8,24},{12,28},{16,0},{20,4},{24,8},{28,12},{1,17},{... | collective-permute-start | bytes 1658888 | tf_op jit(solution)/shard_map/ppermute | solution.py:242
  35.3 27.7 %collective-permute-start.3 = (bf16[432,640]{1,0:T(8,128)(2,1)S(1)}, bf16[432,640]{1,0:T(8,128)(2,1)S(1)}, u32[]{:S(2)}, u32[]{:S(2)}) collective-permute-start(bf16[432,640]{1,0:T(8,128)(2,1)S(1)} %get-tuple-element.66.refs_9_), channel_id=1, source_target_pairs={{0,4},{4,0},{8,12},{12,8},{16,20},{20,16},{24,28},{28,24},{1,5},{5... | collective-permute-start | bytes 1658888 | tf_op jit(solution)/shard_map/ppermute | solution.py:249
  35.8 27.2 %collective-permute-start.4 = (bf16[432,640]{1,0:T(8,128)(2,1)}, bf16[432,640]{1,0:T(8,128)(2,1)S(1)}, u32[]{:S(2)}, u32[]{:S(2)}) collective-permute-start(bf16[432,640]{1,0:T(8,128)(2,1)} %collective-permute-done.refs_3_), channel_id=1, source_target_pairs={{0,4},{4,0},{8,12},{12,8},{16,20},{20,16},{24,28},{28,24},{1,5},{5... | collective-permute-start | bytes 1658888 | tf_op jit(solution)/shard_map/ppermute | solution.py:249
  79.4 29.7 %collective-permute-start.11 = (bf16[128,5120]{1,0:T(8,128)(2,1)}, bf16[128,5120]{1,0:T(8,128)(2,1)}, u32[]{:S(2)}, u32[]{:S(2)}) collective-permute-start(bf16[128,5120]{1,0:T(8,128)(2,1)} %fusion.1), channel_id=1, source_target_pairs={{0,2},{1,3},{2,0},{3,1},{4,6},{5,7},{6,4},{7,5},{8,10},{9,11},{10,... | collective-permute-start | bytes 3932168 | tf_op jit(solution)/shard_map/ppermute | solution.py:341
  82.7 23.1 %collective-permute-start.9 = (bf16[432,640]{1,0:T(8,128)(2,1)S(1)}, bf16[432,640]{1,0:T(8,128)(2,1)S(1)}, u32[]{:S(2)}, u32[]{:S(2)}) collective-permute-start(bf16[432,640]{1,0:T(8,128)(2,1)S(1)} %copy-done.34), channel_id=1, source_target_pairs={{0,24},{4,28},{8,0},{12,4},{16,8},{20,12},{24,16},{28,20},{1,25},{... | collective-permute-start | bytes 1658888 | tf_op jit(solution)/shard_map/ppermute | solution.py:242
  126.7 27.7 %collective-permute-start.14 = (bf16[128,5120]{1,0:T(8,128)(2,1)}, bf16[128,5120]{1,0:T(8,128)(2,1)S(1)}, u32[]{:S(2)}, u32[]{:S(2)}) collective-permute-start(bf16[128,5120]{1,0:T(8,128)(2,1)} %multiply_convert_fusion.refs_17_), channel_id=1, source_target_pairs={{0,8},{4,12},{8,0},{12,4},{16,24},{20,28},{24,16},{28,20},{1,9},{5... | collective-permute-start | bytes 3932168 | tf_op jit(solution)/shard_map/ppermute | solution.py:242
  126.8 27.6 %collective-permute-start.15 = (bf16[128,5120]{1,0:T(8,128)(2,1)}, bf16[128,5120]{1,0:T(8,128)(2,1)}, u32[]{:S(2)}, u32[]{:S(2)}) collective-permute-start(bf16[128,5120]{1,0:T(8,128)(2,1)} %multiply_convert_fusion.refs_17_), channel_id=1, source_target_pairs={{8,16},{12,20},{16,8},{20,12},{9,17},{13,21},{17,9},{21,13},{10,18... | collective-permute-start | bytes 3932168 | tf_op jit(solution)/shard_map/ppermute | solution.py:242
  128.5 27.4 %collective-permute-start.18 = (bf16[128,5120]{1,0:T(8,128)(2,1)}, bf16[128,5120]{1,0:T(8,128)(2,1)}, u32[]{:S(2)}, u32[]{:S(2)}) collective-permute-start(bf16[128,5120]{1,0:T(8,128)(2,1)} %multiply_convert_fusion.refs_17_), channel_id=1, source_target_pairs={{0,2},{1,3},{2,0},{3,1},{4,6},{5,7},{6,4},{7,5},{8,10},{9,11},{10,... | collective-permute-start | bytes 3932168 | tf_op jit(solution)/shard_map/ppermute | solution.py:257
  130.5 21.9 %collective-permute-start.16 = (bf16[432,640]{1,0:T(8,128)(2,1)S(1)}, bf16[432,640]{1,0:T(8,128)(2,1)S(1)}, u32[]{:S(2)}, u32[]{:S(2)}) collective-permute-start(bf16[432,640]{1,0:T(8,128)(2,1)S(1)} %collective-permute-done.12.refs_13_), channel_id=1, source_target_pairs={{0,4},{4,0},{8,12},{12,8},{16,20},{20,16},{24,28},{28,24},{1,5},{5... | collective-permute-start | bytes 1658888 | tf_op jit(solution)/shard_map/ppermute | solution.py:249
  155.9 28.3 %collective-permute-start.19 = (bf16[128,5120]{1,0:T(8,128)(2,1)}, bf16[128,5120]{1,0:T(8,128)(2,1)}, u32[]{:S(2)}, u32[]{:S(2)}) collective-permute-start(bf16[128,5120]{1,0:T(8,128)(2,1)} %collective-permute-done.15), channel_id=1, source_target_pairs={{8,0},{12,4},{16,24},{20,28},{9,1},{13,5},{17,25},{21,29},{10,2},{... | collective-permute-start | bytes 3932168 | tf_op jit(solution)/shard_map/ppermute | solution.py:242
  157.2 27.0 %collective-permute-start.20 = (bf16[128,5120]{1,0:T(8,128)(2,1)S(1)}, bf16[128,5120]{1,0:T(8,128)(2,1)}, u32[]{:S(2)}, u32[]{:S(2)}) collective-permute-start(bf16[128,5120]{1,0:T(8,128)(2,1)S(1)} %collective-permute-done.14.refs_17_), channel_id=1, source_target_pairs={{8,16},{12,20},{16,8},{20,12},{9,17},{13,21},{17,9},{21,13},{10,18... | collective-permute-start | bytes 3932168 | tf_op jit(solution)/shard_map/ppermute | solution.py:242
  158.9 26.2 %collective-permute-start.21 = (bf16[128,5120]{1,0:T(8,128)(2,1)S(1)}, bf16[128,5120]{1,0:T(8,128)(2,1)}, u32[]{:S(2)}, u32[]{:S(2)}) collective-permute-start(bf16[128,5120]{1,0:T(8,128)(2,1)S(1)} %collective-permute-done.14.refs_17_), channel_id=1, source_target_pairs={{0,2},{1,3},{2,0},{3,1},{4,6},{5,7},{6,4},{7,5},{8,10},{9,11},{10,... | collective-permute-start | bytes 3932168 | tf_op jit(solution)/shard_map/ppermute | solution.py:257
  160.4 24.7 %collective-permute-start.23 = (bf16[128,5120]{1,0:T(8,128)(2,1)}, bf16[128,5120]{1,0:T(8,128)(2,1)}, u32[]{:S(2)}, u32[]{:S(2)}) collective-permute-start(bf16[128,5120]{1,0:T(8,128)(2,1)} %collective-permute-done.18.refs_18_), channel_id=1, source_target_pairs={{0,1},{1,0},{2,3},{3,2},{4,5},{5,4},{6,7},{7,6},{8,9},{9,8},{10,11... | collective-permute-start | bytes 3932168 | tf_op jit(solution)/shard_map/ppermute | solution.py:266
  160.4 50.9 %collective-permute-start.26 = (bf16[128,5120]{1,0:T(8,128)(2,1)S(1)}, bf16[128,5120]{1,0:T(8,128)(2,1)}, u32[]{:S(2)}, u32[]{:S(2)}) collective-permute-start(bf16[128,5120]{1,0:T(8,128)(2,1)S(1)} %collective-permute-done.14.refs_17_), channel_id=1, source_target_pairs={{0,1},{1,0},{2,3},{3,2},{4,5},{5,4},{6,7},{7,6},{8,9},{9,8},{10,11... | collective-permute-start | bytes 3932168 | tf_op jit(solution)/shard_map/ppermute | solution.py:266
  185.2 51.1 %all-to-all-start = ((bf16[8,128,512]{2,1,0:T(8,128)(2,1)}), bf16[8,128,512]{2,1,0:T(8,128)(2,1)}, u32[]{:S(2)}, u32[]{:S(2)}) async-start(bf16[8,128,512]{2,1,0:T(8,128)(2,1)} %bitcast.26), calls=%async_computation | async-start | bytes 2097152 | tf_op jit(solution)/shard_map/all_to_all | solution.py:393
  193.9 31.6 %collective-permute-start.25 = (bf16[128,5120]{1,0:T(8,128)(2,1)}, bf16[128,5120]{1,0:T(8,128)(2,1)}, u32[]{:S(2)}, u32[]{:S(2)}) collective-permute-start(bf16[128,5120]{1,0:T(8,128)(2,1)} %broadcast_select_fusion.refs_17_), channel_id=1, source_target_pairs={{0,2},{1,3},{2,0},{3,1},{4,6},{5,7},{6,4},{7,5},{8,10},{9,11},{10,... | collective-permute-start | bytes 3932168 | tf_op jit(solution)/shard_map/ppermute | solution.py:257
  195.4 39.8 %collective-permute-start.24 = (bf16[128,5120]{1,0:T(8,128)(2,1)}, bf16[128,5120]{1,0:T(8,128)(2,1)S(1)}, u32[]{:S(2)}, u32[]{:S(2)}) collective-permute-start(bf16[128,5120]{1,0:T(8,128)(2,1)} %collective-permute-done.20), channel_id=1, source_target_pairs={{8,0},{12,4},{16,24},{20,28},{9,1},{13,5},{17,25},{21,29},{10,2},{... | collective-permute-start | bytes 3932168 | tf_op jit(solution)/shard_map/ppermute | solution.py:242
  197.7 44.8 %collective-permute-start.29 = (bf16[128,5120]{1,0:T(8,128)(2,1)}, bf16[128,5120]{1,0:T(8,128)(2,1)}, u32[]{:S(2)}, u32[]{:S(2)}) collective-permute-start(bf16[128,5120]{1,0:T(8,128)(2,1)} %broadcast_select_fusion.refs_17_), channel_id=1, source_target_pairs={{0,1},{1,0},{2,3},{3,2},{4,5},{5,4},{6,7},{7,6},{8,9},{9,8},{10,11... | collective-permute-start | bytes 3932168 | tf_op jit(solution)/shard_map/ppermute | solution.py:266
  258.9 22.2 %collective-permute-start.37 = (bf16[64,5120]{1,0:T(8,128)(2,1)S(1)}, bf16[64,5120]{1,0:T(8,128)(2,1)}, u32[]{:S(2)}, u32[]{:S(2)}) collective-permute-start(bf16[64,5120]{1,0:T(8,128)(2,1)S(1)} %get-tuple-element.109.refs_17_), channel_id=1, source_target_pairs={{0,1},{1,0},{2,3},{3,2},{4,5},{5,4},{6,7},{7,6},{8,9},{9,8},{10,11... | collective-permute-start | bytes 1966088 | tf_op jit(solution)/shard_map/ppermute | solution.py:266
  275.0 33.1 %collective-permute-start.32 = (bf16[432,512]{1,0:T(8,128)(2,1)}, bf16[432,512]{1,0:T(8,128)(2,1)}, u32[]{:S(2)}, u32[]{:S(2)}) collective-permute-start(bf16[432,512]{1,0:T(8,128)(2,1)} %mlp_block.7), channel_id=1, source_target_pairs={{0,16},{4,20},{8,24},{12,28},{16,0},{20,4},{24,8},{28,12},{1,17},{... | collective-permute-start | bytes 1327112 | tf_op jit(solution)/shard_map/ppermute | solution.py:242
  277.8 31.4 %collective-permute-start.36 = (bf16[432,256]{1,0:T(8,128)(2,1)S(1)}, bf16[432,256]{1,0:T(8,128)(2,1)S(1)}, u32[]{:S(2)}, u32[]{:S(2)}) collective-permute-start(bf16[432,256]{1,0:T(8,128)(2,1)S(1)} %copy-done.38), channel_id=1, source_target_pairs={{0,24},{4,28},{8,16},{12,20},{16,8},{20,12},{24,0},{28,4},{1,25},{... | collective-permute-start | bytes 663560 | tf_op jit(solution)/shard_map/ppermute | solution.py:242
  (62 other events, 937.7 us)

commit v3 on v2

--- a/solution.py
+++ b/solution.py
@@ -389,33 +389,31 @@
 
     pieces_0 = shared(near, near_x)
     next_2e, next_2m, next_1_x, pieces_0 = lax.optimization_barrier((next_2e, next_2m, next_1_x, pieces_0))
-    kv_send = after(kv_send, next_2e, next_2m)
-    kv_in = lax.all_to_all(
-        kv_send.reshape(n_req, PAGE, 2 * kv_heads * HD), "req", split_axis=0, concat_axis=0, tiled=True
-    )
     next_3 = along_z(next_2m, outward)
     next_2 = jnp.where(at_end, next_2e, next_2m)
     next_2_x = along_x(next_2)
     hidden_0 = work(pieces_0)
+    hidden_0, kv_send = lax.optimization_barrier((hidden_0, kv_send))
+    kv_in = lax.all_to_all(
+        kv_send.reshape(n_req, PAGE, 2 * kv_heads * HD), "req", split_axis=0, concat_axis=0, tiled=True
+    )
     hidden_1 = work(shared(next_1, next_1_x))
-    next_3, next_2_x, hidden_0, hidden_1, kv_in = lax.optimization_barrier(
-        (next_3, next_2_x, hidden_0, hidden_1, kv_in)
-    )
+    next_3, next_2_x, hidden_0, hidden_1 = lax.optimization_barrier((next_3, next_2_x, hidden_0, hidden_1))
     next_3a = jnp.where(at_end, next_3[:run], middle_1[:run])
     next_3b = jnp.where(at_end, next_3[run:], middle_1[run:])
     next_3a_x = along_x(next_3a)
     hidden_2 = work(shared(next_2, next_2_x))
     back_1 = along_z(hidden_1, flip[1])
+    next_3b, next_3a_x, hidden_2, back_1, kv_in = lax.optimization_barrier(
+        (next_3b, next_3a_x, hidden_2, back_1, kv_in)
+    )
+    next_3b_x = along_x(next_3b)
+    back_2 = along_z(hidden_2, flip[2])
+    hidden_3a = work(shared(next_3a, next_3a_x))
     mine = page_table[None] == (me_req * REQS + jnp.arange(REQS, dtype=jnp.int32))[:, None, None]
     sources = jnp.sum(jnp.where(mine, jnp.arange(n_req, dtype=jnp.int32)[None, :, None], 0), axis=(1, 2))
     cache_out = write_cache(sources.astype(jnp.int32), kv_in, kv_heads)
-    next_3b, next_3a_x, hidden_2, back_1, cache_out = lax.optimization_barrier(
-        (next_3b, next_3a_x, hidden_2, back_1, cache_out)
-    )
-    next_3b_x = along_x(next_3b)
-    back_2 = along_z(hidden_2, flip[2])
-    hidden_3a = work(shared(next_3a, next_3a_x))
-    next_3b_x, hidden_3a = lax.optimization_barrier((next_3b_x, hidden_3a))
+    next_3b_x, hidden_3a, back_2, cache_out = lax.optimization_barrier((next_3b_x, hidden_3a, back_2, cache_out))
     back_3a = along_z(hidden_3a, flip[3])
     back_3b = along_z(work(shared(next_3b, next_3b_x)), flip[3])
     hidden_t = jnp.zeros((units_all, rows), jnp.bfloat16)

time: 316 us -> 300 us (0.949); the launches traced: 310 us -> 299 us
  waiting for transfers between devices: 149 us -> 143 us
  local copies, waits for them, and re-layouts: 21.3 us -> 18.1 us
    ppermute x5, waiting for transfers between devices: 7.08 us -> 2.45 us  [along_x(): lax.ppermute(value, 'mp', [(a * CORES + b, (a + step) % n_x * CORES + b)...]
where the time goes in v3:
time: 300 us; the launch traced here: 299 us
  waiting for transfers between devices  143 us (48%)
  Pallas kernels  66.8 us (22%)
  starting transfers between devices  42.2 us (14%)
  local copies, waits for them, and re-layouts  18.1 us (6%)
  other arithmetic  17 us (6%)
  matrix products  10.8 us (4%)
    ppermute x15, waiting for transfers between devices, along_z(): lax.ppermute(value, 'req', [(a * n_y + c, b * n_y + c) for a, b in moves...  107 us
    pallas_call x5, Pallas kernels, mlp_block(): pl.pallas_call(lambda *refs: mlp_kernel(count, pieces, halves, *refs), ou...  60.2 us
    ppermute x8, waiting for transfers between devices, along_y(): lax.ppermute(value, 'req', [(a * n_y + b, a * n_y + (b + step) % n_y) for...  29.3 us
    ppermute x15, starting transfers between devices, along_z(): lax.ppermute(value, 'req', [(a * n_y + c, b * n_y + c) for a, b in moves...  18.4 us
    dot_general x2, matrix products, project(): jnp.dot(picked, w_out, preferred_element_type=jnp.float32)  10.8 us
    ppermute x8, starting transfers between devices, along_y(): lax.ppermute(value, 'req', [(a * n_y + b, a * n_y + (b + step) % n_y) for...  8.6 us
    dynamic_slice x3, local copies, waits for them, and re-layouts, share(): lax.dynamic_slice(weight_t, ((z + shift) % N_Z * units, 0), (units, depth))  7.39 us
    all_to_all x1, starting transfers between devices, shards(): lax.all_to_all(kv_send.reshape(n_req, PAGE, 2 * kv_heads * HD), 'req', sp...  7.04 us
  transfers between devices with their start and end apart: 41, of which 20 were waited for; matrix products, arithmetic and copies ran while one was open for 11% of the time, Pallas kernels for 22%

profile of v3, /device:TPU:0, one launch (start us, length us, event | category | flops | bytes accessed | tf_op | source)
XLA Modules:
  0.0 299.3 jit_solution(11547164264599983974)
XLA Ops:
  16.6 4.5 %attention.1 = (bf16[512,768]{1,0:T(8,128)(2,1)S(1)}, bf16[1024,512]{1,0:T(8,128)(2,1)}) custom-call(bf16[512,768]{1,0:T(8,128)(2,1)S(1)} %copy-done, bf16[512,256]{1,0:T(8,128)(2,1)S(1)} %copy-done.1, bf16[512,256]{1,0:T(8,128)(2,1)S(1)} %copy-done.2, f32[1,768]{1,0:T(1,128)S(1)} %broadcast_in_dim.71.refs_3_, f32[1,256]{1,0:T(1,128)S(1)} %bitcast.46, ...), custom_call_target="tpu_custom_call" | custom-call | flops 100000000 | bytes 65536 | tf_op jit(solution)/shard_map/attention/pallas_call | solution.py:95
  21.1 7.1 %convolution_convert_fusion = bf16[256,5120]{1,0:T(8,128)(2,1)} fusion(bf16[768,5120]{1,0:T(8,128)(2,1)} %param.23, bf16[2,256,768]{2,1,0:T(8,128)(2,1)S(1)} %bitcast.48, s32[]{:T(128)S(6)} %select_n.201), kind=kOutput, calls=%fused_computation | convolution fusion | flops 2014576640 | bytes 10878980 | tf_op jit(solution)/shard_map/dot_general | solution.py:313
  28.2 3.8 %convolution_convert_fusion.1 = bf16[256,5120]{1,0:T(8,128)(2,1)} fusion(bf16[768,5120]{1,0:T(8,128)(2,1)S(1)} %bitcast.57, bf16[2,256,768]{2,1,0:T(8,128)(2,1)S(1)} %bitcast.49, s32[]{:T(128)S(6)} %select_n.200), kind=kOutput, calls=%fused_computation.1 | convolution fusion | flops 2014576640 | bytes 10878980 | tf_op jit(solution)/shard_map/dot_general | solution.py:313
  32.0 3.3 %collective-permute-done.refs_3_ = bf16[432,640]{1,0:T(8,128)(2,1)} collective-permute-done((bf16[432,640]{1,0:T(8,128)(2,1)}, bf16[432,640]{1,0:T(8,128)(2,1)}, u32[]{:S(2)}, u32[]{:S(2)}) %collective-permute-start) | collective-permute-done | bytes 552992 | tf_op jit(solution)/shard_map/ppermute | solution.py:242
  37.4 25.6 %collective-permute-done.2.refs_11_ = bf16[432,640]{1,0:T(8,128)(2,1)S(1)} collective-permute-done((bf16[432,640]{1,0:T(8,128)(2,1)S(1)}, bf16[432,640]{1,0:T(8,128)(2,1)S(1)}, u32[]{:S(2)}, u32[]{:S(2)}) %collective-permute-start.2) | collective-permute-done | bytes 552992 | tf_op jit(solution)/shard_map/ppermute | solution.py:242
  66.4 3.4 %convert_add_fusion = f32[256,5120]{1,0:T(8,128)S(1)} fusion(bf16[256,5120]{1,0:T(8,128)(2,1)} %collective-permute-done.5, bf16[256,5120]{1,0:T(8,128)(2,1)} %convolution_convert_fusion.1), kind=kLoop, calls=%fused_computation.2 | loop fusion | flops 3932160 | bytes 10485760 | tf_op jit(solution)/shard_map/add | solution.py:329
  73.3 5.9 %collective-permute-done.6.refs_5_ = bf16[432,640]{1,0:T(8,128)(2,1)S(1)} collective-permute-done((bf16[432,640]{1,0:T(8,128)(2,1)}, bf16[432,640]{1,0:T(8,128)(2,1)S(1)}, u32[]{:S(2)}, u32[]{:S(2)}) %collective-permute-start.6) | collective-permute-done | bytes 552992 | tf_op jit(solution)/shard_map/ppermute | solution.py:242
  85.0 8.8 %collective-permute-done.10.refs_6_ = bf16[432,640]{1,0:T(8,128)(2,1)S(1)} collective-permute-done((bf16[432,640]{1,0:T(8,128)(2,1)S(1)}, bf16[432,640]{1,0:T(8,128)(2,1)S(1)}, u32[]{:S(2)}, u32[]{:S(2)}) %collective-permute-start.10) | collective-permute-done | bytes 552992 | tf_op jit(solution)/shard_map/ppermute | solution.py:249
  93.8 3.1 %collective-permute-done.8.refs_7_ = bf16[432,640]{1,0:T(8,128)(2,1)S(1)} collective-permute-done((bf16[432,640]{1,0:T(8,128)(2,1)S(1)}, bf16[432,640]{1,0:T(8,128)(2,1)S(1)}, u32[]{:S(2)}, u32[]{:S(2)}) %collective-permute-start.8) | collective-permute-done | bytes 552992 | tf_op jit(solution)/shard_map/ppermute | solution.py:242
  96.9 9.0 %collective-permute-done.9.refs_15_ = bf16[432,640]{1,0:T(8,128)(2,1)S(1)} collective-permute-done((bf16[432,640]{1,0:T(8,128)(2,1)S(1)}, bf16[432,640]{1,0:T(8,128)(2,1)S(1)}, u32[]{:S(2)}, u32[]{:S(2)}) %collective-permute-start.9) | collective-permute-done | bytes 552992 | tf_op jit(solution)/shard_map/ppermute | solution.py:242
  105.9 3.3 %collective-permute-done.11 = bf16[128,5120]{1,0:T(8,128)(2,1)} collective-permute-done((bf16[128,5120]{1,0:T(8,128)(2,1)}, bf16[128,5120]{1,0:T(8,128)(2,1)}, u32[]{:S(2)}, u32[]{:S(2)}) %collective-permute-start.11) | collective-permute-done | bytes 1310752 | tf_op jit(solution)/shard_map/ppermute | solution.py:341
  116.2 10.7 %collective-permute-done.12.refs_13_ = bf16[432,640]{1,0:T(8,128)(2,1)S(1)} collective-permute-done((bf16[432,640]{1,0:T(8,128)(2,1)S(1)}, bf16[432,640]{1,0:T(8,128)(2,1)S(1)}, u32[]{:S(2)}, u32[]{:S(2)}) %collective-permute-start.12) | collective-permute-done | bytes 552992 | tf_op jit(solution)/shard_map/ppermute | solution.py:242
  132.3 13.4 %collective-permute-done.17.refs_16_ = bf16[432,640]{1,0:T(8,128)(2,1)S(1)} collective-permute-done((bf16[432,640]{1,0:T(8,128)(2,1)S(1)}, bf16[432,640]{1,0:T(8,128)(2,1)S(1)}, u32[]{:S(2)}, u32[]{:S(2)}) %collective-permute-start.17) | collective-permute-done | bytes 552992 | tf_op jit(solution)/shard_map/ppermute | solution.py:249
  145.8 6.9 %collective-permute-done.16.refs_14_ = bf16[432,640]{1,0:T(8,128)(2,1)S(1)} collective-permute-done((bf16[432,640]{1,0:T(8,128)(2,1)S(1)}, bf16[432,640]{1,0:T(8,128)(2,1)S(1)}, u32[]{:S(2)}, u32[]{:S(2)}) %collective-permute-start.16) | collective-permute-done | bytes 552992 | tf_op jit(solution)/shard_map/ppermute | solution.py:249
  161.2 23.3 %collective-permute-done.19 = bf16[128,5120]{1,0:T(8,128)(2,1)} collective-permute-done((bf16[128,5120]{1,0:T(8,128)(2,1)}, bf16[128,5120]{1,0:T(8,128)(2,1)}, u32[]{:S(2)}, u32[]{:S(2)}) %collective-permute-start.19) | collective-permute-done | bytes 1310752 | tf_op jit(solution)/shard_map/ppermute | solution.py:242
  191.8 13.4 %mlp_block.5 = bf16[432,512]{1,0:T(8,128)(2,1)} custom-call(s32[12]{0:T(128)} %stack.38.refs_0_, bf16[432,640]{1,0:T(8,128)(2,1)} %copy-done.8, bf16[432,640]{1,0:T(8,128)(2,1)} %collective-permute-done.1.refs_2_, bf16[432,640]{1,0:T(8,128)(2,1)} %collective-permute-done.refs_3_, bf16[432,640]{1,0:T(8,128)(2,1)} %copy-done.12, bf16[432,640]{1,0:T(8,128)(2,1)} %copy-done.13, ...), custom_call_target="tpu_custom_call" | custom-call | flops 100000000 | bytes 65536 | tf_op jit(solution)/shard_map/mlp_block/pallas_call | solution.py:205
  205.2 7.0 %all-to-all-start = ((bf16[8,128,512]{2,1,0:T(8,128)(2,1)}), bf16[8,128,512]{2,1,0:T(8,128)(2,1)S(1)}, u32[]{:S(2)}, u32[]{:S(2)}) async-start(bf16[8,128,512]{2,1,0:T(8,128)(2,1)} %bitcast.26), calls=%async_computation | async-start | bytes 2097152 | tf_op jit(solution)/shard_map/all_to_all | solution.py:397
  212.3 13.4 %mlp_block.6 = bf16[432,512]{1,0:T(8,128)(2,1)} custom-call(s32[12]{0:T(128)} %stack.38.refs_0_, bf16[432,640]{1,0:T(8,128)(2,1)} %copy-done.8, bf16[432,640]{1,0:T(8,128)(2,1)} %collective-permute-done.1.refs_2_, bf16[432,640]{1,0:T(8,128)(2,1)} %collective-permute-done.refs_3_, bf16[432,640]{1,0:T(8,128)(2,1)} %copy-done.12, bf16[432,640]{1,0:T(8,128)(2,1)} %copy-done.13, ...), custom_call_target="tpu_custom_call" | custom-call | flops 100000000 | bytes 65536 | tf_op jit(solution)/shard_map/mlp_block/pallas_call | solution.py:205
  225.8 5.6 %collective-permute-done.24 = bf16[128,5120]{1,0:T(8,128)(2,1)} collective-permute-done((bf16[128,5120]{1,0:T(8,128)(2,1)}, bf16[128,5120]{1,0:T(8,128)(2,1)}, u32[]{:S(2)}, u32[]{:S(2)}) %collective-permute-start.24) | collective-permute-done | bytes 1310752 | tf_op jit(solution)/shard_map/ppermute | solution.py:242
  234.8 13.4 %mlp_block.7 = bf16[432,512]{1,0:T(8,128)(2,1)} custom-call(s32[12]{0:T(128)} %stack.38.refs_0_, bf16[432,640]{1,0:T(8,128)(2,1)} %copy-done.8, bf16[432,640]{1,0:T(8,128)(2,1)} %collective-permute-done.1.refs_2_, bf16[432,640]{1,0:T(8,128)(2,1)} %collective-permute-done.refs_3_, bf16[432,640]{1,0:T(8,128)(2,1)} %copy-done.12, bf16[432,640]{1,0:T(8,128)(2,1)} %copy-done.13, ...), custom_call_target="tpu_custom_call" | custom-call | flops 100000000 | bytes 65536 | tf_op jit(solution)/shard_map/mlp_block/pallas_call | solution.py:205
  255.1 10.0 %mlp_block.8 = bf16[432,256]{1,0:T(8,128)(2,1)} custom-call(s32[12]{0:T(128)} %stack.38.refs_0_, bf16[432,640]{1,0:T(8,128)(2,1)} %copy-done.8, bf16[432,640]{1,0:T(8,128)(2,1)} %collective-permute-done.1.refs_2_, bf16[432,640]{1,0:T(8,128)(2,1)} %collective-permute-done.refs_3_, bf16[432,640]{1,0:T(8,128)(2,1)} %copy-done.12, bf16[432,640]{1,0:T(8,128)(2,1)} %copy-done.13, ...), custom_call_target="tpu_custom_call" | custom-call | flops 100000000 | bytes 65536 | tf_op jit(solution)/shard_map/mlp_block/pallas_call | solution.py:205
  265.1 9.3 %collective-permute-done.35 = bf16[432,512]{1,0:T(8,128)(2,1)S(1)} collective-permute-done((bf16[432,512]{1,0:T(8,128)(2,1)}, bf16[432,512]{1,0:T(8,128)(2,1)S(1)}, u32[]{:S(2)}, u32[]{:S(2)}) %collective-permute-start.35) | collective-permute-done | bytes 442400 | tf_op jit(solution)/shard_map/ppermute | solution.py:242
  278.8 10.0 %mlp_block.9 = bf16[432,256]{1,0:T(8,128)(2,1)} custom-call(s32[12]{0:T(128)} %stack.38.refs_0_, bf16[432,640]{1,0:T(8,128)(2,1)} %copy-done.8, bf16[432,640]{1,0:T(8,128)(2,1)} %collective-permute-done.1.refs_2_, bf16[432,640]{1,0:T(8,128)(2,1)} %collective-permute-done.refs_3_, bf16[432,640]{1,0:T(8,128)(2,1)} %copy-done.12, bf16[432,640]{1,0:T(8,128)(2,1)} %copy-done.13, ...), custom_call_target="tpu_custom_call" | custom-call | flops 100000000 | bytes 65536 | tf_op jit(solution)/shard_map/mlp_block/pallas_call | solution.py:205
  291.1 7.0 %collective-permute-done.39 = bf16[432,256]{1,0:T(8,128)(2,1)S(1)} collective-permute-done((bf16[432,256]{1,0:T(8,128)(2,1)}, bf16[432,256]{1,0:T(8,128)(2,1)S(1)}, u32[]{:S(2)}, u32[]{:S(2)}) %collective-permute-start.39) | collective-permute-done | bytes 221216 | tf_op jit(solution)/shard_map/ppermute | solution.py:242
  (190 shorter events, 76.6 us)
Async XLA Ops:
  5.2 26.8 %collective-permute-start.1 = (bf16[432,640]{1,0:T(8,128)(2,1)S(1)}, bf16[432,640]{1,0:T(8,128)(2,1)}, u32[]{:S(2)}, u32[]{:S(2)}) collective-permute-start(bf16[432,640]{1,0:T(8,128)(2,1)S(1)} %get-tuple-element.124.refs_1_), channel_id=1, source_target_pairs={{0,4},{4,0},{8,12},{12,8},{16,20},{20,16},{24,28},{28,24},{1,5},{5... | collective-permute-start | bytes 1658888 | tf_op jit(solution)/shard_map/ppermute | solution.py:249
  8.2 27.1 %collective-permute-start = (bf16[432,640]{1,0:T(8,128)(2,1)}, bf16[432,640]{1,0:T(8,128)(2,1)}, u32[]{:S(2)}, u32[]{:S(2)}) collective-permute-start(bf16[432,640]{1,0:T(8,128)(2,1)} %dynamic-slice_bitcast_fusion), channel_id=1, source_target_pairs={{0,16},{4,20},{8,24},{12,28},{16,0},{20,4},{24,8},{28,12},{1,17},{... | collective-permute-start | bytes 1658888 | tf_op jit(solution)/shard_map/ppermute | solution.py:242
  35.3 27.7 %collective-permute-start.5 = (bf16[256,5120]{1,0:T(8,128)(2,1)}, bf16[256,5120]{1,0:T(8,128)(2,1)}, u32[]{:S(2)}, u32[]{:S(2)}) collective-permute-start(bf16[256,5120]{1,0:T(8,128)(2,1)} %convolution_convert_fusion), channel_id=1, source_target_pairs={{0,1},{1,0},{2,3},{3,2},{4,5},{5,4},{6,7},{7,6},{8,9},{9,8},{10,11... | collective-permute-start | bytes 7864328 | tf_op jit(solution)/shard_map/ppermute | solution.py:266
  35.3 27.7 %collective-permute-start.2 = (bf16[432,640]{1,0:T(8,128)(2,1)S(1)}, bf16[432,640]{1,0:T(8,128)(2,1)S(1)}, u32[]{:S(2)}, u32[]{:S(2)}) collective-permute-start(bf16[432,640]{1,0:T(8,128)(2,1)S(1)} %copy-done.33), channel_id=1, source_target_pairs={{0,16},{4,20},{8,24},{12,28},{16,0},{20,4},{24,8},{28,12},{1,17},{... | collective-permute-start | bytes 1658888 | tf_op jit(solution)/shard_map/ppermute | solution.py:242
  35.3 27.7 %collective-permute-start.3 = (bf16[432,640]{1,0:T(8,128)(2,1)S(1)}, bf16[432,640]{1,0:T(8,128)(2,1)S(1)}, u32[]{:S(2)}, u32[]{:S(2)}) collective-permute-start(bf16[432,640]{1,0:T(8,128)(2,1)S(1)} %get-tuple-element.68.refs_9_), channel_id=1, source_target_pairs={{0,4},{4,0},{8,12},{12,8},{16,20},{20,16},{24,28},{28,24},{1,5},{5... | collective-permute-start | bytes 1658888 | tf_op jit(solution)/shard_map/ppermute | solution.py:249
  35.8 27.2 %collective-permute-start.4 = (bf16[432,640]{1,0:T(8,128)(2,1)}, bf16[432,640]{1,0:T(8,128)(2,1)S(1)}, u32[]{:S(2)}, u32[]{:S(2)}) collective-permute-start(bf16[432,640]{1,0:T(8,128)(2,1)} %collective-permute-done.refs_3_), channel_id=1, source_target_pairs={{0,4},{4,0},{8,12},{12,8},{16,20},{20,16},{24,28},{28,24},{1,5},{5... | collective-permute-start | bytes 1658888 | tf_op jit(solution)/shard_map/ppermute | solution.py:249
  79.4 29.7 %collective-permute-start.11 = (bf16[128,5120]{1,0:T(8,128)(2,1)}, bf16[128,5120]{1,0:T(8,128)(2,1)}, u32[]{:S(2)}, u32[]{:S(2)}) collective-permute-start(bf16[128,5120]{1,0:T(8,128)(2,1)} %fusion.1), channel_id=1, source_target_pairs={{0,2},{1,3},{2,0},{3,1},{4,6},{5,7},{6,4},{7,5},{8,10},{9,11},{10,... | collective-permute-start | bytes 3932168 | tf_op jit(solution)/shard_map/ppermute | solution.py:341
  82.8 23.1 %collective-permute-start.9 = (bf16[432,640]{1,0:T(8,128)(2,1)S(1)}, bf16[432,640]{1,0:T(8,128)(2,1)S(1)}, u32[]{:S(2)}, u32[]{:S(2)}) collective-permute-start(bf16[432,640]{1,0:T(8,128)(2,1)S(1)} %copy-done.32), channel_id=1, source_target_pairs={{0,24},{4,28},{8,0},{12,4},{16,8},{20,12},{24,16},{28,20},{1,25},{... | collective-permute-start | bytes 1658888 | tf_op jit(solution)/shard_map/ppermute | solution.py:242
  127.0 27.7 %collective-permute-start.14 = (bf16[128,5120]{1,0:T(8,128)(2,1)}, bf16[128,5120]{1,0:T(8,128)(2,1)S(1)}, u32[]{:S(2)}, u32[]{:S(2)}) collective-permute-start(bf16[128,5120]{1,0:T(8,128)(2,1)} %multiply_convert_fusion.refs_17_), channel_id=1, source_target_pairs={{0,8},{4,12},{8,0},{12,4},{16,24},{20,28},{24,16},{28,20},{1,9},{5... | collective-permute-start | bytes 3932168 | tf_op jit(solution)/shard_map/ppermute | solution.py:242
  127.1 27.6 %collective-permute-start.15 = (bf16[128,5120]{1,0:T(8,128)(2,1)}, bf16[128,5120]{1,0:T(8,128)(2,1)}, u32[]{:S(2)}, u32[]{:S(2)}) collective-permute-start(bf16[128,5120]{1,0:T(8,128)(2,1)} %multiply_convert_fusion.refs_17_), channel_id=1, source_target_pairs={{8,16},{12,20},{16,8},{20,12},{9,17},{13,21},{17,9},{21,13},{10,18... | collective-permute-start | bytes 3932168 | tf_op jit(solution)/shard_map/ppermute | solution.py:242
  128.8 27.4 %collective-permute-start.18 = (bf16[128,5120]{1,0:T(8,128)(2,1)}, bf16[128,5120]{1,0:T(8,128)(2,1)}, u32[]{:S(2)}, u32[]{:S(2)}) collective-permute-start(bf16[128,5120]{1,0:T(8,128)(2,1)} %multiply_convert_fusion.refs_17_), channel_id=1, source_target_pairs={{0,2},{1,3},{2,0},{3,1},{4,6},{5,7},{6,4},{7,5},{8,10},{9,11},{10,... | collective-permute-start | bytes 3932168 | tf_op jit(solution)/shard_map/ppermute | solution.py:257
  156.2 28.3 %collective-permute-start.19 = (bf16[128,5120]{1,0:T(8,128)(2,1)}, bf16[128,5120]{1,0:T(8,128)(2,1)}, u32[]{:S(2)}, u32[]{:S(2)}) collective-permute-start(bf16[128,5120]{1,0:T(8,128)(2,1)} %collective-permute-done.15), channel_id=1, source_target_pairs={{8,0},{12,4},{16,24},{20,28},{9,1},{13,5},{17,25},{21,29},{10,2},{... | collective-permute-start | bytes 3932168 | tf_op jit(solution)/shard_map/ppermute | solution.py:242
  157.5 27.0 %collective-permute-start.20 = (bf16[128,5120]{1,0:T(8,128)(2,1)S(1)}, bf16[128,5120]{1,0:T(8,128)(2,1)}, u32[]{:S(2)}, u32[]{:S(2)}) collective-permute-start(bf16[128,5120]{1,0:T(8,128)(2,1)S(1)} %collective-permute-done.14.refs_17_), channel_id=1, source_target_pairs={{8,16},{12,20},{16,8},{20,12},{9,17},{13,21},{17,9},{21,13},{10,18... | collective-permute-start | bytes 3932168 | tf_op jit(solution)/shard_map/ppermute | solution.py:242
  159.2 26.2 %collective-permute-start.21 = (bf16[128,5120]{1,0:T(8,128)(2,1)S(1)}, bf16[128,5120]{1,0:T(8,128)(2,1)}, u32[]{:S(2)}, u32[]{:S(2)}) collective-permute-start(bf16[128,5120]{1,0:T(8,128)(2,1)S(1)} %collective-permute-done.14.refs_17_), channel_id=1, source_target_pairs={{0,2},{1,3},{2,0},{3,1},{4,6},{5,7},{6,4},{7,5},{8,10},{9,11},{10,... | collective-permute-start | bytes 3932168 | tf_op jit(solution)/shard_map/ppermute | solution.py:257
  160.7 24.7 %collective-permute-start.23 = (bf16[128,5120]{1,0:T(8,128)(2,1)}, bf16[128,5120]{1,0:T(8,128)(2,1)}, u32[]{:S(2)}, u32[]{:S(2)}) collective-permute-start(bf16[128,5120]{1,0:T(8,128)(2,1)} %collective-permute-done.18.refs_18_), channel_id=1, source_target_pairs={{0,1},{1,0},{2,3},{3,2},{4,5},{5,4},{6,7},{7,6},{8,9},{9,8},{10,11... | collective-permute-start | bytes 3932168 | tf_op jit(solution)/shard_map/ppermute | solution.py:266
  160.7 51.6 %collective-permute-start.26 = (bf16[128,5120]{1,0:T(8,128)(2,1)S(1)}, bf16[128,5120]{1,0:T(8,128)(2,1)}, u32[]{:S(2)}, u32[]{:S(2)}) collective-permute-start(bf16[128,5120]{1,0:T(8,128)(2,1)S(1)} %collective-permute-done.14.refs_17_), channel_id=1, source_target_pairs={{0,1},{1,0},{2,3},{3,2},{4,5},{5,4},{6,7},{7,6},{8,9},{9,8},{10,11... | collective-permute-start | bytes 3932168 | tf_op jit(solution)/shard_map/ppermute | solution.py:266
  185.4 26.8 %collective-permute-start.27 = (bf16[128,5120]{1,0:T(8,128)(2,1)}, bf16[128,5120]{1,0:T(8,128)(2,1)}, u32[]{:S(2)}, u32[]{:S(2)}) collective-permute-start(bf16[128,5120]{1,0:T(8,128)(2,1)} %collective-permute-done.21.refs_18_), channel_id=1, source_target_pairs={{0,1},{1,0},{2,3},{3,2},{4,5},{5,4},{6,7},{7,6},{8,9},{9,8},{10,11... | collective-permute-start | bytes 3932168 | tf_op jit(solution)/shard_map/ppermute | solution.py:266
  188.0 37.8 %collective-permute-start.25 = (bf16[128,5120]{1,0:T(8,128)(2,1)}, bf16[128,5120]{1,0:T(8,128)(2,1)}, u32[]{:S(2)}, u32[]{:S(2)}) collective-permute-start(bf16[128,5120]{1,0:T(8,128)(2,1)} %broadcast_select_fusion.refs_17_), channel_id=1, source_target_pairs={{0,2},{1,3},{2,0},{3,1},{4,6},{5,7},{6,4},{7,5},{8,10},{9,11},{10,... | collective-permute-start | bytes 3932168 | tf_op jit(solution)/shard_map/ppermute | solution.py:257
  189.5 41.9 %collective-permute-start.24 = (bf16[128,5120]{1,0:T(8,128)(2,1)}, bf16[128,5120]{1,0:T(8,128)(2,1)}, u32[]{:S(2)}, u32[]{:S(2)}) collective-permute-start(bf16[128,5120]{1,0:T(8,128)(2,1)} %collective-permute-done.20), channel_id=1, source_target_pairs={{8,0},{12,4},{16,24},{20,28},{9,1},{13,5},{17,25},{21,29},{10,2},{... | collective-permute-start | bytes 3932168 | tf_op jit(solution)/shard_map/ppermute | solution.py:242
  191.6 42.5 %collective-permute-start.29 = (bf16[128,5120]{1,0:T(8,128)(2,1)}, bf16[128,5120]{1,0:T(8,128)(2,1)}, u32[]{:S(2)}, u32[]{:S(2)}) collective-permute-start(bf16[128,5120]{1,0:T(8,128)(2,1)} %broadcast_select_fusion.refs_17_), channel_id=1, source_target_pairs={{0,1},{1,0},{2,3},{3,2},{4,5},{5,4},{6,7},{7,6},{8,9},{9,8},{10,11... | collective-permute-start | bytes 3932168 | tf_op jit(solution)/shard_map/ppermute | solution.py:266
  205.2 45.4 %all-to-all-start = ((bf16[8,128,512]{2,1,0:T(8,128)(2,1)}), bf16[8,128,512]{2,1,0:T(8,128)(2,1)S(1)}, u32[]{:S(2)}, u32[]{:S(2)}) async-start(bf16[8,128,512]{2,1,0:T(8,128)(2,1)} %bitcast.26), calls=%async_computation | async-start | bytes 2097152 | tf_op jit(solution)/shard_map/all_to_all | solution.py:397
  251.4 22.9 %collective-permute-start.32 = (bf16[64,5120]{1,0:T(8,128)(2,1)S(1)}, bf16[64,5120]{1,0:T(8,128)(2,1)S(1)}, u32[]{:S(2)}, u32[]{:S(2)}) collective-permute-start(bf16[64,5120]{1,0:T(8,128)(2,1)S(1)} %get-tuple-element.110.refs_17_), channel_id=1, source_target_pairs={{0,2},{1,3},{2,0},{3,1},{4,6},{5,7},{6,4},{7,5},{8,10},{9,11},{10,... | collective-permute-start | bytes 1966088 | tf_op jit(solution)/shard_map/ppermute | solution.py:257
  251.9 22.4 %collective-permute-start.35 = (bf16[432,512]{1,0:T(8,128)(2,1)}, bf16[432,512]{1,0:T(8,128)(2,1)S(1)}, u32[]{:S(2)}, u32[]{:S(2)}) collective-permute-start(bf16[432,512]{1,0:T(8,128)(2,1)} %mlp_block.7), channel_id=1, source_target_pairs={{0,16},{4,20},{8,24},{12,28},{16,0},{20,4},{24,8},{28,12},{1,17},{... | collective-permute-start | bytes 1327112 | tf_op jit(solution)/shard_map/ppermute | solution.py:242
  253.0 25.8 %collective-permute-start.37 = (bf16[64,5120]{1,0:T(8,128)(2,1)S(1)}, bf16[64,5120]{1,0:T(8,128)(2,1)}, u32[]{:S(2)}, u32[]{:S(2)}) collective-permute-start(bf16[64,5120]{1,0:T(8,128)(2,1)S(1)} %get-tuple-element.110.refs_17_), channel_id=1, source_target_pairs={{0,1},{1,0},{2,3},{3,2},{4,5},{5,4},{6,7},{7,6},{8,9},{9,8},{10,11... | collective-permute-start | bytes 1966088 | tf_op jit(solution)/shard_map/ppermute | solution.py:266
  (62 other events, 928.9 us)

commit v4 on v3

--- a/solution.py
+++ b/solution.py
@@ -280,9 +280,7 @@
     gate_t, up_t = w_gate.T, w_up.T
     gate_2 = share(gate_t, 2)
     gate_t, up_t, gate_2, q_pre, segment_ids = lax.optimization_barrier((gate_t, up_t, gate_2, q_pre, segment_ids))
-    gate_0, up_0 = share(gate_t, 0), share(up_t, 0)
     gate_2 = turn_z(gate_2, 2)
-    gate_0_y = along_y(gate_0)
 
     rows = q_pre.shape[0]
     kv_heads = k_pre.shape[1] // HD
@@ -313,29 +311,29 @@
         return jnp.dot(picked, w_out, preferred_element_type=jnp.float32).astype(jnp.bfloat16)
 
     kept, given = project(core), project(1 - core)
-    up_2, up_0, gate_2, gate_0_y, kept, given = lax.optimization_barrier(
-        (share(up_t, 2), up_0, gate_2, gate_0_y, kept, given)
+    up_2, gate_0, up_0, gate_2, kept, given = lax.optimization_barrier(
+        (share(up_t, 2), share(gate_t, 0), share(up_t, 0), gate_2, kept, given)
     )
     up_2 = turn_z(up_2, 2)
-    up_0_y = along_y(up_0)
-    gate_2_y = along_y(gate_2)
+    gate_0_y, up_0_y = along_y(gate_0), along_y(up_0)
     sibling = across_cores(given)
     width = sibling.shape[1]
-    gate_1, up_2, up_0_y, gate_2_y, sibling = lax.optimization_barrier(
-        (share(gate_t, 1), up_2, up_0_y, gate_2_y, sibling)
+    gate_1, up_2, gate_0_y, up_0_y, gate_2, sibling = lax.optimization_barrier(
+        (share(gate_t, 1), up_2, gate_0_y, up_0_y, gate_2, sibling)
     )
     gate_1 = turn_z(gate_1, 1)
-    up_2_y = along_y(up_2)
+    gate_2_y = along_y(gate_2)
     pair = (kept.astype(jnp.float32) + sibling.astype(jnp.float32)).reshape(n_x, 2 * run, width)
     summed = lax.dynamic_index_in_dim(pair, x, 0, keepdims=False)
     outgoing = [
         lax.dynamic_index_in_dim(pair, (x + step) % n_x, 0, keepdims=False).astype(jnp.bfloat16)
         for step in range(1, n_x)
     ]
-    gate_3, up_3, gate_1, up_2_y, outgoing = lax.optimization_barrier(
-        (share(gate_t, 3), share(up_t, 3), gate_1, up_2_y, outgoing)
+    gate_3, up_3, gate_1, up_2, gate_2_y, outgoing = lax.optimization_barrier(
+        (share(gate_t, 3), share(up_t, 3), gate_1, up_2, gate_2_y, outgoing)
     )
     gate_3, up_3 = turn_z(gate_3, 3), turn_z(up_3, 3)
+    up_2_y = along_y(up_2)
     gate_1_y = along_y(gate_1)
     incoming = [
         lax.ppermute(
@@ -345,8 +343,8 @@
         )
         for step in range(1, n_x)
     ]
-    up_1, gate_3, up_3, gate_1_y, incoming = lax.optimization_barrier(
-        (share(up_t, 1), gate_3, up_3, gate_1_y, incoming)
+    up_1, gate_3, up_3, gate_1_y, up_2_y, incoming = lax.optimization_barrier(
+        (share(up_t, 1), gate_3, up_3, gate_1_y, up_2_y, incoming)
     )
     up_1 = turn_z(up_1, 1)
     gate_3_y = along_y(gate_3)
@@ -408,19 +406,23 @@
         (next_3b, next_3a_x, hidden_2, back_1, kv_in)
     )
     next_3b_x = along_x(next_3b)
-    back_2 = along_z(hidden_2, flip[2])
+    back_2 = [along_z(hidden_2[:, :rows // 2], flip[2]), along_z(hidden_2[:, rows // 2:], flip[2])]
     hidden_3a = work(shared(next_3a, next_3a_x))
     mine = page_table[None] == (me_req * REQS + jnp.arange(REQS, dtype=jnp.int32))[:, None, None]
     sources = jnp.sum(jnp.where(mine, jnp.arange(n_req, dtype=jnp.int32)[None, :, None], 0), axis=(1, 2))
     cache_out = write_cache(sources.astype(jnp.int32), kv_in, kv_heads)
-    next_3b_x, hidden_3a, back_2, cache_out = lax.optimization_barrier((next_3b_x, hidden_3a, back_2, cache_out))
+    next_3b_x, hidden_3a, back_2[0], cache_out = lax.optimization_barrier(
+        (next_3b_x, hidden_3a, back_2[0], cache_out)
+    )
     back_3a = along_z(hidden_3a, flip[3])
-    back_3b = along_z(work(shared(next_3b, next_3b_x)), flip[3])
+    hidden_3b, back_2[1] = lax.optimization_barrier((work(shared(next_3b, next_3b_x)), back_2[1]))
+    back_3b = along_z(hidden_3b, flip[3])
     hidden_t = jnp.zeros((units_all, rows), jnp.bfloat16)
     for by, at, done in (
         (0, 0, hidden_0),
         (1, 0, back_1),
-        (2, 0, back_2),
+        (2, 0, back_2[0]),
+        (2, rows // 2, back_2[1]),
         (3, 0, back_3a),
         (3, rows // 2, back_3b),
     ):

time: 300 us -> 299 us (level); the launches traced: 299 us -> 294 us
  waiting for transfers between devices: 143 us -> 135 us
  starting transfers between devices: 42.2 us -> 46.5 us
    ppermute x15 -> x16, waiting for transfers between devices: 107 us -> 97.6 us  [along_z(): lax.ppermute(value, 'req', [(a * n_y + c, b * n_y + c) for a, b in moves...]
    dynamic_slice x3 -> x2, local copies, waits for them, and re-layouts: 7.39 us -> 3.62 us  [share(): lax.dynamic_slice(weight_t, ((z + shift) % N_Z * units, 0), (units, depth))]
    ppermute x15 -> x16, starting transfers between devices: 18.4 us -> 20.9 us  [along_z(): lax.ppermute(value, 'req', [(a * n_y + c, b * n_y + c) for a, b in moves...]
  transfers between devices with their start and end apart: 41 -> 42, of which waited for: 20 -> 21; matrix products, arithmetic and copies ran while one was open for 11% -> 12% of each run, Pallas kernels for 22% -> 23%
where the time goes in v4:
time: 299 us; the launch traced here: 294 us
  waiting for transfers between devices  135 us (45%)
  Pallas kernels  66.6 us (22%)
  starting transfers between devices  46.5 us (16%)
  other arithmetic  18 us (6%)
  local copies, waits for them, and re-layouts  15.3 us (5%)
  matrix products  10.8 us (4%)
    ppermute x16, waiting for transfers between devices, along_z(): lax.ppermute(value, 'req', [(a * n_y + c, b * n_y + c) for a, b in moves...  97.6 us
    pallas_call x5, Pallas kernels, mlp_block(): pl.pallas_call(lambda *refs: mlp_kernel(count, pieces, halves, *refs), ou...  60.1 us
    ppermute x8, waiting for transfers between devices, along_y(): lax.ppermute(value, 'req', [(a * n_y + b, a * n_y + (b + step) % n_y) for...  30.7 us
    ppermute x16, starting transfers between devices, along_z(): lax.ppermute(value, 'req', [(a * n_y + c, b * n_y + c) for a, b in moves...  20.9 us
    dot_general x2, matrix products, project(): jnp.dot(picked, w_out, preferred_element_type=jnp.float32)  10.8 us
    ppermute x8, starting transfers between devices, along_y(): lax.ppermute(value, 'req', [(a * n_y + b, a * n_y + (b + step) % n_y) for...  9.18 us
    all_to_all x1, starting transfers between devices, shards(): lax.all_to_all(kv_send.reshape(n_req, PAGE, 2 * kv_heads * HD), 'req', sp...  8.07 us
  transfers between devices with their start and end apart: 42, of which 21 were waited for; matrix products, arithmetic and copies ran while one was open for 12% of the time, Pallas kernels for 23%

profile of v4, /device:TPU:0, one launch (start us, length us, event | category | flops | bytes accessed | tf_op | source)
XLA Modules:
  0.0 293.5 jit_solution(4524522570431432881)
XLA Ops:
  2.7 4.0 %collective-permute-start = (bf16[432,640]{1,0:T(8,128)(2,1)}, bf16[432,640]{1,0:T(8,128)(2,1)S(1)}, u32[]{:S(2)}, u32[]{:S(2)}) collective-permute-start(bf16[432,640]{1,0:T(8,128)(2,1)} %dynamic-slice_bitcast_fusion), channel_id=1, source_target_pairs={{0,16},{4,20},{8,24},{12,28},{16,0},{20,4},{24,8},{28,12},{1,17},{... | collective-permute-start | bytes 1658888 | tf_op jit(solution)/shard_map/ppermute | solution.py:242
  11.5 4.5 %attention.1 = (bf16[512,768]{1,0:T(8,128)(2,1)S(1)}, bf16[1024,512]{1,0:T(8,128)(2,1)}) custom-call(bf16[512,768]{1,0:T(8,128)(2,1)S(1)} %copy-done, bf16[512,256]{1,0:T(8,128)(2,1)S(1)} %copy-done.1, bf16[512,256]{1,0:T(8,128)(2,1)S(1)} %copy-done.2, f32[1,768]{1,0:T(1,128)S(1)} %broadcast_in_dim.71.refs_3_, f32[1,256]{1,0:T(1,128)S(1)} %bitcast.46, ...), custom_call_target="tpu_custom_call" | custom-call | flops 100000000 | bytes 65536 | tf_op jit(solution)/shard_map/attention/pallas_call | solution.py:95
  16.1 7.1 %convolution_convert_fusion = bf16[256,5120]{1,0:T(8,128)(2,1)} fusion(bf16[768,5120]{1,0:T(8,128)(2,1)} %param.23, bf16[2,256,768]{2,1,0:T(8,128)(2,1)S(1)} %bitcast.48, s32[]{:T(128)S(6)} %select_n.202), kind=kOutput, calls=%fused_computation | convolution fusion | flops 2014576640 | bytes 10878980 | tf_op jit(solution)/shard_map/dot_general | solution.py:311
  24.8 3.7 %convolution_convert_fusion.1 = bf16[256,5120]{1,0:T(8,128)(2,1)} fusion(bf16[768,5120]{1,0:T(8,128)(2,1)S(1)} %bitcast.57, bf16[2,256,768]{2,1,0:T(8,128)(2,1)S(1)} %bitcast.49, s32[]{:T(128)S(6)} %select_n.201), kind=kOutput, calls=%fused_computation.1 | convolution fusion | flops 2014576640 | bytes 10878980 | tf_op jit(solution)/shard_map/dot_general | solution.py:311
  33.5 25.8 %collective-permute-done.1.refs_11_ = bf16[432,640]{1,0:T(8,128)(2,1)S(1)} collective-permute-done((bf16[432,640]{1,0:T(8,128)(2,1)}, bf16[432,640]{1,0:T(8,128)(2,1)S(1)}, u32[]{:S(2)}, u32[]{:S(2)}) %collective-permute-start.1) | collective-permute-done | bytes 552992 | tf_op jit(solution)/shard_map/ppermute | solution.py:242
  63.6 3.4 %convert_add_fusion = f32[256,5120]{1,0:T(8,128)S(1)} fusion(bf16[256,5120]{1,0:T(8,128)(2,1)} %collective-permute-done.4, bf16[256,5120]{1,0:T(8,128)(2,1)} %convolution_convert_fusion.1), kind=kLoop, calls=%fused_computation.2 | loop fusion | flops 3932160 | bytes 10485760 | tf_op jit(solution)/shard_map/add | solution.py:326
  70.6 4.9 %collective-permute-done.5.refs_5_ = bf16[432,640]{1,0:T(8,128)(2,1)S(1)} collective-permute-done((bf16[432,640]{1,0:T(8,128)(2,1)}, bf16[432,640]{1,0:T(8,128)(2,1)S(1)}, u32[]{:S(2)}, u32[]{:S(2)}) %collective-permute-start.5) | collective-permute-done | bytes 552992 | tf_op jit(solution)/shard_map/ppermute | solution.py:242
  82.6 10.0 %collective-permute-done.10.refs_12_ = bf16[432,640]{1,0:T(8,128)(2,1)S(1)} collective-permute-done((bf16[432,640]{1,0:T(8,128)(2,1)S(1)}, bf16[432,640]{1,0:T(8,128)(2,1)S(1)}, u32[]{:S(2)}, u32[]{:S(2)}) %collective-permute-start.10) | collective-permute-done | bytes 552992 | tf_op jit(solution)/shard_map/ppermute | solution.py:249
  94.4 9.1 %collective-permute-done.8.refs_15_ = bf16[432,640]{1,0:T(8,128)(2,1)S(1)} collective-permute-done((bf16[432,640]{1,0:T(8,128)(2,1)S(1)}, bf16[432,640]{1,0:T(8,128)(2,1)S(1)}, u32[]{:S(2)}, u32[]{:S(2)}) %collective-permute-start.8) | collective-permute-done | bytes 552992 | tf_op jit(solution)/shard_map/ppermute | solution.py:242
  105.5 2.9 multiply_reduce_fusion
  110.2 3.0 %multiply_convert_fusion.refs_17_ = bf16[128,5120]{1,0:T(8,128)(2,1)} fusion(f32[5120]{0:T(1024)S(1)} %copy-done.38, f32[128]{0:T(128)S(1)} %add_rsqrt_fusion, bf16[128,5120]{1,0:T(8,128)(2,1)} %collective-permute-done.11, f32[2,128,5120]{2,1,0:T(8,128)S(1)} %bitcast.52, s32[]{:T(128)S(6)} %select_n.206, bf16[64,5120]{1,0:T(8,128)(2,1)S(1)} %get-tuple-element.131, ...), kind=kLoop, calls=%fused_computation.5 | loop fusion | flops 6553600 | bytes 6574596 | tf_op jit(solution)/shard_map/convert_element_type | solution.py:361
  113.2 9.8 %collective-permute-done.12.refs_13_ = bf16[432,640]{1,0:T(8,128)(2,1)S(1)} collective-permute-done((bf16[432,640]{1,0:T(8,128)(2,1)S(1)}, bf16[432,640]{1,0:T(8,128)(2,1)S(1)}, u32[]{:S(2)}, u32[]{:S(2)}) %collective-permute-start.12) | collective-permute-done | bytes 552992 | tf_op jit(solution)/shard_map/ppermute | solution.py:242
  128.4 13.4 %collective-permute-done.17.refs_16_ = bf16[432,640]{1,0:T(8,128)(2,1)S(1)} collective-permute-done((bf16[432,640]{1,0:T(8,128)(2,1)S(1)}, bf16[432,640]{1,0:T(8,128)(2,1)S(1)}, u32[]{:S(2)}, u32[]{:S(2)}) %collective-permute-start.17) | collective-permute-done | bytes 552992 | tf_op jit(solution)/shard_map/ppermute | solution.py:249
  141.9 7.1 %collective-permute-done.16.refs_14_ = bf16[432,640]{1,0:T(8,128)(2,1)S(1)} collective-permute-done((bf16[432,640]{1,0:T(8,128)(2,1)S(1)}, bf16[432,640]{1,0:T(8,128)(2,1)S(1)}, u32[]{:S(2)}, u32[]{:S(2)}) %collective-permute-start.16) | collective-permute-done | bytes 552992 | tf_op jit(solution)/shard_map/ppermute | solution.py:249
  157.4 23.3 %collective-permute-done.19 = bf16[128,5120]{1,0:T(8,128)(2,1)} collective-permute-done((bf16[128,5120]{1,0:T(8,128)(2,1)}, bf16[128,5120]{1,0:T(8,128)(2,1)}, u32[]{:S(2)}, u32[]{:S(2)}) %collective-permute-start.19) | collective-permute-done | bytes 1310752 | tf_op jit(solution)/shard_map/ppermute | solution.py:242
  187.5 13.5 %mlp_block.5 = bf16[432,512]{1,0:T(8,128)(2,1)} custom-call(s32[12]{0:T(128)} %stack.38.refs_0_, bf16[432,640]{1,0:T(8,128)(2,1)} %copy-done.9, bf16[432,640]{1,0:T(8,128)(2,1)} %copy-done.12, bf16[432,640]{1,0:T(8,128)(2,1)} %copy-done.10, bf16[432,640]{1,0:T(8,128)(2,1)} %copy-done.14, bf16[432,640]{1,0:T(8,128)(2,1)} %copy-done.13, ...), custom_call_target="tpu_custom_call" | custom-call | flops 100000000 | bytes 65536 | tf_op jit(solution)/shard_map/mlp_block/pallas_call | solution.py:205
  201.0 8.1 %all-to-all-start = ((bf16[8,128,512]{2,1,0:T(8,128)(2,1)}), bf16[8,128,512]{2,1,0:T(8,128)(2,1)S(1)}, u32[]{:S(2)}, u32[]{:S(2)}) async-start(bf16[8,128,512]{2,1,0:T(8,128)(2,1)} %bitcast.26), calls=%async_computation | async-start | bytes 2097152 | tf_op jit(solution)/shard_map/all_to_all | solution.py:395
  209.1 13.4 %mlp_block.6 = bf16[432,512]{1,0:T(8,128)(2,1)} custom-call(s32[12]{0:T(128)} %stack.38.refs_0_, bf16[432,640]{1,0:T(8,128)(2,1)} %copy-done.9, bf16[432,640]{1,0:T(8,128)(2,1)} %copy-done.12, bf16[432,640]{1,0:T(8,128)(2,1)} %copy-done.10, bf16[432,640]{1,0:T(8,128)(2,1)} %copy-done.14, bf16[432,640]{1,0:T(8,128)(2,1)} %copy-done.13, ...), custom_call_target="tpu_custom_call" | custom-call | flops 100000000 | bytes 65536 | tf_op jit(solution)/shard_map/mlp_block/pallas_call | solution.py:205
  222.5 4.6 %collective-permute-done.24 = bf16[128,5120]{1,0:T(8,128)(2,1)} collective-permute-done((bf16[128,5120]{1,0:T(8,128)(2,1)}, bf16[128,5120]{1,0:T(8,128)(2,1)}, u32[]{:S(2)}, u32[]{:S(2)}) %collective-permute-start.24) | collective-permute-done | bytes 1310752 | tf_op jit(solution)/shard_map/ppermute | solution.py:242
  230.5 13.4 %mlp_block.7 = bf16[432,512]{1,0:T(8,128)(2,1)} custom-call(s32[12]{0:T(128)} %stack.38.refs_0_, bf16[432,640]{1,0:T(8,128)(2,1)} %copy-done.9, bf16[432,640]{1,0:T(8,128)(2,1)} %copy-done.12, bf16[432,640]{1,0:T(8,128)(2,1)} %copy-done.10, bf16[432,640]{1,0:T(8,128)(2,1)} %copy-done.14, bf16[432,640]{1,0:T(8,128)(2,1)} %copy-done.13, ...), custom_call_target="tpu_custom_call" | custom-call | flops 100000000 | bytes 65536 | tf_op jit(solution)/shard_map/mlp_block/pallas_call | solution.py:205
  253.4 9.8 %mlp_block.8 = bf16[432,256]{1,0:T(8,128)(2,1)} custom-call(s32[12]{0:T(128)} %stack.38.refs_0_, bf16[432,640]{1,0:T(8,128)(2,1)} %copy-done.9, bf16[432,640]{1,0:T(8,128)(2,1)} %copy-done.12, bf16[432,640]{1,0:T(8,128)(2,1)} %copy-done.10, bf16[432,640]{1,0:T(8,128)(2,1)} %copy-done.14, bf16[432,640]{1,0:T(8,128)(2,1)} %copy-done.13, ...), custom_call_target="tpu_custom_call" | custom-call | flops 100000000 | bytes 65536 | tf_op jit(solution)/shard_map/mlp_block/pallas_call | solution.py:205
  269.4 9.8 %mlp_block.9 = bf16[432,256]{1,0:T(8,128)(2,1)} custom-call(s32[12]{0:T(128)} %stack.38.refs_0_, bf16[432,640]{1,0:T(8,128)(2,1)} %copy-done.9, bf16[432,640]{1,0:T(8,128)(2,1)} %copy-done.12, bf16[432,640]{1,0:T(8,128)(2,1)} %copy-done.10, bf16[432,640]{1,0:T(8,128)(2,1)} %copy-done.14, bf16[432,640]{1,0:T(8,128)(2,1)} %copy-done.13, ...), custom_call_target="tpu_custom_call" | custom-call | flops 100000000 | bytes 65536 | tf_op jit(solution)/shard_map/mlp_block/pallas_call | solution.py:205
  279.3 4.3 %collective-permute-done.38 = bf16[432,256]{1,0:T(8,128)(2,1)S(1)} collective-permute-done((bf16[432,256]{1,0:T(8,128)(2,1)}, bf16[432,256]{1,0:T(8,128)(2,1)S(1)}, u32[]{:S(2)}, u32[]{:S(2)}) %collective-permute-start.38) | collective-permute-done | bytes 221216 | tf_op jit(solution)/shard_map/ppermute | solution.py:242
  285.5 6.8 %collective-permute-done.40 = bf16[432,256]{1,0:T(8,128)(2,1)S(1)} collective-permute-done((bf16[432,256]{1,0:T(8,128)(2,1)}, bf16[432,256]{1,0:T(8,128)(2,1)S(1)}, u32[]{:S(2)}, u32[]{:S(2)}) %collective-permute-start.40) | collective-permute-done | bytes 221216 | tf_op jit(solution)/shard_map/ppermute | solution.py:242
  (189 shorter events, 76.2 us)
Async XLA Ops:
  2.7 28.6 %collective-permute-start = (bf16[432,640]{1,0:T(8,128)(2,1)}, bf16[432,640]{1,0:T(8,128)(2,1)S(1)}, u32[]{:S(2)}, u32[]{:S(2)}) collective-permute-start(bf16[432,640]{1,0:T(8,128)(2,1)} %dynamic-slice_bitcast_fusion), channel_id=1, source_target_pairs={{0,16},{4,20},{8,24},{12,28},{16,0},{20,4},{24,8},{28,12},{1,17},{... | collective-permute-start | bytes 1658888 | tf_op jit(solution)/shard_map/ppermute | solution.py:242
  31.4 27.9 %collective-permute-start.4 = (bf16[256,5120]{1,0:T(8,128)(2,1)}, bf16[256,5120]{1,0:T(8,128)(2,1)}, u32[]{:S(2)}, u32[]{:S(2)}) collective-permute-start(bf16[256,5120]{1,0:T(8,128)(2,1)} %convolution_convert_fusion), channel_id=1, source_target_pairs={{0,1},{1,0},{2,3},{3,2},{4,5},{5,4},{6,7},{7,6},{8,9},{9,8},{10,11... | collective-permute-start | bytes 7864328 | tf_op jit(solution)/shard_map/ppermute | solution.py:266
  31.4 27.9 %collective-permute-start.1 = (bf16[432,640]{1,0:T(8,128)(2,1)}, bf16[432,640]{1,0:T(8,128)(2,1)S(1)}, u32[]{:S(2)}, u32[]{:S(2)}) collective-permute-start(bf16[432,640]{1,0:T(8,128)(2,1)} %get-tuple-element.72), channel_id=1, source_target_pairs={{0,16},{4,20},{8,24},{12,28},{16,0},{20,4},{24,8},{28,12},{1,17},{... | collective-permute-start | bytes 1658888 | tf_op jit(solution)/shard_map/ppermute | solution.py:242
  31.4 27.9 %collective-permute-start.2 = (bf16[432,640]{1,0:T(8,128)(2,1)S(1)}, bf16[432,640]{1,0:T(8,128)(2,1)S(1)}, u32[]{:S(2)}, u32[]{:S(2)}) collective-permute-start(bf16[432,640]{1,0:T(8,128)(2,1)S(1)} %get-tuple-element.73.refs_1_), channel_id=1, source_target_pairs={{0,4},{4,0},{8,12},{12,8},{16,20},{20,16},{24,28},{28,24},{1,5},{5... | collective-permute-start | bytes 1658888 | tf_op jit(solution)/shard_map/ppermute | solution.py:249
  33.0 26.3 %collective-permute-start.3 = (bf16[432,640]{1,0:T(8,128)(2,1)S(1)}, bf16[432,640]{1,0:T(8,128)(2,1)}, u32[]{:S(2)}, u32[]{:S(2)}) collective-permute-start(bf16[432,640]{1,0:T(8,128)(2,1)S(1)} %get-tuple-element.74.refs_9_), channel_id=1, source_target_pairs={{0,4},{4,0},{8,12},{12,8},{16,20},{20,16},{24,28},{28,24},{1,5},{5... | collective-permute-start | bytes 1658888 | tf_op jit(solution)/shard_map/ppermute | solution.py:249
  75.7 29.8 %collective-permute-start.11 = (bf16[128,5120]{1,0:T(8,128)(2,1)}, bf16[128,5120]{1,0:T(8,128)(2,1)}, u32[]{:S(2)}, u32[]{:S(2)}) collective-permute-start(bf16[128,5120]{1,0:T(8,128)(2,1)} %fusion.1), channel_id=1, source_target_pairs={{0,2},{1,3},{2,0},{3,1},{4,6},{5,7},{6,4},{7,5},{8,10},{9,11},{10,... | collective-permute-start | bytes 3932168 | tf_op jit(solution)/shard_map/ppermute | solution.py:339
  80.2 23.3 %collective-permute-start.8 = (bf16[432,640]{1,0:T(8,128)(2,1)S(1)}, bf16[432,640]{1,0:T(8,128)(2,1)S(1)}, u32[]{:S(2)}, u32[]{:S(2)}) collective-permute-start(bf16[432,640]{1,0:T(8,128)(2,1)S(1)} %copy-done.33), channel_id=1, source_target_pairs={{0,24},{4,28},{8,0},{12,4},{16,8},{20,12},{24,16},{28,20},{1,25},{... | collective-permute-start | bytes 1658888 | tf_op jit(solution)/shard_map/ppermute | solution.py:242
  80.7 22.7 %collective-permute-start.9 = (bf16[432,640]{1,0:T(8,128)(2,1)S(1)}, bf16[432,640]{1,0:T(8,128)(2,1)S(1)}, u32[]{:S(2)}, u32[]{:S(2)}) collective-permute-start(bf16[432,640]{1,0:T(8,128)(2,1)S(1)} %collective-permute-done.5.refs_5_), channel_id=1, source_target_pairs={{0,4},{4,0},{8,12},{12,8},{16,20},{20,16},{24,28},{28,24},{1,5},{5... | collective-permute-start | bytes 1658888 | tf_op jit(solution)/shard_map/ppermute | solution.py:249
  123.0 27.8 %collective-permute-start.14 = (bf16[128,5120]{1,0:T(8,128)(2,1)}, bf16[128,5120]{1,0:T(8,128)(2,1)}, u32[]{:S(2)}, u32[]{:S(2)}) collective-permute-start(bf16[128,5120]{1,0:T(8,128)(2,1)} %multiply_convert_fusion.refs_17_), channel_id=1, source_target_pairs={{0,8},{4,12},{8,0},{12,4},{16,24},{20,28},{24,16},{28,20},{1,9},{5... | collective-permute-start | bytes 3932168 | tf_op jit(solution)/shard_map/ppermute | solution.py:242
  123.1 27.8 %collective-permute-start.15 = (bf16[128,5120]{1,0:T(8,128)(2,1)}, bf16[128,5120]{1,0:T(8,128)(2,1)}, u32[]{:S(2)}, u32[]{:S(2)}) collective-permute-start(bf16[128,5120]{1,0:T(8,128)(2,1)} %multiply_convert_fusion.refs_17_), channel_id=1, source_target_pairs={{8,16},{12,20},{16,8},{20,12},{9,17},{13,21},{17,9},{21,13},{10,18... | collective-permute-start | bytes 3932168 | tf_op jit(solution)/shard_map/ppermute | solution.py:242
  124.9 27.3 %collective-permute-start.18 = (bf16[128,5120]{1,0:T(8,128)(2,1)}, bf16[128,5120]{1,0:T(8,128)(2,1)S(1)}, u32[]{:S(2)}, u32[]{:S(2)}) collective-permute-start(bf16[128,5120]{1,0:T(8,128)(2,1)} %multiply_convert_fusion.refs_17_), channel_id=1, source_target_pairs={{0,2},{1,3},{2,0},{3,1},{4,6},{5,7},{6,4},{7,5},{8,10},{9,11},{10,... | collective-permute-start | bytes 3932168 | tf_op jit(solution)/shard_map/ppermute | solution.py:257
  127.9 21.0 %collective-permute-start.16 = (bf16[432,640]{1,0:T(8,128)(2,1)S(1)}, bf16[432,640]{1,0:T(8,128)(2,1)S(1)}, u32[]{:S(2)}, u32[]{:S(2)}) collective-permute-start(bf16[432,640]{1,0:T(8,128)(2,1)S(1)} %collective-permute-done.12.refs_13_), channel_id=1, source_target_pairs={{0,4},{4,0},{8,12},{12,8},{16,20},{20,16},{24,28},{28,24},{1,5},{5... | collective-permute-start | bytes 1658888 | tf_op jit(solution)/shard_map/ppermute | solution.py:249
  152.2 28.5 %collective-permute-start.19 = (bf16[128,5120]{1,0:T(8,128)(2,1)}, bf16[128,5120]{1,0:T(8,128)(2,1)}, u32[]{:S(2)}, u32[]{:S(2)}) collective-permute-start(bf16[128,5120]{1,0:T(8,128)(2,1)} %collective-permute-done.15), channel_id=1, source_target_pairs={{8,0},{12,4},{16,24},{20,28},{9,1},{13,5},{17,25},{21,29},{10,2},{... | collective-permute-start | bytes 3932168 | tf_op jit(solution)/shard_map/ppermute | solution.py:242
  153.5 27.2 %collective-permute-start.20 = (bf16[128,5120]{1,0:T(8,128)(2,1)}, bf16[128,5120]{1,0:T(8,128)(2,1)}, u32[]{:S(2)}, u32[]{:S(2)}) collective-permute-start(bf16[128,5120]{1,0:T(8,128)(2,1)} %collective-permute-done.14.refs_17_), channel_id=1, source_target_pairs={{8,16},{12,20},{16,8},{20,12},{9,17},{13,21},{17,9},{21,13},{10,18... | collective-permute-start | bytes 3932168 | tf_op jit(solution)/shard_map/ppermute | solution.py:242
  155.2 26.6 %collective-permute-start.21 = (bf16[128,5120]{1,0:T(8,128)(2,1)}, bf16[128,5120]{1,0:T(8,128)(2,1)}, u32[]{:S(2)}, u32[]{:S(2)}) collective-permute-start(bf16[128,5120]{1,0:T(8,128)(2,1)} %collective-permute-done.14.refs_17_), channel_id=1, source_target_pairs={{0,2},{1,3},{2,0},{3,1},{4,6},{5,7},{6,4},{7,5},{8,10},{9,11},{10,... | collective-permute-start | bytes 3932168 | tf_op jit(solution)/shard_map/ppermute | solution.py:257
  156.9 25.0 %collective-permute-start.23 = (bf16[128,5120]{1,0:T(8,128)(2,1)S(1)}, bf16[128,5120]{1,0:T(8,128)(2,1)}, u32[]{:S(2)}, u32[]{:S(2)}) collective-permute-start(bf16[128,5120]{1,0:T(8,128)(2,1)S(1)} %collective-permute-done.18.refs_18_), channel_id=1, source_target_pairs={{0,1},{1,0},{2,3},{3,2},{4,5},{5,4},{6,7},{7,6},{8,9},{9,8},{10,11... | collective-permute-start | bytes 3932168 | tf_op jit(solution)/shard_map/ppermute | solution.py:266
  156.9 52.2 %collective-permute-start.26 = (bf16[128,5120]{1,0:T(8,128)(2,1)}, bf16[128,5120]{1,0:T(8,128)(2,1)}, u32[]{:S(2)}, u32[]{:S(2)}) collective-permute-start(bf16[128,5120]{1,0:T(8,128)(2,1)} %collective-permute-done.14.refs_17_), channel_id=1, source_target_pairs={{0,1},{1,0},{2,3},{3,2},{4,5},{5,4},{6,7},{7,6},{8,9},{9,8},{10,11... | collective-permute-start | bytes 3932168 | tf_op jit(solution)/shard_map/ppermute | solution.py:266
  181.9 27.2 %collective-permute-start.27 = (bf16[128,5120]{1,0:T(8,128)(2,1)}, bf16[128,5120]{1,0:T(8,128)(2,1)}, u32[]{:S(2)}, u32[]{:S(2)}) collective-permute-start(bf16[128,5120]{1,0:T(8,128)(2,1)} %collective-permute-done.21.refs_18_), channel_id=1, source_target_pairs={{0,1},{1,0},{2,3},{3,2},{4,5},{5,4},{6,7},{7,6},{8,9},{9,8},{10,11... | collective-permute-start | bytes 3932168 | tf_op jit(solution)/shard_map/ppermute | solution.py:266
  183.3 39.2 %collective-permute-start.25 = (bf16[128,5120]{1,0:T(8,128)(2,1)S(1)}, bf16[128,5120]{1,0:T(8,128)(2,1)}, u32[]{:S(2)}, u32[]{:S(2)}) collective-permute-start(bf16[128,5120]{1,0:T(8,128)(2,1)S(1)} %broadcast_select_fusion.refs_17_), channel_id=1, source_target_pairs={{0,2},{1,3},{2,0},{3,1},{4,6},{5,7},{6,4},{7,5},{8,10},{9,11},{10,... | collective-permute-start | bytes 3932168 | tf_op jit(solution)/shard_map/ppermute | solution.py:257
  185.2 42.0 %collective-permute-start.24 = (bf16[128,5120]{1,0:T(8,128)(2,1)}, bf16[128,5120]{1,0:T(8,128)(2,1)}, u32[]{:S(2)}, u32[]{:S(2)}) collective-permute-start(bf16[128,5120]{1,0:T(8,128)(2,1)} %collective-permute-done.20), channel_id=1, source_target_pairs={{8,0},{12,4},{16,24},{20,28},{9,1},{13,5},{17,25},{21,29},{10,2},{... | collective-permute-start | bytes 3932168 | tf_op jit(solution)/shard_map/ppermute | solution.py:242
  187.2 43.3 %collective-permute-start.29 = (bf16[128,5120]{1,0:T(8,128)(2,1)S(1)}, bf16[128,5120]{1,0:T(8,128)(2,1)}, u32[]{:S(2)}, u32[]{:S(2)}) collective-permute-start(bf16[128,5120]{1,0:T(8,128)(2,1)S(1)} %broadcast_select_fusion.refs_17_), channel_id=1, source_target_pairs={{0,1},{1,0},{2,3},{3,2},{4,5},{5,4},{6,7},{7,6},{8,9},{9,8},{10,11... | collective-permute-start | bytes 3932168 | tf_op jit(solution)/shard_map/ppermute | solution.py:266
  201.0 45.4 %all-to-all-start = ((bf16[8,128,512]{2,1,0:T(8,128)(2,1)}), bf16[8,128,512]{2,1,0:T(8,128)(2,1)S(1)}, u32[]{:S(2)}, u32[]{:S(2)}) async-start(bf16[8,128,512]{2,1,0:T(8,128)(2,1)} %bitcast.26), calls=%async_computation | async-start | bytes 2097152 | tf_op jit(solution)/shard_map/all_to_all | solution.py:395
  230.2 22.3 %collective-permute-start.33 = (bf16[64,5120]{1,0:T(8,128)(2,1)}, bf16[64,5120]{1,0:T(8,128)(2,1)}, u32[]{:S(2)}, u32[]{:S(2)}) collective-permute-start(bf16[64,5120]{1,0:T(8,128)(2,1)} %get-tuple-element.132.refs_17_), channel_id=1, source_target_pairs={{0,1},{1,0},{2,3},{3,2},{4,5},{5,4},{6,7},{7,6},{8,9},{9,8},{10,11... | collective-permute-start | bytes 1966088 | tf_op jit(solution)/shard_map/ppermute | solution.py:266
  250.3 19.1 %collective-permute-start.36 = (bf16[64,5120]{1,0:T(8,128)(2,1)S(1)}, bf16[64,5120]{1,0:T(8,128)(2,1)}, u32[]{:S(2)}, u32[]{:S(2)}) collective-permute-start(bf16[64,5120]{1,0:T(8,128)(2,1)S(1)} %get-tuple-element.118.refs_17_), channel_id=1, source_target_pairs={{0,1},{1,0},{2,3},{3,2},{4,5},{5,4},{6,7},{7,6},{8,9},{9,8},{10,11... | collective-permute-start | bytes 1966088 | tf_op jit(solution)/shard_map/ppermute | solution.py:266
  (61 other events, 939.3 us)

commit v5 on v4

--- a/solution.py
+++ b/solution.py
@@ -131,10 +131,11 @@
     )(sources, pages_in)
 
 
-def mlp_kernel(count, pieces, halves, ids_ref, *refs):
+def mlp_kernel(count, pieces, halves, outs, ids_ref, *refs):
     weights = (refs[:count], refs[count:2 * count])
     rows_in = refs[2 * count:2 * count + pieces]
-    out_ref, gate_buf, up_buf, row_buf, acc, weight_sems, row_sems = refs[2 * count + pieces:]
+    out_refs = refs[2 * count + pieces:2 * count + pieces + outs]
+    gate_buf, up_buf, row_buf, acc, weight_sems, row_sems = refs[2 * count + pieces + outs:]
     units, depth = weights[0][0].shape
     parts = weight_sems.shape[2]
     piece = rows_in[0].shape[0] // halves
@@ -162,8 +163,8 @@
         copy.start()
     for copy in first:
         copy.wait()
-    tokens = out_ref.shape[1]
-    tile = min(256, tokens)
+    tokens, span = row_buf.shape[0], out_refs[0].shape[1]
+    tile = min(256, span)
     for index in range(count):
         for copy in second[2 * parts * index:2 * parts * (index + 1)]:
             copy.wait()
@@ -178,10 +179,11 @@
     for start in range(0, tokens, tile):
         gate = acc[0, :, start:start + tile]
         up = acc[1, :, start:start + tile]
-        out_ref[:, start:start + tile] = (gate / (1.0 + jnp.exp(-gate)) * up).astype(jnp.bfloat16)
-
-
-def mlp_block(weights, weight_ids, rows_in, row_ids, halves):
+        at = start % span
+        out_refs[start // span][:, at:at + tile] = (gate / (1.0 + jnp.exp(-gate)) * up).astype(jnp.bfloat16)
+
+
+def mlp_block(weights, weight_ids, rows_in, row_ids, halves, outs):
     count, pieces = len(weight_ids), len(row_ids)
     units, depth = weights[0].shape
     width = rows_in[0].shape[1]
@@ -199,14 +201,14 @@
                 rows = lax.dynamic_update_slice(rows, rows_in[index][half * piece:(half + 1) * piece], (at, 0))
         gate = lax.dot_general(both[0], rows, NT, preferred_element_type=jnp.float32)
         up = lax.dot_general(both[1], rows, NT, preferred_element_type=jnp.float32)
-        return (jax.nn.silu(gate) * up).astype(jnp.bfloat16)
+        return jnp.split((jax.nn.silu(gate) * up).astype(jnp.bfloat16), outs, axis=1)
     ids = jnp.stack([jnp.asarray(i, jnp.int32) for i in list(weight_ids) + list(row_ids)])
     anywhere = pl.BlockSpec(memory_space=pl.ANY)
     return pl.pallas_call(
-        lambda *refs: mlp_kernel(count, pieces, halves, *refs),
-        out_shape=jax.ShapeDtypeStruct((units, tokens), jnp.bfloat16),
+        lambda *refs: mlp_kernel(count, pieces, halves, outs, *refs),
+        out_shape=[jax.ShapeDtypeStruct((units, tokens // outs), jnp.bfloat16)] * outs,
         in_specs=[pl.BlockSpec(memory_space=pltpu.SMEM)] + [anywhere] * (2 * count + pieces),
-        out_specs=pl.BlockSpec(memory_space=pltpu.VMEM),
+        out_specs=[pl.BlockSpec(memory_space=pltpu.VMEM)] * outs,
         scratch_shapes=[
             pltpu.VMEM((count, units, depth), jnp.bfloat16),
             pltpu.VMEM((count, units, depth), jnp.bfloat16),
@@ -382,8 +384,9 @@
     def shared(block, block_x):
         return [block, *block_x, *[across_cores(p) for p in (block, *block_x)]]
 
-    def work(pieces):
-        return mlp_block(weights, weight_ids, pieces, row_ids, pieces[0].shape[0] // run)
+    def work(pieces, outs=1):
+        done = mlp_block(weights, weight_ids, pieces, row_ids, pieces[0].shape[0] // run, outs)
+        return done[0] if outs == 1 else list(done)
 
     pieces_0 = shared(near, near_x)
     next_2e, next_2m, next_1_x, pieces_0 = lax.optimization_barrier((next_2e, next_2m, next_1_x, pieces_0))
@@ -398,25 +401,24 @@
     hidden_1 = work(shared(next_1, next_1_x))
     next_3, next_2_x, hidden_0, hidden_1 = lax.optimization_barrier((next_3, next_2_x, hidden_0, hidden_1))
     next_3a = jnp.where(at_end, next_3[:run], middle_1[:run])
+    next_3a, next_3 = lax.optimization_barrier((next_3a, next_3))
+    next_3a_x = along_x(next_3a)
     next_3b = jnp.where(at_end, next_3[run:], middle_1[run:])
-    next_3a_x = along_x(next_3a)
-    hidden_2 = work(shared(next_2, next_2_x))
+    hidden_2 = work(shared(next_2, next_2_x), 2)
     back_1 = along_z(hidden_1, flip[1])
     next_3b, next_3a_x, hidden_2, back_1, kv_in = lax.optimization_barrier(
         (next_3b, next_3a_x, hidden_2, back_1, kv_in)
     )
     next_3b_x = along_x(next_3b)
-    back_2 = [along_z(hidden_2[:, :rows // 2], flip[2]), along_z(hidden_2[:, rows // 2:], flip[2])]
+    back_2 = [along_z(half, flip[2]) for half in hidden_2]
     hidden_3a = work(shared(next_3a, next_3a_x))
+    next_3b_x, hidden_3a, back_2[0] = lax.optimization_barrier((next_3b_x, hidden_3a, back_2[0]))
+    back_3a = along_z(hidden_3a, flip[3])
+    hidden_3b, back_2[1], kv_in = lax.optimization_barrier((work(shared(next_3b, next_3b_x)), back_2[1], kv_in))
+    back_3b = along_z(hidden_3b, flip[3])
     mine = page_table[None] == (me_req * REQS + jnp.arange(REQS, dtype=jnp.int32))[:, None, None]
     sources = jnp.sum(jnp.where(mine, jnp.arange(n_req, dtype=jnp.int32)[None, :, None], 0), axis=(1, 2))
     cache_out = write_cache(sources.astype(jnp.int32), kv_in, kv_heads)
-    next_3b_x, hidden_3a, back_2[0], cache_out = lax.optimization_barrier(
-        (next_3b_x, hidden_3a, back_2[0], cache_out)
-    )
-    back_3a = along_z(hidden_3a, flip[3])
-    hidden_3b, back_2[1] = lax.optimization_barrier((work(shared(next_3b, next_3b_x)), back_2[1]))
-    back_3b = along_z(hidden_3b, flip[3])
     hidden_t = jnp.zeros((units_all, rows), jnp.bfloat16)
     for by, at, done in (
         (0, 0, hidden_0),

time: 299 us -> 297 us (level)
    ppermute x16, waiting for transfers between devices: 97.6 us -> 94.1 us  [along_z(): lax.ppermute(value, 'req', [(a * n_y + c, b * n_y + c) for a, b in moves...]
    unnamed x86 -> x92, local copies, waits for them, and re-layouts: 4.54 us -> 6.04 us
  transfers between devices with their start and end apart: 42 -> 42, of which waited for: 21 -> 23; matrix products, arithmetic and copies ran while one was open for 12% -> 11% of each run, Pallas kernels for 23% -> 23%
where the time goes in v5:
time: 297 us; the launch traced here: 292 us
  waiting for transfers between devices  133 us (45%)
  Pallas kernels  66.5 us (22%)
  starting transfers between devices  45.9 us (15%)
  other arithmetic  18.8 us (6%)
  local copies, waits for them, and re-layouts  15 us (5%)
  matrix products  10.8 us (4%)
    ppermute x16, waiting for transfers between devices, along_z(): lax.ppermute(value, 'req', [(a * n_y + c, b * n_y + c) for a, b in moves...  94.1 us
    pallas_call x5, Pallas kernels, mlp_block(): pl.pallas_call(lambda *refs: mlp_kernel(count, pieces, halves, outs, *ref...  59.9 us
    ppermute x8, waiting for transfers between devices, along_y(): lax.ppermute(value, 'req', [(a * n_y + b, a * n_y + (b + step) % n_y) for...  30.5 us
    ppermute x16, starting transfers between devices, along_z(): lax.ppermute(value, 'req', [(a * n_y + c, b * n_y + c) for a, b in moves...  20.5 us
    dot_general x2, matrix products, project(): jnp.dot(picked, w_out, preferred_element_type=jnp.float32)  10.8 us
    ppermute x8, starting transfers between devices, along_y(): lax.ppermute(value, 'req', [(a * n_y + b, a * n_y + (b + step) % n_y) for...  9.18 us
    all_to_all x1, starting transfers between devices, shards(): lax.all_to_all(kv_send.reshape(n_req, PAGE, 2 * kv_heads * HD), 'req', sp...  8.18 us
    ppermute x5, waiting for transfers between devices, along_x(): lax.ppermute(value, 'mp', [(a * CORES + b, (a + step) % n_x * CORES + b)...  6.19 us
  transfers between devices with their start and end apart: 42, of which 23 were waited for; matrix products, arithmetic and copies ran while one was open for 11% of the time, Pallas kernels for 23%

profile of v5, /device:TPU:0, one launch (start us, length us, event | category | flops | bytes accessed | tf_op | source)
XLA Modules:
  0.0 292.0 jit_solution(17331768476440797669)
XLA Ops:
  2.8 4.0 %collective-permute-start = (bf16[432,640]{1,0:T(8,128)(2,1)}, bf16[432,640]{1,0:T(8,128)(2,1)S(1)}, u32[]{:S(2)}, u32[]{:S(2)}) collective-permute-start(bf16[432,640]{1,0:T(8,128)(2,1)} %dynamic-slice_bitcast_fusion), channel_id=1, source_target_pairs={{0,16},{4,20},{8,24},{12,28},{16,0},{20,4},{24,8},{28,12},{1,17},{... | collective-permute-start | bytes 1658888 | tf_op jit(solution)/shard_map/ppermute | solution.py:244
  11.6 4.5 %attention.1 = (bf16[512,768]{1,0:T(8,128)(2,1)S(1)}, bf16[1024,512]{1,0:T(8,128)(2,1)}) custom-call(bf16[512,768]{1,0:T(8,128)(2,1)S(1)} %copy-done, bf16[512,256]{1,0:T(8,128)(2,1)S(1)} %copy-done.1, bf16[512,256]{1,0:T(8,128)(2,1)S(1)} %copy-done.2, f32[1,768]{1,0:T(1,128)S(1)} %broadcast_in_dim.71.refs_3_, f32[1,256]{1,0:T(1,128)S(1)} %bitcast.46, ...), custom_call_target="tpu_custom_call" | custom-call | flops 100000000 | bytes 65536 | tf_op jit(solution)/shard_map/attention/pallas_call | solution.py:95
  16.1 7.1 %convolution_convert_fusion = bf16[256,5120]{1,0:T(8,128)(2,1)} fusion(bf16[768,5120]{1,0:T(8,128)(2,1)} %param.23, bf16[2,256,768]{2,1,0:T(8,128)(2,1)S(1)} %bitcast.48, s32[]{:T(128)S(6)} %select_n.202), kind=kOutput, calls=%fused_computation | convolution fusion | flops 2014576640 | bytes 10878980 | tf_op jit(solution)/shard_map/dot_general | solution.py:313
  24.8 3.7 %convolution_convert_fusion.1 = bf16[256,5120]{1,0:T(8,128)(2,1)} fusion(bf16[768,5120]{1,0:T(8,128)(2,1)S(1)} %bitcast.57, bf16[2,256,768]{2,1,0:T(8,128)(2,1)S(1)} %bitcast.49, s32[]{:T(128)S(6)} %select_n.201), kind=kOutput, calls=%fused_computation.1 | convolution fusion | flops 2014576640 | bytes 10878980 | tf_op jit(solution)/shard_map/dot_general | solution.py:313
  33.5 25.6 %collective-permute-done.1.refs_11_ = bf16[432,640]{1,0:T(8,128)(2,1)S(1)} collective-permute-done((bf16[432,640]{1,0:T(8,128)(2,1)S(1)}, bf16[432,640]{1,0:T(8,128)(2,1)S(1)}, u32[]{:S(2)}, u32[]{:S(2)}) %collective-permute-start.1) | collective-permute-done | bytes 552992 | tf_op jit(solution)/shard_map/ppermute | solution.py:244
  59.1 3.0 %collective-permute-start.5 = (bf16[432,640]{1,0:T(8,128)(2,1)}, bf16[432,640]{1,0:T(8,128)(2,1)S(1)}, u32[]{:S(2)}, u32[]{:S(2)}) collective-permute-start(bf16[432,640]{1,0:T(8,128)(2,1)} %get-tuple-element.83), channel_id=1, source_target_pairs={{0,8},{4,12},{8,16},{12,20},{16,24},{20,28},{24,0},{28,4},{1,9},{5... | collective-permute-start | bytes 1658888 | tf_op jit(solution)/shard_map/ppermute | solution.py:244
  63.7 3.4 %convert_add_fusion = f32[256,5120]{1,0:T(8,128)S(1)} fusion(bf16[256,5120]{1,0:T(8,128)(2,1)} %collective-permute-done.4, bf16[256,5120]{1,0:T(8,128)(2,1)} %convolution_convert_fusion.1), kind=kLoop, calls=%fused_computation.2 | loop fusion | flops 3932160 | bytes 10485760 | tf_op jit(solution)/shard_map/add | solution.py:328
  69.6 5.8 %collective-permute-done.5.refs_5_ = bf16[432,640]{1,0:T(8,128)(2,1)S(1)} collective-permute-done((bf16[432,640]{1,0:T(8,128)(2,1)}, bf16[432,640]{1,0:T(8,128)(2,1)S(1)}, u32[]{:S(2)}, u32[]{:S(2)}) %collective-permute-start.5) | collective-permute-done | bytes 552992 | tf_op jit(solution)/shard_map/ppermute | solution.py:244
  82.7 10.0 %collective-permute-done.10.refs_12_ = bf16[432,640]{1,0:T(8,128)(2,1)S(1)} collective-permute-done((bf16[432,640]{1,0:T(8,128)(2,1)S(1)}, bf16[432,640]{1,0:T(8,128)(2,1)S(1)}, u32[]{:S(2)}, u32[]{:S(2)}) %collective-permute-start.10) | collective-permute-done | bytes 552992 | tf_op jit(solution)/shard_map/ppermute | solution.py:251
  94.4 8.9 %collective-permute-done.8.refs_15_ = bf16[432,640]{1,0:T(8,128)(2,1)S(1)} collective-permute-done((bf16[432,640]{1,0:T(8,128)(2,1)}, bf16[432,640]{1,0:T(8,128)(2,1)S(1)}, u32[]{:S(2)}, u32[]{:S(2)}) %collective-permute-start.8) | collective-permute-done | bytes 552992 | tf_op jit(solution)/shard_map/ppermute | solution.py:244
  113.1 9.6 %collective-permute-done.12.refs_13_ = bf16[432,640]{1,0:T(8,128)(2,1)S(1)} collective-permute-done((bf16[432,640]{1,0:T(8,128)(2,1)S(1)}, bf16[432,640]{1,0:T(8,128)(2,1)S(1)}, u32[]{:S(2)}, u32[]{:S(2)}) %collective-permute-start.12) | collective-permute-done | bytes 552992 | tf_op jit(solution)/shard_map/ppermute | solution.py:244
  128.1 13.4 %collective-permute-done.17.refs_16_ = bf16[432,640]{1,0:T(8,128)(2,1)S(1)} collective-permute-done((bf16[432,640]{1,0:T(8,128)(2,1)S(1)}, bf16[432,640]{1,0:T(8,128)(2,1)S(1)}, u32[]{:S(2)}, u32[]{:S(2)}) %collective-permute-start.17) | collective-permute-done | bytes 552992 | tf_op jit(solution)/shard_map/ppermute | solution.py:251
  141.6 6.7 %collective-permute-done.16.refs_14_ = bf16[432,640]{1,0:T(8,128)(2,1)S(1)} collective-permute-done((bf16[432,640]{1,0:T(8,128)(2,1)S(1)}, bf16[432,640]{1,0:T(8,128)(2,1)S(1)}, u32[]{:S(2)}, u32[]{:S(2)}) %collective-permute-start.16) | collective-permute-done | bytes 552992 | tf_op jit(solution)/shard_map/ppermute | solution.py:251
  156.6 22.9 %collective-permute-done.19 = bf16[128,5120]{1,0:T(8,128)(2,1)} collective-permute-done((bf16[128,5120]{1,0:T(8,128)(2,1)}, bf16[128,5120]{1,0:T(8,128)(2,1)}, u32[]{:S(2)}, u32[]{:S(2)}) %collective-permute-start.19) | collective-permute-done | bytes 1310752 | tf_op jit(solution)/shard_map/ppermute | solution.py:244
  186.3 13.4 %mlp_block.5 = bf16[432,512]{1,0:T(8,128)(2,1)} custom-call(s32[12]{0:T(128)} %stack.38.refs_0_, bf16[432,640]{1,0:T(8,128)(2,1)} %copy-done.9, bf16[432,640]{1,0:T(8,128)(2,1)} %copy-done.12, bf16[432,640]{1,0:T(8,128)(2,1)} %copy-done.10, bf16[432,640]{1,0:T(8,128)(2,1)} %copy-done.14, bf16[432,640]{1,0:T(8,128)(2,1)} %copy-done.13, ...), custom_call_target="tpu_custom_call" | custom-call | flops 100000000 | bytes 65536 | tf_op jit(solution)/shard_map/mlp_block/pallas_call | solution.py:207
  199.7 8.2 %all-to-all-start = ((bf16[8,128,512]{2,1,0:T(8,128)(2,1)}), bf16[8,128,512]{2,1,0:T(8,128)(2,1)S(1)}, u32[]{:S(2)}, u32[]{:S(2)}) async-start(bf16[8,128,512]{2,1,0:T(8,128)(2,1)} %bitcast.26), calls=%async_computation | async-start | bytes 2097152 | tf_op jit(solution)/shard_map/all_to_all | solution.py:398
  207.9 13.4 %mlp_block.6 = bf16[432,512]{1,0:T(8,128)(2,1)} custom-call(s32[12]{0:T(128)} %stack.38.refs_0_, bf16[432,640]{1,0:T(8,128)(2,1)} %copy-done.9, bf16[432,640]{1,0:T(8,128)(2,1)} %copy-done.12, bf16[432,640]{1,0:T(8,128)(2,1)} %copy-done.10, bf16[432,640]{1,0:T(8,128)(2,1)} %copy-done.14, bf16[432,640]{1,0:T(8,128)(2,1)} %copy-done.13, ...), custom_call_target="tpu_custom_call" | custom-call | flops 100000000 | bytes 65536 | tf_op jit(solution)/shard_map/mlp_block/pallas_call | solution.py:207
  221.4 4.8 %collective-permute-done.24 = bf16[128,5120]{1,0:T(8,128)(2,1)} collective-permute-done((bf16[128,5120]{1,0:T(8,128)(2,1)}, bf16[128,5120]{1,0:T(8,128)(2,1)}, u32[]{:S(2)}, u32[]{:S(2)}) %collective-permute-start.24) | collective-permute-done | bytes 1310752 | tf_op jit(solution)/shard_map/ppermute | solution.py:244
  230.2 13.3 %mlp_block.7 = (bf16[432,256]{1,0:T(8,128)(2,1)}, bf16[432,256]{1,0:T(8,128)(2,1)}) custom-call(s32[12]{0:T(128)} %stack.38.refs_0_, bf16[432,640]{1,0:T(8,128)(2,1)} %copy-done.9, bf16[432,640]{1,0:T(8,128)(2,1)} %copy-done.12, bf16[432,640]{1,0:T(8,128)(2,1)} %copy-done.10, bf16[432,640]{1,0:T(8,128)(2,1)} %copy-done.14, bf16[432,640]{1,0:T(8,128)(2,1)} %copy-done.13, ...), custom_call_target="tpu_custom_call" | custom-call | flops 100000000 | bytes 65536 | tf_op jit(solution)/shard_map/mlp_block/pallas_call | solution.py:207
  249.0 9.9 %mlp_block.8 = bf16[432,256]{1,0:T(8,128)(2,1)} custom-call(s32[12]{0:T(128)} %stack.38.refs_0_, bf16[432,640]{1,0:T(8,128)(2,1)} %copy-done.9, bf16[432,640]{1,0:T(8,128)(2,1)} %copy-done.12, bf16[432,640]{1,0:T(8,128)(2,1)} %copy-done.10, bf16[432,640]{1,0:T(8,128)(2,1)} %copy-done.14, bf16[432,640]{1,0:T(8,128)(2,1)} %copy-done.13, ...), custom_call_target="tpu_custom_call" | custom-call | flops 100000000 | bytes 65536 | tf_op jit(solution)/shard_map/mlp_block/pallas_call | solution.py:207
  259.5 3.4 %collective-permute-done.32.refs_18_ = bf16[64,5120]{1,0:T(8,128)(2,1)S(1)} collective-permute-done((bf16[64,5120]{1,0:T(8,128)(2,1)S(1)}, bf16[64,5120]{1,0:T(8,128)(2,1)S(1)}, u32[]{:S(2)}, u32[]{:S(2)}) %collective-permute-start.32) | collective-permute-done | bytes 655392 | tf_op jit(solution)/shard_map/ppermute | solution.py:259
  268.5 9.9 %mlp_block.9 = bf16[432,256]{1,0:T(8,128)(2,1)} custom-call(s32[12]{0:T(128)} %stack.38.refs_0_, bf16[432,640]{1,0:T(8,128)(2,1)} %copy-done.9, bf16[432,640]{1,0:T(8,128)(2,1)} %copy-done.12, bf16[432,640]{1,0:T(8,128)(2,1)} %copy-done.10, bf16[432,640]{1,0:T(8,128)(2,1)} %copy-done.14, bf16[432,640]{1,0:T(8,128)(2,1)} %copy-done.13, ...), custom_call_target="tpu_custom_call" | custom-call | flops 100000000 | bytes 65536 | tf_op jit(solution)/shard_map/mlp_block/pallas_call | solution.py:207
  278.5 3.4 %collective-permute-done.38 = bf16[432,256]{1,0:T(8,128)(2,1)S(1)} collective-permute-done((bf16[432,256]{1,0:T(8,128)(2,1)}, bf16[432,256]{1,0:T(8,128)(2,1)S(1)}, u32[]{:S(2)}, u32[]{:S(2)}) %collective-permute-start.38) | collective-permute-done | bytes 221216 | tf_op jit(solution)/shard_map/ppermute | solution.py:244
  287.1 4.2 %collective-permute-done.40 = bf16[432,256]{1,0:T(8,128)(2,1)S(1)} collective-permute-done((bf16[432,256]{1,0:T(8,128)(2,1)}, bf16[432,256]{1,0:T(8,128)(2,1)S(1)}, u32[]{:S(2)}, u32[]{:S(2)}) %collective-permute-start.40) | collective-permute-done | bytes 221216 | tf_op jit(solution)/shard_map/ppermute | solution.py:244
  (195 shorter events, 78.0 us)
Async XLA Ops:
  2.8 28.6 %collective-permute-start = (bf16[432,640]{1,0:T(8,128)(2,1)}, bf16[432,640]{1,0:T(8,128)(2,1)S(1)}, u32[]{:S(2)}, u32[]{:S(2)}) collective-permute-start(bf16[432,640]{1,0:T(8,128)(2,1)} %dynamic-slice_bitcast_fusion), channel_id=1, source_target_pairs={{0,16},{4,20},{8,24},{12,28},{16,0},{20,4},{24,8},{28,12},{1,17},{... | collective-permute-start | bytes 1658888 | tf_op jit(solution)/shard_map/ppermute | solution.py:244
  31.4 27.7 %collective-permute-start.4 = (bf16[256,5120]{1,0:T(8,128)(2,1)}, bf16[256,5120]{1,0:T(8,128)(2,1)}, u32[]{:S(2)}, u32[]{:S(2)}) collective-permute-start(bf16[256,5120]{1,0:T(8,128)(2,1)} %convolution_convert_fusion), channel_id=1, source_target_pairs={{0,1},{1,0},{2,3},{3,2},{4,5},{5,4},{6,7},{7,6},{8,9},{9,8},{10,11... | collective-permute-start | bytes 7864328 | tf_op jit(solution)/shard_map/ppermute | solution.py:268
  31.4 27.7 %collective-permute-start.1 = (bf16[432,640]{1,0:T(8,128)(2,1)S(1)}, bf16[432,640]{1,0:T(8,128)(2,1)S(1)}, u32[]{:S(2)}, u32[]{:S(2)}) collective-permute-start(bf16[432,640]{1,0:T(8,128)(2,1)S(1)} %get-tuple-element.77), channel_id=1, source_target_pairs={{0,16},{4,20},{8,24},{12,28},{16,0},{20,4},{24,8},{28,12},{1,17},{... | collective-permute-start | bytes 1658888 | tf_op jit(solution)/shard_map/ppermute | solution.py:244
  31.4 27.7 %collective-permute-start.2 = (bf16[432,640]{1,0:T(8,128)(2,1)S(1)}, bf16[432,640]{1,0:T(8,128)(2,1)S(1)}, u32[]{:S(2)}, u32[]{:S(2)}) collective-permute-start(bf16[432,640]{1,0:T(8,128)(2,1)S(1)} %get-tuple-element.78.refs_1_), channel_id=1, source_target_pairs={{0,4},{4,0},{8,12},{12,8},{16,20},{20,16},{24,28},{28,24},{1,5},{5... | collective-permute-start | bytes 1658888 | tf_op jit(solution)/shard_map/ppermute | solution.py:251
  33.1 26.1 %collective-permute-start.3 = (bf16[432,640]{1,0:T(8,128)(2,1)S(1)}, bf16[432,640]{1,0:T(8,128)(2,1)}, u32[]{:S(2)}, u32[]{:S(2)}) collective-permute-start(bf16[432,640]{1,0:T(8,128)(2,1)S(1)} %get-tuple-element.79.refs_9_), channel_id=1, source_target_pairs={{0,4},{4,0},{8,12},{12,8},{16,20},{20,16},{24,28},{28,24},{1,5},{5... | collective-permute-start | bytes 1658888 | tf_op jit(solution)/shard_map/ppermute | solution.py:251
  75.7 29.3 %collective-permute-start.11 = (bf16[128,5120]{1,0:T(8,128)(2,1)S(1)}, bf16[128,5120]{1,0:T(8,128)(2,1)}, u32[]{:S(2)}, u32[]{:S(2)}) collective-permute-start(bf16[128,5120]{1,0:T(8,128)(2,1)S(1)} %fusion.1), channel_id=1, source_target_pairs={{0,2},{1,3},{2,0},{3,1},{4,6},{5,7},{6,4},{7,5},{8,10},{9,11},{10,... | collective-permute-start | bytes 3932168 | tf_op jit(solution)/shard_map/ppermute | solution.py:341
  80.0 23.3 %collective-permute-start.8 = (bf16[432,640]{1,0:T(8,128)(2,1)}, bf16[432,640]{1,0:T(8,128)(2,1)S(1)}, u32[]{:S(2)}, u32[]{:S(2)}) collective-permute-start(bf16[432,640]{1,0:T(8,128)(2,1)} %get-tuple-element.87), channel_id=1, source_target_pairs={{0,24},{4,28},{8,0},{12,4},{16,8},{20,12},{24,16},{28,20},{1,25},{... | collective-permute-start | bytes 1658888 | tf_op jit(solution)/shard_map/ppermute | solution.py:244
  80.7 22.5 %collective-permute-start.9 = (bf16[432,640]{1,0:T(8,128)(2,1)S(1)}, bf16[432,640]{1,0:T(8,128)(2,1)S(1)}, u32[]{:S(2)}, u32[]{:S(2)}) collective-permute-start(bf16[432,640]{1,0:T(8,128)(2,1)S(1)} %collective-permute-done.5.refs_5_), channel_id=1, source_target_pairs={{0,4},{4,0},{8,12},{12,8},{16,20},{20,16},{24,28},{28,24},{1,5},{5... | collective-permute-start | bytes 1658888 | tf_op jit(solution)/shard_map/ppermute | solution.py:251
  122.7 27.6 %collective-permute-start.14 = (bf16[128,5120]{1,0:T(8,128)(2,1)}, bf16[128,5120]{1,0:T(8,128)(2,1)}, u32[]{:S(2)}, u32[]{:S(2)}) collective-permute-start(bf16[128,5120]{1,0:T(8,128)(2,1)} %multiply_convert_fusion.refs_17_), channel_id=1, source_target_pairs={{0,8},{4,12},{8,0},{12,4},{16,24},{20,28},{24,16},{28,20},{1,9},{5... | collective-permute-start | bytes 3932168 | tf_op jit(solution)/shard_map/ppermute | solution.py:244
  122.8 27.6 %collective-permute-start.15 = (bf16[128,5120]{1,0:T(8,128)(2,1)}, bf16[128,5120]{1,0:T(8,128)(2,1)}, u32[]{:S(2)}, u32[]{:S(2)}) collective-permute-start(bf16[128,5120]{1,0:T(8,128)(2,1)} %multiply_convert_fusion.refs_17_), channel_id=1, source_target_pairs={{8,16},{12,20},{16,8},{20,12},{9,17},{13,21},{17,9},{21,13},{10,18... | collective-permute-start | bytes 3932168 | tf_op jit(solution)/shard_map/ppermute | solution.py:244
  124.5 26.9 %collective-permute-start.18 = (bf16[128,5120]{1,0:T(8,128)(2,1)}, bf16[128,5120]{1,0:T(8,128)(2,1)S(1)}, u32[]{:S(2)}, u32[]{:S(2)}) collective-permute-start(bf16[128,5120]{1,0:T(8,128)(2,1)} %multiply_convert_fusion.refs_17_), channel_id=1, source_target_pairs={{0,2},{1,3},{2,0},{3,1},{4,6},{5,7},{6,4},{7,5},{8,10},{9,11},{10,... | collective-permute-start | bytes 3932168 | tf_op jit(solution)/shard_map/ppermute | solution.py:259
  127.6 20.6 %collective-permute-start.16 = (bf16[432,640]{1,0:T(8,128)(2,1)S(1)}, bf16[432,640]{1,0:T(8,128)(2,1)S(1)}, u32[]{:S(2)}, u32[]{:S(2)}) collective-permute-start(bf16[432,640]{1,0:T(8,128)(2,1)S(1)} %collective-permute-done.12.refs_13_), channel_id=1, source_target_pairs={{0,4},{4,0},{8,12},{12,8},{16,20},{20,16},{24,28},{28,24},{1,5},{5... | collective-permute-start | bytes 1658888 | tf_op jit(solution)/shard_map/ppermute | solution.py:251
  151.5 28.1 %collective-permute-start.19 = (bf16[128,5120]{1,0:T(8,128)(2,1)}, bf16[128,5120]{1,0:T(8,128)(2,1)}, u32[]{:S(2)}, u32[]{:S(2)}) collective-permute-start(bf16[128,5120]{1,0:T(8,128)(2,1)} %collective-permute-done.15), channel_id=1, source_target_pairs={{8,0},{12,4},{16,24},{20,28},{9,1},{13,5},{17,25},{21,29},{10,2},{... | collective-permute-start | bytes 3932168 | tf_op jit(solution)/shard_map/ppermute | solution.py:244
  152.7 26.8 %collective-permute-start.20 = (bf16[128,5120]{1,0:T(8,128)(2,1)}, bf16[128,5120]{1,0:T(8,128)(2,1)}, u32[]{:S(2)}, u32[]{:S(2)}) collective-permute-start(bf16[128,5120]{1,0:T(8,128)(2,1)} %collective-permute-done.14.refs_17_), channel_id=1, source_target_pairs={{8,16},{12,20},{16,8},{20,12},{9,17},{13,21},{17,9},{21,13},{10,18... | collective-permute-start | bytes 3932168 | tf_op jit(solution)/shard_map/ppermute | solution.py:244
  154.5 26.2 %collective-permute-start.21 = (bf16[128,5120]{1,0:T(8,128)(2,1)}, bf16[128,5120]{1,0:T(8,128)(2,1)}, u32[]{:S(2)}, u32[]{:S(2)}) collective-permute-start(bf16[128,5120]{1,0:T(8,128)(2,1)} %collective-permute-done.14.refs_17_), channel_id=1, source_target_pairs={{0,2},{1,3},{2,0},{3,1},{4,6},{5,7},{6,4},{7,5},{8,10},{9,11},{10,... | collective-permute-start | bytes 3932168 | tf_op jit(solution)/shard_map/ppermute | solution.py:259
  156.1 24.6 %collective-permute-start.23 = (bf16[128,5120]{1,0:T(8,128)(2,1)S(1)}, bf16[128,5120]{1,0:T(8,128)(2,1)}, u32[]{:S(2)}, u32[]{:S(2)}) collective-permute-start(bf16[128,5120]{1,0:T(8,128)(2,1)S(1)} %collective-permute-done.18.refs_18_), channel_id=1, source_target_pairs={{0,1},{1,0},{2,3},{3,2},{4,5},{5,4},{6,7},{7,6},{8,9},{9,8},{10,11... | collective-permute-start | bytes 3932168 | tf_op jit(solution)/shard_map/ppermute | solution.py:268
  156.1 51.8 %collective-permute-start.26 = (bf16[128,5120]{1,0:T(8,128)(2,1)}, bf16[128,5120]{1,0:T(8,128)(2,1)}, u32[]{:S(2)}, u32[]{:S(2)}) collective-permute-start(bf16[128,5120]{1,0:T(8,128)(2,1)} %collective-permute-done.14.refs_17_), channel_id=1, source_target_pairs={{0,1},{1,0},{2,3},{3,2},{4,5},{5,4},{6,7},{7,6},{8,9},{9,8},{10,11... | collective-permute-start | bytes 3932168 | tf_op jit(solution)/shard_map/ppermute | solution.py:268
  180.7 27.2 %collective-permute-start.27 = (bf16[128,5120]{1,0:T(8,128)(2,1)}, bf16[128,5120]{1,0:T(8,128)(2,1)}, u32[]{:S(2)}, u32[]{:S(2)}) collective-permute-start(bf16[128,5120]{1,0:T(8,128)(2,1)} %collective-permute-done.21.refs_18_), channel_id=1, source_target_pairs={{0,1},{1,0},{2,3},{3,2},{4,5},{5,4},{6,7},{7,6},{8,9},{9,8},{10,11... | collective-permute-start | bytes 3932168 | tf_op jit(solution)/shard_map/ppermute | solution.py:268
  182.2 39.1 %collective-permute-start.25 = (bf16[128,5120]{1,0:T(8,128)(2,1)S(1)}, bf16[128,5120]{1,0:T(8,128)(2,1)}, u32[]{:S(2)}, u32[]{:S(2)}) collective-permute-start(bf16[128,5120]{1,0:T(8,128)(2,1)S(1)} %broadcast_select_fusion.refs_17_), channel_id=1, source_target_pairs={{0,2},{1,3},{2,0},{3,1},{4,6},{5,7},{6,4},{7,5},{8,10},{9,11},{10,... | collective-permute-start | bytes 3932168 | tf_op jit(solution)/shard_map/ppermute | solution.py:259
  184.0 42.1 %collective-permute-start.24 = (bf16[128,5120]{1,0:T(8,128)(2,1)}, bf16[128,5120]{1,0:T(8,128)(2,1)}, u32[]{:S(2)}, u32[]{:S(2)}) collective-permute-start(bf16[128,5120]{1,0:T(8,128)(2,1)} %collective-permute-done.20), channel_id=1, source_target_pairs={{8,0},{12,4},{16,24},{20,28},{9,1},{13,5},{17,25},{21,29},{10,2},{... | collective-permute-start | bytes 3932168 | tf_op jit(solution)/shard_map/ppermute | solution.py:244
  186.1 44.1 %collective-permute-start.29 = (bf16[128,5120]{1,0:T(8,128)(2,1)S(1)}, bf16[128,5120]{1,0:T(8,128)(2,1)}, u32[]{:S(2)}, u32[]{:S(2)}) collective-permute-start(bf16[128,5120]{1,0:T(8,128)(2,1)S(1)} %broadcast_select_fusion.refs_17_), channel_id=1, source_target_pairs={{0,1},{1,0},{2,3},{3,2},{4,5},{5,4},{6,7},{7,6},{8,9},{9,8},{10,11... | collective-permute-start | bytes 3932168 | tf_op jit(solution)/shard_map/ppermute | solution.py:268
  199.7 45.6 %all-to-all-start = ((bf16[8,128,512]{2,1,0:T(8,128)(2,1)}), bf16[8,128,512]{2,1,0:T(8,128)(2,1)S(1)}, u32[]{:S(2)}, u32[]{:S(2)}) async-start(bf16[8,128,512]{2,1,0:T(8,128)(2,1)} %bitcast.26), calls=%async_computation | async-start | bytes 2097152 | tf_op jit(solution)/shard_map/all_to_all | solution.py:398
  247.3 19.2 %collective-permute-start.36 = (bf16[64,5120]{1,0:T(8,128)(2,1)S(1)}, bf16[64,5120]{1,0:T(8,128)(2,1)}, u32[]{:S(2)}, u32[]{:S(2)}) collective-permute-start(bf16[64,5120]{1,0:T(8,128)(2,1)S(1)} %slice_select_fusion.refs_17_), channel_id=1, source_target_pairs={{0,1},{1,0},{2,3},{3,2},{4,5},{5,4},{6,7},{7,6},{8,9},{9,8},{10,11... | collective-permute-start | bytes 1966088 | tf_op jit(solution)/shard_map/ppermute | solution.py:268
  264.7 21.7 %collective-permute-start.39 = (bf16[432,256]{1,0:T(8,128)(2,1)S(1)}, bf16[432,256]{1,0:T(8,128)(2,1)S(1)}, u32[]{:S(2)}, u32[]{:S(2)}) collective-permute-start(bf16[432,256]{1,0:T(8,128)(2,1)S(1)} %copy-done.38), channel_id=1, source_target_pairs={{0,24},{4,28},{8,16},{12,20},{16,8},{20,12},{24,0},{28,4},{1,25},{... | collective-permute-start | bytes 663560 | tf_op jit(solution)/shard_map/ppermute | solution.py:244
  (64 other events, 930.8 us)

commit v6 on v5

--- a/solution.py
+++ b/solution.py
@@ -214,7 +214,7 @@
             pltpu.VMEM((count, units, depth), jnp.bfloat16),
             pltpu.VMEM((tokens, width), jnp.bfloat16),
             pltpu.VMEM((2, units, tokens), jnp.float32),
-            pltpu.SemaphoreType.DMA((2, count, 3 if units % 48 == 0 else 1)),
+            pltpu.SemaphoreType.DMA((2, count, 1)),
             pltpu.SemaphoreType.DMA((pieces, halves)),
         ],
         compiler_params=pltpu.CompilerParams(vmem_limit_bytes=60 * 2**20),
@@ -312,9 +312,11 @@
         picked = lax.dynamic_index_in_dim(attended, which, 0, keepdims=False)
         return jnp.dot(picked, w_out, preferred_element_type=jnp.float32).astype(jnp.bfloat16)
 
+    mine = page_table[None] == (me_req * REQS + jnp.arange(REQS, dtype=jnp.int32))[:, None, None]
+    sources = jnp.sum(jnp.where(mine, jnp.arange(n_req, dtype=jnp.int32)[None, :, None], 0), axis=(1, 2))
     kept, given = project(core), project(1 - core)
-    up_2, gate_0, up_0, gate_2, kept, given = lax.optimization_barrier(
-        (share(up_t, 2), share(gate_t, 0), share(up_t, 0), gate_2, kept, given)
+    up_2, gate_0, up_0, gate_2, kept, given, sources = lax.optimization_barrier(
+        (share(up_t, 2), share(gate_t, 0), share(up_t, 0), gate_2, kept, given, sources)
     )
     up_2 = turn_z(up_2, 2)
     gate_0_y, up_0_y = along_y(gate_0), along_y(up_0)
@@ -331,8 +333,8 @@
         lax.dynamic_index_in_dim(pair, (x + step) % n_x, 0, keepdims=False).astype(jnp.bfloat16)
         for step in range(1, n_x)
     ]
-    gate_3, up_3, gate_1, up_2, gate_2_y, outgoing = lax.optimization_barrier(
-        (share(gate_t, 3), share(up_t, 3), gate_1, up_2, gate_2_y, outgoing)
+    gate_3, up_3, gate_1, up_2, gate_2_y = lax.optimization_barrier(
+        (share(gate_t, 3), share(up_t, 3), gate_1, up_2, gate_2_y)
     )
     gate_3, up_3 = turn_z(gate_3, 3), turn_z(up_3, 3)
     up_2_y = along_y(up_2)
@@ -416,8 +418,6 @@
     back_3a = along_z(hidden_3a, flip[3])
     hidden_3b, back_2[1], kv_in = lax.optimization_barrier((work(shared(next_3b, next_3b_x)), back_2[1], kv_in))
     back_3b = along_z(hidden_3b, flip[3])
-    mine = page_table[None] == (me_req * REQS + jnp.arange(REQS, dtype=jnp.int32))[:, None, None]
-    sources = jnp.sum(jnp.where(mine, jnp.arange(n_req, dtype=jnp.int32)[None, :, None], 0), axis=(1, 2))
     cache_out = write_cache(sources.astype(jnp.int32), kv_in, kv_heads)
     hidden_t = jnp.zeros((units_all, rows), jnp.bfloat16)
     for by, at, done in (

time: 297 us -> 299 us (level)
  waiting for transfers between devices: 133 us -> 142 us
  starting transfers between devices: 45.9 us -> 41.8 us
    ppermute x16, waiting for transfers between devices: 94.1 us -> 105 us  [along_z(): lax.ppermute(value, 'req', [(a * n_y + c, b * n_y + c) for a, b in moves...]
  transfers between devices with their start and end apart: 42 -> 42, of which waited for: 23 -> 21; matrix products, arithmetic and copies ran while one was open for 11% -> 10% of each run, Pallas kernels for 23% -> 22%
where the time goes in v6:
time: 299 us; the launch traced here: 295 us
  waiting for transfers between devices  142 us (47%)
  Pallas kernels  64.3 us (22%)
  starting transfers between devices  41.8 us (14%)
  other arithmetic  19.2 us (6%)
  local copies, waits for them, and re-layouts  15.7 us (5%)
  matrix products  10.8 us (4%)
    ppermute x16, waiting for transfers between devices, along_z(): lax.ppermute(value, 'req', [(a * n_y + c, b * n_y + c) for a, b in moves...  105 us
    pallas_call x5, Pallas kernels, mlp_block(): pl.pallas_call(lambda *refs: mlp_kernel(count, pieces, halves, outs, *ref...  57.7 us
    ppermute x8, waiting for transfers between devices, along_y(): lax.ppermute(value, 'req', [(a * n_y + b, a * n_y + (b + step) % n_y) for...  30.2 us
    ppermute x16, starting transfers between devices, along_z(): lax.ppermute(value, 'req', [(a * n_y + c, b * n_y + c) for a, b in moves...  19 us
    dot_general x2, matrix products, project(): jnp.dot(picked, w_out, preferred_element_type=jnp.float32)  10.8 us
    ppermute x8, starting transfers between devices, along_y(): lax.ppermute(value, 'req', [(a * n_y + b, a * n_y + (b + step) % n_y) for...  8.23 us
    all_to_all x1, starting transfers between devices, shards(): lax.all_to_all(kv_send.reshape(n_req, PAGE, 2 * kv_heads * HD), 'req', sp...  7.2 us
    unnamed x92, local copies, waits for them, and re-layouts  6.6 us
  transfers between devices with their start and end apart: 42, of which 21 were waited for; matrix products, arithmetic and copies ran while one was open for 10% of the time, Pallas kernels for 22%

profile of v6, /device:TPU:0, one launch (start us, length us, event | category | flops | bytes accessed | tf_op | source)
XLA Modules:
  0.0 294.9 jit_solution(8303626630397036244)
XLA Ops:
  2.8 4.0 %collective-permute-start = (bf16[432,640]{1,0:T(8,128)(2,1)}, bf16[432,640]{1,0:T(8,128)(2,1)S(1)}, u32[]{:S(2)}, u32[]{:S(2)}) collective-permute-start(bf16[432,640]{1,0:T(8,128)(2,1)} %dynamic-slice_bitcast_fusion), channel_id=1, source_target_pairs={{0,16},{4,20},{8,24},{12,28},{16,0},{20,4},{24,8},{28,12},{1,17},{... | collective-permute-start | bytes 1658888 | tf_op jit(solution)/shard_map/ppermute | solution.py:244
  12.4 4.5 %attention.1 = (bf16[512,768]{1,0:T(8,128)(2,1)S(1)}, bf16[1024,512]{1,0:T(8,128)(2,1)}) custom-call(bf16[512,768]{1,0:T(8,128)(2,1)S(1)} %copy-done, bf16[512,256]{1,0:T(8,128)(2,1)S(1)} %copy-done.1, bf16[512,256]{1,0:T(8,128)(2,1)S(1)} %copy-done.2, f32[1,768]{1,0:T(1,128)S(1)} %broadcast_in_dim.71.refs_3_, f32[1,256]{1,0:T(1,128)S(1)} %bitcast.46, ...), custom_call_target="tpu_custom_call" | custom-call | flops 100000000 | bytes 65536 | tf_op jit(solution)/shard_map/attention/pallas_call | solution.py:95
  16.9 7.1 %convolution_convert_fusion = bf16[256,5120]{1,0:T(8,128)(2,1)} fusion(bf16[768,5120]{1,0:T(8,128)(2,1)} %param.23, bf16[2,256,768]{2,1,0:T(8,128)(2,1)S(1)} %bitcast.48, s32[]{:T(128)S(6)} %select_n.202), kind=kOutput, calls=%fused_computation | convolution fusion | flops 2014576640 | bytes 10878980 | tf_op jit(solution)/shard_map/dot_general | solution.py:313
  25.6 3.7 %convolution_convert_fusion.1 = bf16[256,5120]{1,0:T(8,128)(2,1)} fusion(bf16[768,5120]{1,0:T(8,128)(2,1)S(1)} %bitcast.57, bf16[2,256,768]{2,1,0:T(8,128)(2,1)S(1)} %bitcast.49, s32[]{:T(128)S(6)} %select_n.201), kind=kOutput, calls=%fused_computation.1 | convolution fusion | flops 2014576640 | bytes 10878980 | tf_op jit(solution)/shard_map/dot_general | solution.py:313
  33.5 25.6 %collective-permute-done.1.refs_11_ = bf16[432,640]{1,0:T(8,128)(2,1)S(1)} collective-permute-done((bf16[432,640]{1,0:T(8,128)(2,1)S(1)}, bf16[432,640]{1,0:T(8,128)(2,1)S(1)}, u32[]{:S(2)}, u32[]{:S(2)}) %collective-permute-start.1) | collective-permute-done | bytes 552992 | tf_op jit(solution)/shard_map/ppermute | solution.py:244
  59.1 3.8 %convert_add_fusion = f32[256,5120]{1,0:T(8,128)S(1)} fusion(bf16[256,5120]{1,0:T(8,128)(2,1)} %collective-permute-done.4, bf16[256,5120]{1,0:T(8,128)(2,1)} %convolution_convert_fusion.1), kind=kLoop, calls=%fused_computation.2 | loop fusion | flops 3932160 | bytes 10485760 | tf_op jit(solution)/shard_map/add | solution.py:330
  71.1 11.8 %collective-permute-done.5.refs_5_ = bf16[432,640]{1,0:T(8,128)(2,1)S(1)} collective-permute-done((bf16[432,640]{1,0:T(8,128)(2,1)}, bf16[432,640]{1,0:T(8,128)(2,1)S(1)}, u32[]{:S(2)}, u32[]{:S(2)}) %collective-permute-start.5) | collective-permute-done | bytes 552992 | tf_op jit(solution)/shard_map/ppermute | solution.py:244
  88.4 10.1 %collective-permute-done.10.refs_12_ = bf16[432,640]{1,0:T(8,128)(2,1)S(1)} collective-permute-done((bf16[432,640]{1,0:T(8,128)(2,1)S(1)}, bf16[432,640]{1,0:T(8,128)(2,1)S(1)}, u32[]{:S(2)}, u32[]{:S(2)}) %collective-permute-start.10) | collective-permute-done | bytes 552992 | tf_op jit(solution)/shard_map/ppermute | solution.py:251
  100.2 9.1 %collective-permute-done.8.refs_15_ = bf16[432,640]{1,0:T(8,128)(2,1)S(1)} collective-permute-done((bf16[432,640]{1,0:T(8,128)(2,1)}, bf16[432,640]{1,0:T(8,128)(2,1)S(1)}, u32[]{:S(2)}, u32[]{:S(2)}) %collective-permute-start.8) | collective-permute-done | bytes 552992 | tf_op jit(solution)/shard_map/ppermute | solution.py:244
  116.9 10.2 %collective-permute-done.12.refs_13_ = bf16[432,640]{1,0:T(8,128)(2,1)S(1)} collective-permute-done((bf16[432,640]{1,0:T(8,128)(2,1)S(1)}, bf16[432,640]{1,0:T(8,128)(2,1)S(1)}, u32[]{:S(2)}, u32[]{:S(2)}) %collective-permute-start.12) | collective-permute-done | bytes 552992 | tf_op jit(solution)/shard_map/ppermute | solution.py:244
  131.5 13.4 %collective-permute-done.17.refs_16_ = bf16[432,640]{1,0:T(8,128)(2,1)S(1)} collective-permute-done((bf16[432,640]{1,0:T(8,128)(2,1)S(1)}, bf16[432,640]{1,0:T(8,128)(2,1)S(1)}, u32[]{:S(2)}, u32[]{:S(2)}) %collective-permute-start.17) | collective-permute-done | bytes 552992 | tf_op jit(solution)/shard_map/ppermute | solution.py:251
  145.0 6.6 %collective-permute-done.16.refs_14_ = bf16[432,640]{1,0:T(8,128)(2,1)S(1)} collective-permute-done((bf16[432,640]{1,0:T(8,128)(2,1)S(1)}, bf16[432,640]{1,0:T(8,128)(2,1)S(1)}, u32[]{:S(2)}, u32[]{:S(2)}) %collective-permute-start.16) | collective-permute-done | bytes 552992 | tf_op jit(solution)/shard_map/ppermute | solution.py:251
  151.6 3.4 %collective-permute-done.14.refs_17_ = bf16[128,5120]{1,0:T(8,128)(2,1)} collective-permute-done((bf16[128,5120]{1,0:T(8,128)(2,1)}, bf16[128,5120]{1,0:T(8,128)(2,1)}, u32[]{:S(2)}, u32[]{:S(2)}) %collective-permute-start.14) | collective-permute-done | bytes 1310752 | tf_op jit(solution)/shard_map/ppermute | solution.py:244
  160.0 24.1 %collective-permute-done.19 = bf16[128,5120]{1,0:T(8,128)(2,1)} collective-permute-done((bf16[128,5120]{1,0:T(8,128)(2,1)}, bf16[128,5120]{1,0:T(8,128)(2,1)}, u32[]{:S(2)}, u32[]{:S(2)}) %collective-permute-start.19) | collective-permute-done | bytes 1310752 | tf_op jit(solution)/shard_map/ppermute | solution.py:244
  189.6 12.9 %mlp_block.5 = bf16[432,512]{1,0:T(8,128)(2,1)} custom-call(s32[12]{0:T(128)} %stack.38.refs_0_, bf16[432,640]{1,0:T(8,128)(2,1)} %copy-done.9, bf16[432,640]{1,0:T(8,128)(2,1)} %copy-done.12, bf16[432,640]{1,0:T(8,128)(2,1)} %copy-done.10, bf16[432,640]{1,0:T(8,128)(2,1)} %copy-done.14, bf16[432,640]{1,0:T(8,128)(2,1)} %copy-done.13, ...), custom_call_target="tpu_custom_call" | custom-call | flops 100000000 | bytes 65536 | tf_op jit(solution)/shard_map/mlp_block/pallas_call | solution.py:207
  202.5 7.2 %all-to-all-start = ((bf16[8,128,512]{2,1,0:T(8,128)(2,1)}), bf16[8,128,512]{2,1,0:T(8,128)(2,1)S(1)}, u32[]{:S(2)}, u32[]{:S(2)}) async-start(bf16[8,128,512]{2,1,0:T(8,128)(2,1)} %bitcast.26), calls=%async_computation | async-start | bytes 2097152 | tf_op jit(solution)/shard_map/all_to_all | solution.py:400
  209.8 12.9 %mlp_block.6 = bf16[432,512]{1,0:T(8,128)(2,1)} custom-call(s32[12]{0:T(128)} %stack.38.refs_0_, bf16[432,640]{1,0:T(8,128)(2,1)} %copy-done.9, bf16[432,640]{1,0:T(8,128)(2,1)} %copy-done.12, bf16[432,640]{1,0:T(8,128)(2,1)} %copy-done.10, bf16[432,640]{1,0:T(8,128)(2,1)} %copy-done.14, bf16[432,640]{1,0:T(8,128)(2,1)} %copy-done.13, ...), custom_call_target="tpu_custom_call" | custom-call | flops 100000000 | bytes 65536 | tf_op jit(solution)/shard_map/mlp_block/pallas_call | solution.py:207
  222.7 6.6 %collective-permute-done.24 = bf16[128,5120]{1,0:T(8,128)(2,1)} collective-permute-done((bf16[128,5120]{1,0:T(8,128)(2,1)}, bf16[128,5120]{1,0:T(8,128)(2,1)}, u32[]{:S(2)}, u32[]{:S(2)}) %collective-permute-start.24) | collective-permute-done | bytes 1310752 | tf_op jit(solution)/shard_map/ppermute | solution.py:244
  234.6 12.9 %mlp_block.7 = (bf16[432,256]{1,0:T(8,128)(2,1)}, bf16[432,256]{1,0:T(8,128)(2,1)}) custom-call(s32[12]{0:T(128)} %stack.38.refs_0_, bf16[432,640]{1,0:T(8,128)(2,1)} %copy-done.9, bf16[432,640]{1,0:T(8,128)(2,1)} %copy-done.12, bf16[432,640]{1,0:T(8,128)(2,1)} %copy-done.10, bf16[432,640]{1,0:T(8,128)(2,1)} %copy-done.14, bf16[432,640]{1,0:T(8,128)(2,1)} %copy-done.13, ...), custom_call_target="tpu_custom_call" | custom-call | flops 100000000 | bytes 65536 | tf_op jit(solution)/shard_map/mlp_block/pallas_call | solution.py:207
  252.2 9.5 %mlp_block.8 = bf16[432,256]{1,0:T(8,128)(2,1)} custom-call(s32[12]{0:T(128)} %stack.38.refs_0_, bf16[432,640]{1,0:T(8,128)(2,1)} %copy-done.9, bf16[432,640]{1,0:T(8,128)(2,1)} %copy-done.12, bf16[432,640]{1,0:T(8,128)(2,1)} %copy-done.10, bf16[432,640]{1,0:T(8,128)(2,1)} %copy-done.14, bf16[432,640]{1,0:T(8,128)(2,1)} %copy-done.13, ...), custom_call_target="tpu_custom_call" | custom-call | flops 100000000 | bytes 65536 | tf_op jit(solution)/shard_map/mlp_block/pallas_call | solution.py:207
  263.1 3.1 %collective-permute-done.32.refs_18_ = bf16[64,5120]{1,0:T(8,128)(2,1)S(1)} collective-permute-done((bf16[64,5120]{1,0:T(8,128)(2,1)S(1)}, bf16[64,5120]{1,0:T(8,128)(2,1)S(1)}, u32[]{:S(2)}, u32[]{:S(2)}) %collective-permute-start.32) | collective-permute-done | bytes 655392 | tf_op jit(solution)/shard_map/ppermute | solution.py:259
  271.7 9.6 %mlp_block.9 = bf16[432,256]{1,0:T(8,128)(2,1)} custom-call(s32[12]{0:T(128)} %stack.38.refs_0_, bf16[432,640]{1,0:T(8,128)(2,1)} %copy-done.9, bf16[432,640]{1,0:T(8,128)(2,1)} %copy-done.12, bf16[432,640]{1,0:T(8,128)(2,1)} %copy-done.10, bf16[432,640]{1,0:T(8,128)(2,1)} %copy-done.14, bf16[432,640]{1,0:T(8,128)(2,1)} %copy-done.13, ...), custom_call_target="tpu_custom_call" | custom-call | flops 100000000 | bytes 65536 | tf_op jit(solution)/shard_map/mlp_block/pallas_call | solution.py:207
  281.2 3.8 %collective-permute-done.38 = bf16[432,256]{1,0:T(8,128)(2,1)S(1)} collective-permute-done((bf16[432,256]{1,0:T(8,128)(2,1)}, bf16[432,256]{1,0:T(8,128)(2,1)S(1)}, u32[]{:S(2)}, u32[]{:S(2)}) %collective-permute-start.38) | collective-permute-done | bytes 221216 | tf_op jit(solution)/shard_map/ppermute | solution.py:244
  289.7 4.4 %collective-permute-done.40 = bf16[432,256]{1,0:T(8,128)(2,1)S(1)} collective-permute-done((bf16[432,256]{1,0:T(8,128)(2,1)}, bf16[432,256]{1,0:T(8,128)(2,1)S(1)}, u32[]{:S(2)}, u32[]{:S(2)}) %collective-permute-start.40) | collective-permute-done | bytes 221216 | tf_op jit(solution)/shard_map/ppermute | solution.py:244
  (195 shorter events, 73.2 us)
Async XLA Ops:
  2.8 28.6 %collective-permute-start = (bf16[432,640]{1,0:T(8,128)(2,1)}, bf16[432,640]{1,0:T(8,128)(2,1)S(1)}, u32[]{:S(2)}, u32[]{:S(2)}) collective-permute-start(bf16[432,640]{1,0:T(8,128)(2,1)} %dynamic-slice_bitcast_fusion), channel_id=1, source_target_pairs={{0,16},{4,20},{8,24},{12,28},{16,0},{20,4},{24,8},{28,12},{1,17},{... | collective-permute-start | bytes 1658888 | tf_op jit(solution)/shard_map/ppermute | solution.py:244
  31.4 27.7 %collective-permute-start.4 = (bf16[256,5120]{1,0:T(8,128)(2,1)}, bf16[256,5120]{1,0:T(8,128)(2,1)}, u32[]{:S(2)}, u32[]{:S(2)}) collective-permute-start(bf16[256,5120]{1,0:T(8,128)(2,1)} %convolution_convert_fusion), channel_id=1, source_target_pairs={{0,1},{1,0},{2,3},{3,2},{4,5},{5,4},{6,7},{7,6},{8,9},{9,8},{10,11... | collective-permute-start | bytes 7864328 | tf_op jit(solution)/shard_map/ppermute | solution.py:268
  31.4 27.7 %collective-permute-start.1 = (bf16[432,640]{1,0:T(8,128)(2,1)S(1)}, bf16[432,640]{1,0:T(8,128)(2,1)S(1)}, u32[]{:S(2)}, u32[]{:S(2)}) collective-permute-start(bf16[432,640]{1,0:T(8,128)(2,1)S(1)} %get-tuple-element.77), channel_id=1, source_target_pairs={{0,16},{4,20},{8,24},{12,28},{16,0},{20,4},{24,8},{28,12},{1,17},{... | collective-permute-start | bytes 1658888 | tf_op jit(solution)/shard_map/ppermute | solution.py:244
  31.4 27.7 %collective-permute-start.2 = (bf16[432,640]{1,0:T(8,128)(2,1)S(1)}, bf16[432,640]{1,0:T(8,128)(2,1)S(1)}, u32[]{:S(2)}, u32[]{:S(2)}) collective-permute-start(bf16[432,640]{1,0:T(8,128)(2,1)S(1)} %get-tuple-element.78.refs_1_), channel_id=1, source_target_pairs={{0,4},{4,0},{8,12},{12,8},{16,20},{20,16},{24,28},{28,24},{1,5},{5... | collective-permute-start | bytes 1658888 | tf_op jit(solution)/shard_map/ppermute | solution.py:251
  33.1 26.1 %collective-permute-start.3 = (bf16[432,640]{1,0:T(8,128)(2,1)S(1)}, bf16[432,640]{1,0:T(8,128)(2,1)}, u32[]{:S(2)}, u32[]{:S(2)}) collective-permute-start(bf16[432,640]{1,0:T(8,128)(2,1)S(1)} %get-tuple-element.79.refs_9_), channel_id=1, source_target_pairs={{0,4},{4,0},{8,12},{12,8},{16,20},{20,16},{24,28},{28,24},{1,5},{5... | collective-permute-start | bytes 1658888 | tf_op jit(solution)/shard_map/ppermute | solution.py:251
  65.4 43.9 %collective-permute-start.11 = (bf16[128,5120]{1,0:T(8,128)(2,1)S(1)}, bf16[128,5120]{1,0:T(8,128)(2,1)}, u32[]{:S(2)}, u32[]{:S(2)}) collective-permute-start(bf16[128,5120]{1,0:T(8,128)(2,1)S(1)} %fusion.1), channel_id=1, source_target_pairs={{0,2},{1,3},{2,0},{3,1},{4,6},{5,7},{6,4},{7,5},{8,10},{9,11},{10,... | collective-permute-start | bytes 3932168 | tf_op jit(solution)/shard_map/ppermute | solution.py:343
  86.0 23.3 %collective-permute-start.8 = (bf16[432,640]{1,0:T(8,128)(2,1)}, bf16[432,640]{1,0:T(8,128)(2,1)S(1)}, u32[]{:S(2)}, u32[]{:S(2)}) collective-permute-start(bf16[432,640]{1,0:T(8,128)(2,1)} %get-tuple-element.87), channel_id=1, source_target_pairs={{0,24},{4,28},{8,0},{12,4},{16,8},{20,12},{24,16},{28,20},{1,25},{... | collective-permute-start | bytes 1658888 | tf_op jit(solution)/shard_map/ppermute | solution.py:244
  86.4 22.8 %collective-permute-start.9 = (bf16[432,640]{1,0:T(8,128)(2,1)S(1)}, bf16[432,640]{1,0:T(8,128)(2,1)S(1)}, u32[]{:S(2)}, u32[]{:S(2)}) collective-permute-start(bf16[432,640]{1,0:T(8,128)(2,1)S(1)} %collective-permute-done.5.refs_5_), channel_id=1, source_target_pairs={{0,4},{4,0},{8,12},{12,8},{16,20},{20,16},{24,28},{28,24},{1,5},{5... | collective-permute-start | bytes 1658888 | tf_op jit(solution)/shard_map/ppermute | solution.py:251
  127.1 27.8 %collective-permute-start.14 = (bf16[128,5120]{1,0:T(8,128)(2,1)}, bf16[128,5120]{1,0:T(8,128)(2,1)}, u32[]{:S(2)}, u32[]{:S(2)}) collective-permute-start(bf16[128,5120]{1,0:T(8,128)(2,1)} %multiply_convert_fusion.refs_17_), channel_id=1, source_target_pairs={{0,8},{4,12},{8,0},{12,4},{16,24},{20,28},{24,16},{28,20},{1,9},{5... | collective-permute-start | bytes 3932168 | tf_op jit(solution)/shard_map/ppermute | solution.py:244
  127.2 27.8 %collective-permute-start.15 = (bf16[128,5120]{1,0:T(8,128)(2,1)}, bf16[128,5120]{1,0:T(8,128)(2,1)}, u32[]{:S(2)}, u32[]{:S(2)}) collective-permute-start(bf16[128,5120]{1,0:T(8,128)(2,1)} %multiply_convert_fusion.refs_17_), channel_id=1, source_target_pairs={{8,16},{12,20},{16,8},{20,12},{9,17},{13,21},{17,9},{21,13},{10,18... | collective-permute-start | bytes 3932168 | tf_op jit(solution)/shard_map/ppermute | solution.py:244
  128.9 27.0 %collective-permute-start.18 = (bf16[128,5120]{1,0:T(8,128)(2,1)}, bf16[128,5120]{1,0:T(8,128)(2,1)S(1)}, u32[]{:S(2)}, u32[]{:S(2)}) collective-permute-start(bf16[128,5120]{1,0:T(8,128)(2,1)} %multiply_convert_fusion.refs_17_), channel_id=1, source_target_pairs={{0,2},{1,3},{2,0},{3,1},{4,6},{5,7},{6,4},{7,5},{8,10},{9,11},{10,... | collective-permute-start | bytes 3932168 | tf_op jit(solution)/shard_map/ppermute | solution.py:259
  129.9 21.6 %collective-permute-start.16 = (bf16[432,640]{1,0:T(8,128)(2,1)S(1)}, bf16[432,640]{1,0:T(8,128)(2,1)S(1)}, u32[]{:S(2)}, u32[]{:S(2)}) collective-permute-start(bf16[432,640]{1,0:T(8,128)(2,1)S(1)} %collective-permute-done.12.refs_13_), channel_id=1, source_target_pairs={{0,4},{4,0},{8,12},{12,8},{16,20},{20,16},{24,28},{28,24},{1,5},{5... | collective-permute-start | bytes 1658888 | tf_op jit(solution)/shard_map/ppermute | solution.py:251
  155.9 28.1 %collective-permute-start.19 = (bf16[128,5120]{1,0:T(8,128)(2,1)}, bf16[128,5120]{1,0:T(8,128)(2,1)}, u32[]{:S(2)}, u32[]{:S(2)}) collective-permute-start(bf16[128,5120]{1,0:T(8,128)(2,1)} %collective-permute-done.15), channel_id=1, source_target_pairs={{8,0},{12,4},{16,24},{20,28},{9,1},{13,5},{17,25},{21,29},{10,2},{... | collective-permute-start | bytes 3932168 | tf_op jit(solution)/shard_map/ppermute | solution.py:244
  157.2 26.8 %collective-permute-start.20 = (bf16[128,5120]{1,0:T(8,128)(2,1)}, bf16[128,5120]{1,0:T(8,128)(2,1)}, u32[]{:S(2)}, u32[]{:S(2)}) collective-permute-start(bf16[128,5120]{1,0:T(8,128)(2,1)} %collective-permute-done.14.refs_17_), channel_id=1, source_target_pairs={{8,16},{12,20},{16,8},{20,12},{9,17},{13,21},{17,9},{21,13},{10,18... | collective-permute-start | bytes 3932168 | tf_op jit(solution)/shard_map/ppermute | solution.py:244
  158.9 26.2 %collective-permute-start.21 = (bf16[128,5120]{1,0:T(8,128)(2,1)}, bf16[128,5120]{1,0:T(8,128)(2,1)}, u32[]{:S(2)}, u32[]{:S(2)}) collective-permute-start(bf16[128,5120]{1,0:T(8,128)(2,1)} %collective-permute-done.14.refs_17_), channel_id=1, source_target_pairs={{0,2},{1,3},{2,0},{3,1},{4,6},{5,7},{6,4},{7,5},{8,10},{9,11},{10,... | collective-permute-start | bytes 3932168 | tf_op jit(solution)/shard_map/ppermute | solution.py:259
  159.5 25.7 %collective-permute-start.23 = (bf16[128,5120]{1,0:T(8,128)(2,1)S(1)}, bf16[128,5120]{1,0:T(8,128)(2,1)}, u32[]{:S(2)}, u32[]{:S(2)}) collective-permute-start(bf16[128,5120]{1,0:T(8,128)(2,1)S(1)} %collective-permute-done.18.refs_18_), channel_id=1, source_target_pairs={{0,1},{1,0},{2,3},{3,2},{4,5},{5,4},{6,7},{7,6},{8,9},{9,8},{10,11... | collective-permute-start | bytes 3932168 | tf_op jit(solution)/shard_map/ppermute | solution.py:268
  159.5 50.3 %collective-permute-start.26 = (bf16[128,5120]{1,0:T(8,128)(2,1)}, bf16[128,5120]{1,0:T(8,128)(2,1)}, u32[]{:S(2)}, u32[]{:S(2)}) collective-permute-start(bf16[128,5120]{1,0:T(8,128)(2,1)} %collective-permute-done.14.refs_17_), channel_id=1, source_target_pairs={{0,1},{1,0},{2,3},{3,2},{4,5},{5,4},{6,7},{7,6},{8,9},{9,8},{10,11... | collective-permute-start | bytes 3932168 | tf_op jit(solution)/shard_map/ppermute | solution.py:268
  185.2 24.6 %collective-permute-start.27 = (bf16[128,5120]{1,0:T(8,128)(2,1)}, bf16[128,5120]{1,0:T(8,128)(2,1)}, u32[]{:S(2)}, u32[]{:S(2)}) collective-permute-start(bf16[128,5120]{1,0:T(8,128)(2,1)} %collective-permute-done.21.refs_18_), channel_id=1, source_target_pairs={{0,1},{1,0},{2,3},{3,2},{4,5},{5,4},{6,7},{7,6},{8,9},{9,8},{10,11... | collective-permute-start | bytes 3932168 | tf_op jit(solution)/shard_map/ppermute | solution.py:268
  186.7 36.0 %collective-permute-start.25 = (bf16[128,5120]{1,0:T(8,128)(2,1)S(1)}, bf16[128,5120]{1,0:T(8,128)(2,1)}, u32[]{:S(2)}, u32[]{:S(2)}) collective-permute-start(bf16[128,5120]{1,0:T(8,128)(2,1)S(1)} %broadcast_select_fusion.refs_17_), channel_id=1, source_target_pairs={{0,2},{1,3},{2,0},{3,1},{4,6},{5,7},{6,4},{7,5},{8,10},{9,11},{10,... | collective-permute-start | bytes 3932168 | tf_op jit(solution)/shard_map/ppermute | solution.py:259
  187.3 42.0 %collective-permute-start.24 = (bf16[128,5120]{1,0:T(8,128)(2,1)}, bf16[128,5120]{1,0:T(8,128)(2,1)}, u32[]{:S(2)}, u32[]{:S(2)}) collective-permute-start(bf16[128,5120]{1,0:T(8,128)(2,1)} %collective-permute-done.20), channel_id=1, source_target_pairs={{8,0},{12,4},{16,24},{20,28},{9,1},{13,5},{17,25},{21,29},{10,2},{... | collective-permute-start | bytes 3932168 | tf_op jit(solution)/shard_map/ppermute | solution.py:244
  189.4 45.2 %collective-permute-start.29 = (bf16[128,5120]{1,0:T(8,128)(2,1)S(1)}, bf16[128,5120]{1,0:T(8,128)(2,1)}, u32[]{:S(2)}, u32[]{:S(2)}) collective-permute-start(bf16[128,5120]{1,0:T(8,128)(2,1)S(1)} %broadcast_select_fusion.refs_17_), channel_id=1, source_target_pairs={{0,1},{1,0},{2,3},{3,2},{4,5},{5,4},{6,7},{7,6},{8,9},{9,8},{10,11... | collective-permute-start | bytes 3932168 | tf_op jit(solution)/shard_map/ppermute | solution.py:268
  202.5 46.0 %all-to-all-start = ((bf16[8,128,512]{2,1,0:T(8,128)(2,1)}), bf16[8,128,512]{2,1,0:T(8,128)(2,1)S(1)}, u32[]{:S(2)}, u32[]{:S(2)}) async-start(bf16[8,128,512]{2,1,0:T(8,128)(2,1)} %bitcast.26), calls=%async_computation | async-start | bytes 2097152 | tf_op jit(solution)/shard_map/all_to_all | solution.py:400
  250.4 19.2 %collective-permute-start.36 = (bf16[64,5120]{1,0:T(8,128)(2,1)S(1)}, bf16[64,5120]{1,0:T(8,128)(2,1)}, u32[]{:S(2)}, u32[]{:S(2)}) collective-permute-start(bf16[64,5120]{1,0:T(8,128)(2,1)S(1)} %slice_select_fusion.refs_17_), channel_id=1, source_target_pairs={{0,1},{1,0},{2,3},{3,2},{4,5},{5,4},{6,7},{7,6},{8,9},{9,8},{10,11... | collective-permute-start | bytes 1966088 | tf_op jit(solution)/shard_map/ppermute | solution.py:268
  267.3 21.7 %collective-permute-start.39 = (bf16[432,256]{1,0:T(8,128)(2,1)S(1)}, bf16[432,256]{1,0:T(8,128)(2,1)S(1)}, u32[]{:S(2)}, u32[]{:S(2)}) collective-permute-start(bf16[432,256]{1,0:T(8,128)(2,1)S(1)} %copy-done.38), channel_id=1, source_target_pairs={{0,24},{4,28},{8,16},{12,20},{16,8},{20,12},{24,0},{28,4},{1,25},{... | collective-permute-start | bytes 663560 | tf_op jit(solution)/shard_map/ppermute | solution.py:244
  (64 other events, 915.5 us)
